TPU v7x, 128 devices: a whole 4x4x4 slice. The times are simulated.
128 devices in a mesh: tp: 4 (over y_lo, core), dp: 32 (over x, z, y_hi).
Axes of the slice: x: 4, y: 4 (y_hi: 2, y_lo: 2; y = y_hi * 2 + y_lo), z: 4, core: 2. Of those that a mesh axis runs over, the one named last changes fastest.
Arguments:
- hidden: bfloat16 [32768, 7168], P('dp', 'tp'), may hold values from -6 to 6
- grad_out: bfloat16 [32768, 2048], P('dp', 'tp'), may hold values from -6 to 6
- momentum: bfloat16 [7168, 2048], P('tp'), may hold values from -6 to 6
- worker_err: bfloat16 [32, 7168, 2048], P('dp', 'tp'), may hold values from -6 to 6
- server_err: float32 [7168, 2048], P(('tp', 'dp')), may hold values from -6 to 6
Outputs:
- update: bfloat16 [7168, 2048], P('tp')
- corrected: float32 [7168, 2048], P(('tp', 'dp'))
All inputs are finite; a program needn't handle non-finite values.
Results may differ from a plain program's by a relative error of at most 0.015.
Values may be sent and summed in bfloat16 or wider, within the bound.
No kernel may reach another device: no remote copies, remote signals or barrier semaphores. Data moves between devices by JAX's collectives and lax.ppermute only.
A program may use at most 192 MiB of HBM per device.

v0:
```python
import jax
import jax.numpy as jnp
from jax import lax
from jax.sharding import PartitionSpec as P

clip_bound = 1.5


def compress(values):
    rows = values.shape[0]
    blocks = values.reshape(rows, values.shape[1] // 128, 128)
    scale = jnp.sqrt(jnp.mean(blocks * blocks, axis=-1) + 1e-06)
    codes = jnp.clip(blocks / scale[..., None], -clip_bound, clip_bound).astype(jnp.bfloat16)
    return (codes, scale)


def body(hidden, grad_out, momentum, worker_err, server_err):
    replicas = lax.axis_size("dp")
    local_rows = hidden.shape[1]
    grad = lax.dot_general(
        hidden,
        lax.all_gather(grad_out, "tp", axis=1, tiled=True),
        (((0,), (0,)), ((), ())),
        preferred_element_type=jnp.float32,
    )
    values = 0.9 * momentum.astype(jnp.float32) + 0.1 * grad + worker_err[0].astype(jnp.float32)
    codes, scale = compress(values)
    owned = local_rows // replicas
    nblocks = codes.shape[1]
    codes_out = codes.reshape(replicas, owned, nblocks, 128)
    scale_out = scale.reshape(replicas, owned, nblocks)
    codes_in, scale_in = (
        lax.all_to_all(codes_out, "dp", split_axis=0, concat_axis=0, tiled=True),
        lax.all_to_all(
            scale_out.astype(jnp.bfloat16), "dp", split_axis=0, concat_axis=0, tiled=True
        ).astype(scale_out.dtype),
    )
    total = jnp.sum(codes_in.astype(jnp.float32) * scale_in[..., None], axis=0)
    corrected = total.reshape(owned, nblocks * 128) / replicas + server_err
    new_codes, new_scale = compress(corrected)
    all_codes, all_scale = (
        lax.all_gather(new_codes, "dp", axis=0, tiled=True),
        lax.all_gather(new_scale.astype(jnp.bfloat16), "dp", axis=0, tiled=True).astype(
            new_scale.dtype
        ),
    )
    update = (
        (all_codes.astype(jnp.float32) * all_scale[..., None])
        .reshape(local_rows, -1)
        .astype(jnp.bfloat16)
    )
    return (update, corrected)


def solution(mesh):
    placed = (
        P("dp", "tp"),
        P("dp", "tp"),
        P("tp", None),
        P("dp", "tp", None),
        P(("tp", "dp"), None),
    )
    return jax.shard_map(
        body,
        mesh=mesh,
        in_specs=placed,
        out_specs=(P("tp", None), P(("tp", "dp"), None)),
        check_vma=False,
    )
```

profile of v0, /device:TPU:0, one launch (start us, length us, event | category | flops | bytes accessed | tf_op | source)
XLA Modules:
  0.0 401.9 jit_solution(539350978513635495)
XLA Ops:
  7.2 0.0 all-gather.4.cloned.1.call-start
  7.2 0.7 all-gather.4.cloned.1.call-update
  7.9 50.3 %all-gather.4.cloned.1.call-done = bf16[1024,2048]{1,0:T(8,128)(2,1)} async-done(((bf16[1024,512]{1,0:T(8,128)(2,1)}), bf16[1024,2048]{1,0:T(8,128)(2,1)}) %all-gather.4.cloned.1.call-update) | async-done | bytes 4194320 | tf_op jit(solution)/shard_map/all_gather | solution.py:22
  58.2 18.7 %convert_add_fusion = f32[1792,2048]{1,0:T(8,128)} fusion(bf16[1792,2048]{1,0:T(8,128)(2,1)} %param.7, bf16[1024,1792]{1,0:T(8,128)(2,1)} %param.5, bf16[1024,2048]{1,0:T(8,128)(2,1)} %all-gather.4.cloned.1.call-done, bf16[1,1792,2048]{2,1,0:T(8,128)(2,1)} %param.8), kind=kOutput, calls=%fused_computation.3 | convolution fusion | flops 7538212864 | bytes 37224448 | tf_op jit(solution)/shard_map/dot_general | solution.py:20
  76.8 13.6 %multiply_bitcast_fusion = f32[224,8,16,128]{3,1,2,0:T(8,128)} fusion(f32[1792,2048]{1,0:T(8,128)} %convert_add_fusion), kind=kLoop, calls=%fused_computation.6 | loop fusion | flops 3670016 | bytes 29360128
  90.4 14.0 %copy.33 = f32[224,8,16,128]{3,2,1,0:T(8,128)} copy(f32[224,8,16,128]{3,1,2,0:T(8,128)} %multiply_bitcast_fusion) | data formatting | bytes 29360128
  104.4 7.7 %reduce_sum.27 = f32[1792,16]{1,0:T(8,128)S(1)} reduce(f32[1792,16,128]{2,1,0:T(8,128)} %bitcast.37, f32[]{:T(128)} %constant.4.clone.1), dimensions={2}, to_apply=%region_0.0 | reduce | flops 3641344 | bytes 14794756 | tf_op jit(solution)/shard_map/reduce_sum | solution.py:12
  112.1 0.3 copy.23
  112.4 0.2 sqrt.19
  112.7 0.3 copy.24
  113.0 14.0 %copy.32 = f32[224,8,16,128]{3,2,1,0:T(8,128)} copy(f32[224,8,16,128]{3,1,2,0:T(8,128)} %bitcast.36) | data formatting | bytes 29360128
  127.0 0.1 copy.41
  127.0 0.8 reshape.48
  127.8 9.4 %all-to-all-start.1 = ((bf16[32,2,448]{2,1,0:T(2,128)(2,1)}), bf16[32,2,448]{2,1,0:T(2,128)(2,1)S(1)}, u32[]{:S(2)}, u32[]{:S(2)}) async-start(bf16[32,2,448]{2,1,0:T(2,128)(2,1)} %reshape.48), calls=%async_computation.1 | async-start | bytes 131072 | tf_op jit(solution)/shard_map/all_to_all | solution.py:34
  137.2 9.6 %fusion.1 = bf16[32,56,16,128]{3,2,1,0:T(8,128)(2,1)} fusion(f32[32,56,16]{2,1,0:T(8,128)S(1)} %copy.24, f32[32,56,16,128]{3,2,1,0:T(8,128)} %bitcast.38), kind=kLoop, calls=%fused_computation.2 | loop fusion | flops 11010048 | bytes 22134784 | tf_op jit(solution)/shard_map/convert_element_type | solution.py:13
  146.8 0.0 copy-start.1
  146.8 0.2 all-to-all-done.1
  147.0 9.9 %all-to-all-start = ((bf16[32,56,16,128]{3,2,1,0:T(8,128)(2,1)}), bf16[32,56,16,128]{3,2,1,0:T(8,128)(2,1)}, u32[]{:S(2)}, u32[]{:S(2)}) async-start(bf16[32,56,16,128]{3,2,1,0:T(8,128)(2,1)} %fusion.1), calls=%async_computation | async-start | bytes 14680064 | tf_op jit(solution)/shard_map/all_to_all | solution.py:33
  156.9 0.0 all-gather.6.cloned.1.call-start
  156.9 0.2 reshape.49
  157.1 0.2 copy.26
  157.3 111.3 %all-to-all-done = bf16[32,56,16,128]{3,2,1,0:T(8,128)(2,1)} async-done(((bf16[32,56,16,128]{3,2,1,0:T(8,128)(2,1)}), bf16[32,56,16,128]{3,2,1,0:T(8,128)(2,1)}, u32[]{:S(2)}, u32[]{:S(2)}) %all-to-all-start) | async-done | bytes 7340064 | tf_op jit(solution)/shard_map/all_to_all | solution.py:33
  268.6 7.7 %multiply_reduce_fusion = f32[56,16,128]{2,1,0:T(8,128)S(1)} fusion(bf16[32,56,16,128]{3,2,1,0:T(8,128)(2,1)} %all-to-all-done, f32[32,56,16]{2,1,0:T(8,128)S(1)} %copy.26), kind=kLoop, calls=%fused_computation.5 | loop fusion | flops 10895360 | bytes 7913472 | tf_op jit(solution)/shard_map/reduce_sum | solution.py:38
  276.4 0.0 copy-done.1
  276.4 0.2 bitcast_add_fusion
  276.6 0.0 copy-start
  276.6 0.1 copy.35
  276.7 0.2 multiply_reduce_fusion.1
  276.9 0.9 clamp_convert_fusion
  277.8 0.0 all-gather.6.cloned.1.call-update
  277.8 0.1 copy.27
  277.9 90.4 %all-gather = bf16[32,56,16]{1,2,0:T(8,128)(2,1)S(1)} all-gather(bf16[1,56,16]{1,2,0:T(8,128)(2,1)S(1)} %copy.27), channel_id=1, replica_groups=mesh['tp'=4,'dp'=32] {'dp'}, dimensions={0}, use_global_device_ids=true | all-gather | bytes 59136 | tf_op jit(solution)/shard_map/all_gather | solution.py:43
  368.3 0.2 copy.30
  368.5 12.2 %all-gather.6.cloned.1.call-done = bf16[1792,16,128]{2,1,0:T(8,128)(2,1)} async-done(((bf16[56,16,128]{2,1,0:T(8,128)(2,1)}), bf16[1792,16,128]{2,1,0:T(8,128)(2,1)}) %all-gather.6.cloned.1.call-update) | async-done | bytes 7340048 | tf_op jit(solution)/shard_map/all_gather | solution.py:42
  380.7 7.6 %multiply_convert_fusion = bf16[1792,16,128]{2,1,0:T(8,128)(2,1)S(1)} fusion(bf16[1792,16,128]{2,1,0:T(8,128)(2,1)} %all-gather.6.cloned.1.call-done, f32[1792,16]{1,0:T(8,128)S(1)} %bitcast.42), kind=kLoop, calls=%fused_computation.4 | loop fusion | flops 11010048 | bytes 14794752 | tf_op jit(solution)/shard_map/convert_element_type | solution.py:50
  388.3 6.8 %copy.40 = bf16[224,8,16,128]{3,1,2,0:T(8,128)(2,1)} copy(bf16[224,8,16,128]{3,2,1,0:T(8,128)(2,1)S(1)} %bitcast.39) | data formatting | bytes 14680064
  395.1 0.0 copy-done
  (4 shorter events, 0.1 us)
Async XLA Ops:
  7.2 51.0 %all-gather.4.cloned.1.call-start = ((), (), s32[]{:S(2)}) async-start(), calls=%async_computation.2 | async-start | bytes 5242880 | tf_op jit(solution)/shard_map/all_gather | solution.py:22
  127.8 19.2 %all-to-all-start.1 = ((bf16[32,2,448]{2,1,0:T(2,128)(2,1)}), bf16[32,2,448]{2,1,0:T(2,128)(2,1)S(1)}, u32[]{:S(2)}, u32[]{:S(2)}) async-start(bf16[32,2,448]{2,1,0:T(2,128)(2,1)} %reshape.48), calls=%async_computation.1 | async-start | bytes 131072 | tf_op jit(solution)/shard_map/all_to_all | solution.py:34
  146.8 129.5 %copy-start.1 = (f32[56,2048]{1,0:T(8,128)S(1)}, f32[56,2048]{1,0:T(8,128)}, u32[]{:S(2)}) copy-start(f32[56,2048]{1,0:T(8,128)} %param.9) | copy-start | bytes 1376260
  147.0 121.6 %all-to-all-start = ((bf16[32,56,16,128]{3,2,1,0:T(8,128)(2,1)}), bf16[32,56,16,128]{3,2,1,0:T(8,128)(2,1)}, u32[]{:S(2)}, u32[]{:S(2)}) async-start(bf16[32,56,16,128]{3,2,1,0:T(8,128)(2,1)} %fusion.1), calls=%async_computation | async-start | bytes 14680064 | tf_op jit(solution)/shard_map/all_to_all | solution.py:33
  156.9 223.8 %all-gather.6.cloned.1.call-start = ((), (), s32[]{:S(2)}) async-start(), calls=%async_computation.3 | async-start | bytes 7569408 | tf_op jit(solution)/shard_map/all_gather | solution.py:42
  276.6 118.5 %copy-start = (f32[56,2048]{1,0:T(8,128)}, f32[56,2048]{1,0:T(8,128)S(1)}, u32[]{:S(2)}) copy-start(f32[56,2048]{1,0:T(8,128)S(1)} %bitcast_add_fusion) | copy-start | bytes 1376260
Sparse Core Ops, SparseCore 0:
  9.7 48.4 all-gather.3
  277.9 102.7 all-gather.5
where the time goes:
time: 403 us; the launch traced here: 402 us
  waiting for transfers between devices  175 us (43%)
  blocking collectives  90.4 us (22%)
  other arithmetic  47.7 us (12%)
  local copies, waits for them, and re-layouts  37.1 us (9%)
  starting transfers between devices  19.3 us (5%)
  matrix products  18.7 us (5%)
  between operations  14.2 us (4%)
    all_to_all x1, waiting for transfers between devices, body(): lax.all_to_all(codes_out, 'dp', split_axis=0, concat_axis=0, tiled=True)  111 us
    all_gather x1, blocking collectives, body(): lax.all_gather(new_scale.astype(jnp.bfloat16), 'dp', axis=0, tiled=True)  90.4 us
    all_gather x1, waiting for transfers between devices, body(): lax.all_gather(grad_out, 'tp', axis=1, tiled=True)  50.3 us
    unnamed x11, local copies, waits for them, and re-layouts  35.9 us
    dot_general x1, matrix products, body(): lax.dot_general(hidden, lax.all_gather(grad_out, 'tp', axis=1, tiled=True...  18.7 us
    unnamed x2, other arithmetic  13.6 us
    all_gather x1, waiting for transfers between devices, body(): lax.all_gather(new_codes, 'dp', axis=0, tiled=True)  12.2 us
    convert_element_type x2, other arithmetic, compress(): jnp.clip(blocks / scale[..., None], -clip_bound, clip_bound)  10.5 us
  transfers between devices with their start and end apart: 4, of which 4 were waited for; matrix products, arithmetic and copies ran while one was open for 3% of the time, Pallas kernels for 0%

commit v1 on v0

v1 whole, which is shorter than its diff:
```python
import jax
import jax.numpy as jnp
from jax import lax
from jax.experimental import pallas as pl
from jax.experimental.pallas import tpu as pltpu
from jax.sharding import PartitionSpec as P

CLIP = 1.5
BLOCK = 128
WAYS = 4
GRAY = (0, 1, 3, 2)
ROW_TILE = 256
GROUP = 128
MIB = 1024 * 1024
F32 = jnp.float32
BF16 = jnp.bfloat16
AXES = ("tp", "dp")


def permute(array, phase, mask):
    pairs = []
    for tp in range(4):
        for x in range(4):
            for z in range(4):
                for half in range(2):
                    to_x, to_z, to_half = x, z, half
                    if phase == 2:
                        to_half = 1 - half
                    elif (tp + phase) % 2 == 0:
                        to_x = GRAY[GRAY[x] ^ mask]
                    else:
                        to_z = GRAY[GRAY[z] ^ mask]
                    pairs.append((tp * 32 + x * 8 + z * 2 + half, tp * 32 + to_x * 8 + to_z * 2 + to_half))
    return lax.ppermute(array, AXES, pairs)


def swap_tp(array, mask):
    return lax.ppermute(array, "tp", [(i, i ^ mask) for i in range(4)])


def clipped(part):
    square = jnp.sum(part * part, axis=1, keepdims=True) * (CLIP * CLIP / BLOCK) + CLIP * CLIP * 1e-06
    bound = square * lax.rsqrt(square)
    return jnp.clip(part, -bound, bound)


def coordinates():
    tp, dp = lax.axis_index("tp"), lax.axis_index("dp")
    return tp, dp // 8, (dp // 2) % 4, dp % 2


def ring_rows(first, second):
    tp, x, z, _ = coordinates()
    core = tp % 2
    on_x = first + core * (second - first)
    on_z = second + core * (first - second)
    code_x = x ^ (x >> 1) ^ on_x
    code_z = z ^ (z >> 1) ^ on_z
    return pl.multiple_of((code_x ^ (code_x >> 1)) * 448 + (code_z ^ (code_z >> 1)) * 112, 16)


def local_kernel(chunk, side, *refs):
    hidden, cotan, momentum, resid = refs[:4]
    send, keep, cross, values, grad = refs[-5:]
    depth, rows = hidden.shape
    width = cotan.shape[1]
    column = coordinates()[0] ^ (2 * chunk + side)

    def tile(hidden, momentum, resid):
        step = pl.program_id(0)
        grad[...] = jnp.dot(hidden[...].T, cotan[...], preferred_element_type=F32)

        def group(index, carry):
            at = pl.ds(pl.multiple_of(index * GROUP, GROUP), GROUP)
            to = pl.ds(pl.multiple_of(step * ROW_TILE + index * GROUP, GROUP), GROUP)
            for start in range(0, width, BLOCK):
                lanes = slice(start, start + BLOCK)
                total = 0.9 * momentum[at, lanes].astype(F32) + 0.1 * grad[at, lanes] + resid[at, lanes].astype(F32)
                values[to, lanes] = clipped(total).astype(BF16)
            return carry

        lax.fori_loop(0, ROW_TILE // GROUP, group, 0)

    pltpu.emit_pipeline(
        tile,
        grid=(rows // ROW_TILE,),
        in_specs=[
            pl.BlockSpec((depth, ROW_TILE), lambda i: (0, i)),
            pl.BlockSpec((ROW_TILE, width), lambda i: (i, column)),
            pl.BlockSpec((ROW_TILE, width), lambda i: (i, column)),
        ],
        out_specs=[],
    )(hidden, momentum, resid)

    for second in range(WAYS):
        for first in range(WAYS):
            piece = values[pl.ds(ring_rows(first, second), 112), :]
            if first == 0:
                keep[second] = piece
            elif first == 1 + side:
                send[0, second] = piece
            elif first == 2 - side:
                cross[second] = piece
            else:
                send[1, second] = piece


def local_values(chunk, side, hidden, cotan, momentum, resid, after):
    depth, rows = hidden.shape
    width = cotan.shape[1]
    out_shape = [shape(BF16, 2, WAYS, 112, width), shape(BF16, WAYS, 112, width), shape(BF16, WAYS, 112, width)]
    hbm, vmem = pl.BlockSpec(memory_space=pltpu.HBM), pl.BlockSpec(memory_space=pltpu.VMEM)
    return pl.pallas_call(
        lambda *refs: local_kernel(chunk, side, *refs),
        in_specs=[hbm, vmem, hbm, hbm] + [pl.BlockSpec(memory_space=pl.ANY)] * len(after),
        out_specs=[vmem] * 3,
        out_shape=out_shape,
        scratch_shapes=[pltpu.VMEM((rows, width), BF16), pltpu.VMEM((ROW_TILE, width), F32)],
        compiler_params=pltpu.CompilerParams(vmem_limit_bytes=12 * MIB),
        cost_estimate=pl.CostEstimate(
            flops=2 * rows * depth * width, bytes_accessed=2 * rows * (depth + 4 * width), transcendentals=0
        ),
        name="local_values",
    )(hidden, cotan, momentum, resid, *after)


def add(*terms):
    total = terms[0].astype(F32)
    for term in terms[1:]:
        total = total + term.astype(F32)
    return total


def small_call(kernel, name, out_shape, *args, after=()):
    count = len(args)
    moved = sum(a.size * a.dtype.itemsize for a in args) + sum(o.size * o.dtype.itemsize for o in out_shape)
    return pl.pallas_call(
        lambda *refs: kernel(*refs[:count], *refs[count + len(after) :]),
        in_specs=[pl.BlockSpec(memory_space=pltpu.VMEM)] * count + [pl.BlockSpec(memory_space=pl.ANY)] * len(after),
        out_specs=[pl.BlockSpec(memory_space=pltpu.VMEM)] * len(out_shape),
        out_shape=out_shape,
        compiler_params=pltpu.CompilerParams(vmem_limit_bytes=4 * MIB),
        cost_estimate=pl.CostEstimate(flops=moved, bytes_accessed=moved, transcendentals=0),
        name=name,
    )(*args, *after)


def shape(dtype, *dims):
    return jax.ShapeDtypeStruct(dims, dtype)


def forward_kernel(cross, got, out):
    out[...] = add(cross[...], got[1]).astype(BF16)


def ring_sum_kernel(keep0, keep1, r0, r1, u0, u1, *outs):
    width = keep0.shape[-1]
    for second, out in enumerate(outs):
        out[:, :width] = add(keep0[second], r0[0, second], u1[second]).astype(out.dtype)
        out[:, width:] = add(keep1[second], r1[0, second], u0[second]).astype(out.dtype)


def split_kernel(z0, w1, w2, w3, keep, send):
    total = add(z0[...], w1[...], w2[...], w3[...])
    low, high = total[:56], total[56:]
    is_low = coordinates()[3] == 0
    keep[...] = jnp.where(is_low, low, high)
    send[...] = jnp.where(is_low, high, low).astype(BF16)


def owner_kernel(keep, got, server, corrected, update):
    value = add(keep[...], got[...]) * (1.0 / 32) + server[...]
    corrected[...] = value
    for start in range(0, value.shape[1], BLOCK):
        lanes = slice(start, start + BLOCK)
        update[:, lanes] = clipped(value[:, lanes]).astype(BF16)


def pair_kernel(own, other, out):
    is_low = coordinates()[3] == 0
    out[:56] = jnp.where(is_low, own[...], other[...])
    out[56:] = jnp.where(is_low, other[...], own[...])


def stack_kernel(a, b, c, d, out0, out1):
    width = out0.shape[-1]
    for index, piece in enumerate((a, b, c, d)):
        out0[index] = piece[:, :width]
        out1[index] = piece[:, width:]


def place_kernel(pieces, *refs):
    count = len(pieces)
    out, sems = refs[-2:]
    tp = coordinates()[0]
    running = []
    for source, (first, chunk, side) in zip(refs[:count], pieces):
        width = source.shape[-1]
        columns = pl.ds(pl.multiple_of((tp ^ (2 * chunk + side)) * width, width), width)
        for second in range(WAYS):
            rows = pl.ds(ring_rows(first, second), 112)
            copy = pltpu.make_async_copy(source.at[second], out.at[rows, columns], sems.at[len(running)])
            copy.start()
            running.append(copy)
    for copy in running:
        copy.wait()


def place(pieces, arrays, rows, columns, so_far):
    chained = so_far is not None
    any_space = pl.BlockSpec(memory_space=pl.ANY)
    return pl.pallas_call(
        lambda *refs: place_kernel(pieces, *refs),
        in_specs=[pl.BlockSpec(memory_space=pltpu.VMEM)] * len(arrays) + [any_space] * chained,
        out_specs=any_space,
        out_shape=shape(BF16, rows, columns),
        scratch_shapes=[pltpu.SemaphoreType.DMA((WAYS * len(arrays),))],
        input_output_aliases={len(arrays): 0} if chained else {},
        compiler_params=pltpu.CompilerParams(vmem_limit_bytes=4 * MIB),
        cost_estimate=pl.CostEstimate(flops=0, bytes_accessed=arrays[0].size * 4 * len(arrays), transcendentals=0),
        name="place_update",
    )(*arrays, *((so_far,) if chained else ()))


class Chunk:
    def __init__(self, index, data, cotans):
        self.index, self.data, self.cotans = index, data, cotans
        self.rows, self.width = data[0].shape[1], cotans[0].shape[1]
        self.part = shape(BF16, WAYS, 112, self.width)
        self.held = {}

    def local(self, side, after):
        hidden, momentum, resid, _ = self.data
        send, keep, cross = local_values(self.index, side, hidden, self.cotans[side], momentum, resid, after)
        self.held[side] = (permute(send, 0, 1 + side), keep, cross)
        return cross

    def forward(self, side, after):
        got, _, _ = self.held[side]
        (out,) = small_call(forward_kernel, "forward", [self.part], self.held[side][2], got, after=after)
        self.held[side] += (permute(out, 0, 2 - side),)
        return out

    def ring_sum(self, after):
        (r0, keep0, _, u1), (r1, keep1, _, u0) = self.held[0], self.held[1]
        wide = [shape(t, 112, 2 * self.width) for t in (F32, BF16, BF16, BF16)]
        outs = small_call(ring_sum_kernel, "ring_sum", wide, keep0, keep1, r0, r1, u0, u1, after=after)
        self.sums = [outs[0]] + [permute(z, 1, mask) for mask, z in enumerate(outs) if mask]
        return outs[0]

    def split(self, after):
        out_shape = [shape(F32, 56, 2 * self.width), shape(BF16, 56, 2 * self.width)]
        self.kept, send = small_call(split_kernel, "split", out_shape, *self.sums, after=after)
        self.got = permute(send, 2, 0)
        return send

    def owner(self, after):
        tp = lax.axis_index("tp")
        server_err, width = self.data[3], self.width
        at = [(tp ^ (2 * self.index + side)) * width for side in (0, 1)]
        server = jnp.concatenate([lax.dynamic_slice_in_dim(server_err, a, width, 1) for a in at], 1)
        out_shape = [shape(F32, 56, 2 * width), shape(BF16, 56, 2 * width)]
        value, self.mine = small_call(owner_kernel, "owner", out_shape, self.kept, self.got, server, after=after)
        self.corrected = [(at[side], value[:, side * width : (side + 1) * width]) for side in (0, 1)]
        self.other = permute(self.mine, 2, 0)
        return self.mine

    def pair(self, after):
        (out,) = small_call(
            pair_kernel, "pair", [shape(BF16, 112, 2 * self.width)], self.mine, self.other, after=after
        )
        self.ring = [out] + [permute(out, 1, mask) for mask in (1, 2, 3)]
        return out

    def stack(self, after):
        own0, own1 = small_call(stack_kernel, "stack", [self.part, self.part], *self.ring, after=after)
        a0, b1 = permute(own0, 0, 1), permute(own1, 0, 2)
        b0, a1 = permute(own0, 0, 2), permute(own1, 0, 1)
        self.near = (own0, own1, a0, a1, b0, b1)
        self.far = (permute(a0, 0, 2), permute(b1, 0, 1))
        return own0

    def place(self, update, far):
        if far:
            return place([(3, self.index, 0), (3, self.index, 1)], self.far, self.rows, 4 * self.width, update)
        pieces = [(first, self.index, side) for first in (0, 1, 2) for side in (0, 1)]
        return place(pieces, self.near, self.rows, 4 * self.width, update)


def body(hidden, grad_out, momentum, worker_err, server_err):
    far = swap_tp(grad_out, 2)
    near = swap_tp(grad_out, 1)
    data = (hidden, momentum, worker_err[0], server_err)
    a = Chunk(0, data, (grad_out, near))
    b = Chunk(1, data, (far, swap_tp(far, 1)))
    last = ()
    for step in (
        lambda w: a.local(0, w),
        lambda w: a.local(1, w),
        lambda w: a.forward(0, w),
        lambda w: a.forward(1, w),
        lambda w: b.local(0, w),
        a.ring_sum,
        lambda w: b.local(1, w),
        a.split,
        lambda w: b.forward(0, w),
        a.owner,
        lambda w: b.forward(1, w),
        a.pair,
        b.ring_sum,
        a.stack,
        b.split,
        b.owner,
        b.pair,
        b.stack,
    ):
        last = (step(last),)
    update = a.place(None, False)
    update = a.place(update, True)
    update = b.place(update, False)
    update = b.place(update, True)
    whole = jnp.zeros(server_err.shape, F32)
    for at, value in a.corrected + b.corrected:
        whole = lax.dynamic_update_slice_in_dim(whole, value, at, 1)
    return (update, whole)


def solution(mesh):
    placed = (
        P("dp", "tp"),
        P("dp", "tp"),
        P("tp", None),
        P("dp", "tp", None),
        P(("tp", "dp"), None),
    )
    return jax.shard_map(
        body,
        mesh=mesh,
        in_specs=placed,
        out_specs=(P("tp", None), P(("tp", "dp"), None)),
        check_vma=False,
    )
```

time: 403 us -> 168 us (0.42)
  waiting for transfers between devices: 175 us -> 57.3 us
  blocking collectives: 90.4 us -> 0 us
  other arithmetic: 47.7 us -> 0.03 us
  Pallas kernels: 0 us -> 39.2 us
  starting transfers between devices: 19.3 us -> 58.1 us
  local copies, waits for them, and re-layouts: 37.1 us -> 11.5 us
  matrix products: 18.7 us -> 0 us
  between operations: 14.2 us -> 1.08 us
    all_to_all x2 -> x0, waiting for transfers between devices: 111 us -> none  [the longest x1 111 us: body(): lax.all_to_all(codes_out, 'dp', split_axis=0, concat_axis=0, tiled=True)]
    all_gather x1 -> x0, blocking collectives: 90.4 us -> none  [body(): lax.all_gather(new_scale.astype(jnp.bfloat16), 'dp', axis=0, tiled=True)]
    all_gather x2 -> x0, waiting for transfers between devices: 62.4 us -> none  [the longest x1 50.3 us: body(): lax.all_gather(grad_out, 'tp', axis=1, tiled=True)]
    ppermute x0 -> x39, starting transfers between devices: none -> 58.1 us  [the longest x36 55.8 us: permute(): return lax.ppermute(array, AXES, pairs)]
    ppermute x0 -> x39, waiting for transfers between devices: none -> 57.3 us  [the longest x36 57.3 us: permute(): return lax.ppermute(array, AXES, pairs)]
    pallas_call x0 -> x22, Pallas kernels: none -> 39.2 us  [the longest x4 30.1 us: local_values(): pl.pallas_call(lambda *refs: local_kernel(chunk, side, *refs), in_specs=[...]
    unnamed x11 -> x22, local copies, waits for them, and re-layouts: 35.9 us -> 10.3 us
    all_to_all x2 -> x0, starting transfers between devices: 19.3 us -> none  [the longest x1 9.88 us: body(): lax.all_to_all(codes_out, 'dp', split_axis=0, concat_axis=0, tiled=True)]
  transfers between devices with their start and end apart: 4 -> 39, of which waited for: 4 -> 19; matrix products, arithmetic and copies ran while one was open for 3% -> 1% of each run, Pallas kernels for 0% -> 23%
where the time goes in v1:
time: 168 us; the launch traced here: 167 us
  starting transfers between devices  58.1 us (35%)
  waiting for transfers between devices  57.3 us (34%)
  Pallas kernels  39.2 us (23%)
  local copies, waits for them, and re-layouts  11.5 us (7%)
    ppermute x36, waiting for transfers between devices, permute(): return lax.ppermute(array, AXES, pairs)  57.3 us
    ppermute x36, starting transfers between devices, permute(): return lax.ppermute(array, AXES, pairs)  55.8 us
    pallas_call x4, Pallas kernels, local_values(): pl.pallas_call(lambda *refs: local_kernel(chunk, side, *refs), in_specs=[...  30.1 us
    unnamed x22, local copies, waits for them, and re-layouts  10.3 us
    pallas_call x4, Pallas kernels, place(): pl.pallas_call(lambda *refs: place_kernel(pieces, *refs), in_specs=[pl.Bl...  5.58 us
    pallas_call x14, Pallas kernels, small_call(): pl.pallas_call(lambda *refs: kernel(*refs[:count], *refs[count + len(afte...  3.53 us
  transfers between devices with their start and end apart: 39, of which 19 were waited for; matrix products, arithmetic and copies ran while one was open for 1% of the time, Pallas kernels for 23%

profile of v1, /device:TPU:0, one launch (start us, length us, event | category | flops | bytes accessed | tf_op | source)
XLA Modules:
  0.0 167.3 jit_solution(18440149761581261592)
XLA Ops:
  0.7 1.7 %collective-permute-start = (bf16[1024,512]{1,0:T(8,128)(2,1)}, bf16[1024,512]{1,0:T(8,128)(2,1)S(1)}, u32[]{:S(2)}, u32[]{:S(2)}) collective-permute-start(bf16[1024,512]{1,0:T(8,128)(2,1)} %refs_1_.1), channel_id=1, source_target_pairs={{0,64},{32,96},{64,0},{96,32},{1,65},{33,97},{65,1},{97,33},{2,66}... | collective-permute-start | bytes 3145736 | tf_op jit(solution)/shard_map/ppermute | solution.py:38
  2.5 3.1 %copy-done = bf16[1792,2048]{1,0:T(8,128)(2,1)S(1)} copy-done((bf16[1792,2048]{1,0:T(8,128)(2,1)S(1)}, bf16[1792,2048]{1,0:T(8,128)(2,1)}, u32[]{:S(2)}) %copy-start) | copy-done | bytes 7340056
  5.6 3.1 %copy-done.2 = bf16[1,1792,2048]{2,1,0:T(8,128)(2,1)S(1)} copy-done((bf16[1,1792,2048]{2,1,0:T(8,128)(2,1)S(1)}, bf16[1,1792,2048]{2,1,0:T(8,128)(2,1)}, u32[]{:S(2)}) %copy-start.2) | copy-done | bytes 7340056
  8.7 2.0 %copy-done.4 = bf16[1024,1792]{1,0:T(8,128)(2,1)S(1)} copy-done((bf16[1024,1792]{1,0:T(8,128)(2,1)S(1)}, bf16[1024,1792]{1,0:T(8,128)(2,1)}, u32[]{:S(2)}) %copy-start.4) | copy-done | bytes 3670040
  10.7 1.2 copy-done.5
  11.9 7.0 %local_values.4 = (bf16[2,4,112,512]{3,2,1,0:T(8,128)(2,1)S(1)}, bf16[4,112,512]{2,1,0:T(8,128)(2,1)S(1)}, bf16[4,112,512]{2,1,0:T(8,128)(2,1)S(1)}) custom-call(bf16[1024,1792]{1,0:T(8,128)(2,1)S(1)} %copy-done.4, bf16[1024,512]{1,0:T(8,128)(2,1)S(1)} %copy-done.5, bf16[1792,2048]{1,0:T(8,128)(2,1)S(1)} %copy-done, bf16[1792,2048]{1,0:T(8,128)(2,1)S(1)} %bitcast.1), custom_call_target="tpu_custom_call" | custom-call | flops 1879048192 | bytes 11010048 | tf_op jit(solution)/shard_map/local_values/pallas_call | solution.py:113
  19.0 1.6 collective-permute-start.3
  20.6 7.1 %local_values.5 = (bf16[2,4,112,512]{3,2,1,0:T(8,128)(2,1)S(1)}, bf16[4,112,512]{2,1,0:T(8,128)(2,1)S(1)}, bf16[4,112,512]{2,1,0:T(8,128)(2,1)S(1)}) custom-call(bf16[1024,1792]{1,0:T(8,128)(2,1)S(1)} %copy-done.4, bf16[1024,512]{1,0:T(8,128)(2,1)S(1)} %collective-permute-done.1.refs_1_, bf16[1792,2048]{1,0:T(8,128)(2,1)S(1)} %copy-done.1, ...), custom_call_target="tpu_custom_call" | custom-call | flops 1879048192 | bytes 11010048 | tf_op jit(solution)/shard_map/local_values/pallas_call | solution.py:113
  27.7 2.2 %collective-permute-start.2 = (bf16[2,4,112,512]{3,2,1,0:T(8,128)(2,1)S(1)}, bf16[2,4,112,512]{3,2,1,0:T(8,128)(2,1)S(1)}, u32[]{:S(2)}, u32[]{:S(2)}) collective-permute-start(bf16[2,4,112,512]{3,2,1,0:T(8,128)(2,1)S(1)} %get-tuple-element.36), channel_id=1, source_target_pairs={{0,24},{1,25},{2,26},{3,27},{4,28},{5,29},{6,30},{7,31},{8,16},{9,... | collective-permute-start | bytes 2752520 | tf_op jit(solution)/shard_map/ppermute | solution.py:34
  29.8 0.4 collective-permute-start.4
  30.3 2.2 %collective-permute-done.3.refs_1_.refs_2_ = bf16[2,4,112,512]{3,2,1,0:T(8,128)(2,1)S(1)} collective-permute-done((bf16[2,4,112,512]{3,2,1,0:T(8,128)(2,1)S(1)}, bf16[2,4,112,512]{3,2,1,0:T(8,128)(2,1)S(1)}, u32[]{:S(2)}, u32[]{:S(2)}) %collective-permute-start.3) | collective-permute-done | bytes 917536 | tf_op jit(solution)/shard_map/ppermute | solution.py:34
  32.6 2.8 %collective-permute-start.6 = (bf16[4,112,512]{2,1,0:T(8,128)(2,1)S(1)}, bf16[4,112,512]{2,1,0:T(8,128)(2,1)S(1)}, u32[]{:S(2)}, u32[]{:S(2)}) collective-permute-start(bf16[4,112,512]{2,1,0:T(8,128)(2,1)S(1)} %forward.4.refs_2_), channel_id=1, source_target_pairs={{0,24},{1,25},{2,26},{3,27},{4,28},{5,29},{6,30},{7,31},{8,16},{9,... | collective-permute-start | bytes 1376264 | tf_op jit(solution)/shard_map/ppermute | solution.py:34
  35.4 6.9 %collective-permute-done.2.refs_1_.refs_3_ = bf16[2,4,112,512]{3,2,1,0:T(8,128)(2,1)S(1)} collective-permute-done((bf16[2,4,112,512]{3,2,1,0:T(8,128)(2,1)S(1)}, bf16[2,4,112,512]{3,2,1,0:T(8,128)(2,1)S(1)}, u32[]{:S(2)}, u32[]{:S(2)}) %collective-permute-start.2) | collective-permute-done | bytes 917536 | tf_op jit(solution)/shard_map/ppermute | solution.py:34
  42.6 8.0 %local_values.6 = (bf16[2,4,112,512]{3,2,1,0:T(8,128)(2,1)}, bf16[4,112,512]{2,1,0:T(8,128)(2,1)S(1)}, bf16[4,112,512]{2,1,0:T(8,128)(2,1)S(1)}) custom-call(bf16[1024,1792]{1,0:T(8,128)(2,1)S(1)} %copy-done.4, bf16[1024,512]{1,0:T(8,128)(2,1)S(1)} %collective-permute-done.refs_1_, bf16[1792,2048]{1,0:T(8,128)(2,1)S(1)} %copy-done.1, ...), custom_call_target="tpu_custom_call" | custom-call | flops 1879048192 | bytes 11010048 | tf_op jit(solution)/shard_map/local_values/pallas_call | solution.py:113
  50.6 2.0 %collective-permute-start.7 = (bf16[2,4,112,512]{3,2,1,0:T(8,128)(2,1)}, bf16[2,4,112,512]{3,2,1,0:T(8,128)(2,1)S(1)}, u32[]{:S(2)}, u32[]{:S(2)}) collective-permute-start(bf16[2,4,112,512]{3,2,1,0:T(8,128)(2,1)} %get-tuple-element.44), channel_id=1, source_target_pairs={{0,8},{1,9},{2,10},{3,11},{4,12},{5,13},{6,14},{7,15},{8,0},{9,1},... | collective-permute-start | bytes 2752520 | tf_op jit(solution)/shard_map/ppermute | solution.py:34
  52.6 1.0 ring_sum.2
  53.6 8.0 %local_values.7 = (bf16[2,4,112,512]{3,2,1,0:T(8,128)(2,1)}, bf16[4,112,512]{2,1,0:T(8,128)(2,1)S(1)}, bf16[4,112,512]{2,1,0:T(8,128)(2,1)S(1)}) custom-call(bf16[1024,1792]{1,0:T(8,128)(2,1)S(1)} %copy-done.4, bf16[1024,512]{1,0:T(8,128)(2,1)S(1)} %collective-permute-done.4.refs_1_, bf16[1792,2048]{1,0:T(8,128)(2,1)S(1)} %copy-done.1, ...), custom_call_target="tpu_custom_call" | custom-call | flops 1879048192 | bytes 11010048 | tf_op jit(solution)/shard_map/local_values/pallas_call | solution.py:113
  61.6 0.8 copy-done.8
  62.4 2.1 %collective-permute-start.8 = (bf16[2,4,112,512]{3,2,1,0:T(8,128)(2,1)}, bf16[2,4,112,512]{3,2,1,0:T(8,128)(2,1)S(1)}, u32[]{:S(2)}, u32[]{:S(2)}) collective-permute-start(bf16[2,4,112,512]{3,2,1,0:T(8,128)(2,1)} %get-tuple-element.45), channel_id=1, source_target_pairs={{0,24},{1,25},{2,26},{3,27},{4,28},{5,29},{6,30},{7,31},{8,16},{9,... | collective-permute-start | bytes 2752520 | tf_op jit(solution)/shard_map/ppermute | solution.py:34
  64.5 4.0 %collective-permute-start.10 = (bf16[112,1024]{1,0:T(8,128)(2,1)}, bf16[112,1024]{1,0:T(8,128)(2,1)S(1)}, u32[]{:S(2)}, u32[]{:S(2)}) collective-permute-start(bf16[112,1024]{1,0:T(8,128)(2,1)} %get-tuple-element.48), channel_id=1, source_target_pairs={{0,6},{1,7},{2,4},{3,5},{4,2},{5,3},{6,0},{7,1},{8,14},{9,15},{10,... | collective-permute-start | bytes 688136 | tf_op jit(solution)/shard_map/ppermute | solution.py:34
  68.5 0.9 collective-permute-start.9
  69.4 1.2 constant_dynamic-slice_fusion.1
  70.6 7.1 %collective-permute-done.10.refs_2_ = bf16[112,1024]{1,0:T(8,128)(2,1)S(1)} collective-permute-done((bf16[112,1024]{1,0:T(8,128)(2,1)}, bf16[112,1024]{1,0:T(8,128)(2,1)S(1)}, u32[]{:S(2)}, u32[]{:S(2)}) %collective-permute-start.10) | collective-permute-done | bytes 229408 | tf_op jit(solution)/shard_map/ppermute | solution.py:34
  77.7 1.2 split.2
  78.9 3.0 %collective-permute-start.12 = (bf16[56,1024]{1,0:T(8,128)(2,1)S(1)}, bf16[56,1024]{1,0:T(8,128)(2,1)S(1)}, u32[]{:S(2)}, u32[]{:S(2)}) collective-permute-start(bf16[56,1024]{1,0:T(8,128)(2,1)S(1)} %get-tuple-element.51.refs_2_), channel_id=1, source_target_pairs={{0,1},{1,0},{2,3},{3,2},{4,5},{5,4},{6,7},{7,6},{8,9},{9,8},{10,11... | collective-permute-start | bytes 344072 | tf_op jit(solution)/shard_map/ppermute | solution.py:34
  82.0 1.2 collective-permute-start.14
  83.2 2.1 %collective-permute-done.12.refs_1_ = bf16[56,1024]{1,0:T(8,128)(2,1)S(1)} collective-permute-done((bf16[56,1024]{1,0:T(8,128)(2,1)S(1)}, bf16[56,1024]{1,0:T(8,128)(2,1)S(1)}, u32[]{:S(2)}, u32[]{:S(2)}) %collective-permute-start.12) | collective-permute-done | bytes 114720 | tf_op jit(solution)/shard_map/ppermute | solution.py:34
  85.6 3.0 %collective-permute-start.15 = (bf16[56,1024]{1,0:T(8,128)(2,1)S(1)}, bf16[56,1024]{1,0:T(8,128)(2,1)S(1)}, u32[]{:S(2)}, u32[]{:S(2)}) collective-permute-start(bf16[56,1024]{1,0:T(8,128)(2,1)S(1)} %get-tuple-element.52.refs_2_.refs_0_), channel_id=1, source_target_pairs={{0,1},{1,0},{2,3},{3,2},{4,5},{5,4},{6,7},{7,6},{8,9},{9,8},{10,11... | collective-permute-start | bytes 344072 | tf_op jit(solution)/shard_map/ppermute | solution.py:34
  88.6 3.4 %collective-permute-done.15.refs_1_ = bf16[56,1024]{1,0:T(8,128)(2,1)S(1)} collective-permute-done((bf16[56,1024]{1,0:T(8,128)(2,1)S(1)}, bf16[56,1024]{1,0:T(8,128)(2,1)S(1)}, u32[]{:S(2)}, u32[]{:S(2)}) %collective-permute-start.15) | collective-permute-done | bytes 114720 | tf_op jit(solution)/shard_map/ppermute | solution.py:34
  92.1 4.3 %collective-permute-start.20 = (bf16[112,1024]{1,0:T(8,128)(2,1)S(1)}, bf16[112,1024]{1,0:T(8,128)(2,1)S(1)}, u32[]{:S(2)}, u32[]{:S(2)}) collective-permute-start(bf16[112,1024]{1,0:T(8,128)(2,1)S(1)} %pair.2.refs_6_.refs_0_), channel_id=1, source_target_pairs={{0,6},{1,7},{2,4},{3,5},{4,2},{5,3},{6,0},{7,1},{8,14},{9,15},{10,... | collective-permute-start | bytes 688136 | tf_op jit(solution)/shard_map/ppermute | solution.py:34
  96.4 1.4 collective-permute-start.21
  97.8 0.6 collective-permute-done.13.refs_4_
  98.4 0.3 ring_sum.3
  98.9 4.9 %collective-permute-start.17 = (bf16[112,1024]{1,0:T(8,128)(2,1)S(1)}, bf16[112,1024]{1,0:T(8,128)(2,1)S(1)}, u32[]{:S(2)}, u32[]{:S(2)}) collective-permute-start(bf16[112,1024]{1,0:T(8,128)(2,1)S(1)} %get-tuple-element.55), channel_id=1, source_target_pairs={{0,6},{1,7},{2,4},{3,5},{4,2},{5,3},{6,0},{7,1},{8,14},{9,15},{10,... | collective-permute-start | bytes 688136 | tf_op jit(solution)/shard_map/ppermute | solution.py:34
  103.8 1.4 collective-permute-start.18
  105.2 2.9 %collective-permute-start.33 = (bf16[4,112,512]{2,1,0:T(8,128)(2,1)S(1)}, bf16[4,112,512]{2,1,0:T(8,128)(2,1)S(1)}, u32[]{:S(2)}, u32[]{:S(2)}) collective-permute-start(bf16[4,112,512]{2,1,0:T(8,128)(2,1)S(1)} %get-tuple-element.57.refs_4_.refs_0_), channel_id=1, source_target_pairs={{0,8},{1,9},{2,10},{3,11},{4,12},{5,13},{6,14},{7,15},{8,0},{9,1},... | collective-permute-start | bytes 1376264 | tf_op jit(solution)/shard_map/ppermute | solution.py:34
  108.2 4.0 %collective-permute-done.17.refs_2_ = bf16[112,1024]{1,0:T(8,128)(2,1)S(1)} collective-permute-done((bf16[112,1024]{1,0:T(8,128)(2,1)S(1)}, bf16[112,1024]{1,0:T(8,128)(2,1)S(1)}, u32[]{:S(2)}, u32[]{:S(2)}) %collective-permute-start.17) | collective-permute-done | bytes 229408 | tf_op jit(solution)/shard_map/ppermute | solution.py:34
  112.2 3.0 %collective-permute-done.18.refs_3_ = bf16[112,1024]{1,0:T(8,128)(2,1)S(1)} collective-permute-done((bf16[112,1024]{1,0:T(8,128)(2,1)S(1)}, bf16[112,1024]{1,0:T(8,128)(2,1)S(1)}, u32[]{:S(2)}, u32[]{:S(2)}) %collective-permute-start.18) | collective-permute-done | bytes 229408 | tf_op jit(solution)/shard_map/ppermute | solution.py:34
  115.2 3.0 %collective-permute-start.22 = (bf16[56,1024]{1,0:T(8,128)(2,1)S(1)}, bf16[56,1024]{1,0:T(8,128)(2,1)S(1)}, u32[]{:S(2)}, u32[]{:S(2)}) collective-permute-start(bf16[56,1024]{1,0:T(8,128)(2,1)S(1)} %get-tuple-element.59.refs_3_), channel_id=1, source_target_pairs={{0,1},{1,0},{2,3},{3,2},{4,5},{5,4},{6,7},{7,6},{8,9},{9,8},{10,11... | collective-permute-start | bytes 344072 | tf_op jit(solution)/shard_map/ppermute | solution.py:34
  118.2 3.4 %collective-permute-done.22.refs_1_ = bf16[56,1024]{1,0:T(8,128)(2,1)S(1)} collective-permute-done((bf16[56,1024]{1,0:T(8,128)(2,1)S(1)}, bf16[56,1024]{1,0:T(8,128)(2,1)S(1)}, u32[]{:S(2)}, u32[]{:S(2)}) %collective-permute-start.22) | collective-permute-done | bytes 114720 | tf_op jit(solution)/shard_map/ppermute | solution.py:34
  121.8 3.0 %collective-permute-start.23 = (bf16[56,1024]{1,0:T(8,128)(2,1)S(1)}, bf16[56,1024]{1,0:T(8,128)(2,1)S(1)}, u32[]{:S(2)}, u32[]{:S(2)}) collective-permute-start(bf16[56,1024]{1,0:T(8,128)(2,1)S(1)} %get-tuple-element.60.refs_0_.refs_2_), channel_id=1, source_target_pairs={{0,1},{1,0},{2,3},{3,2},{4,5},{5,4},{6,7},{7,6},{8,9},{9,8},{10,11... | collective-permute-start | bytes 344072 | tf_op jit(solution)/shard_map/ppermute | solution.py:34
  124.7 3.4 %collective-permute-done.23.refs_1_ = bf16[56,1024]{1,0:T(8,128)(2,1)S(1)} collective-permute-done((bf16[56,1024]{1,0:T(8,128)(2,1)S(1)}, bf16[56,1024]{1,0:T(8,128)(2,1)S(1)}, u32[]{:S(2)}, u32[]{:S(2)}) %collective-permute-start.23) | collective-permute-done | bytes 114720 | tf_op jit(solution)/shard_map/ppermute | solution.py:34
  128.4 1.5 collective-permute-start.25
  129.9 2.5 %collective-permute-start.26 = (bf16[112,1024]{1,0:T(8,128)(2,1)S(1)}, bf16[112,1024]{1,0:T(8,128)(2,1)S(1)}, u32[]{:S(2)}, u32[]{:S(2)}) collective-permute-start(bf16[112,1024]{1,0:T(8,128)(2,1)S(1)} %pair.3.refs_0_.refs_4_), channel_id=1, source_target_pairs={{0,4},{1,5},{2,6},{3,7},{4,0},{5,1},{6,2},{7,3},{8,12},{9,13},{10,... | collective-permute-start | bytes 688136 | tf_op jit(solution)/shard_map/ppermute | solution.py:34
  132.4 0.9 collective-permute-start.37
  133.3 3.5 %collective-permute-done.24.refs_1_ = bf16[112,1024]{1,0:T(8,128)(2,1)S(1)} collective-permute-done((bf16[112,1024]{1,0:T(8,128)(2,1)S(1)}, bf16[112,1024]{1,0:T(8,128)(2,1)S(1)}, u32[]{:S(2)}, u32[]{:S(2)}) %collective-permute-start.24) | collective-permute-done | bytes 229408 | tf_op jit(solution)/shard_map/ppermute | solution.py:34
  136.8 0.3 collective-permute-start.38
  137.1 2.1 %collective-permute-done.25.refs_2_ = bf16[112,1024]{1,0:T(8,128)(2,1)S(1)} collective-permute-done((bf16[112,1024]{1,0:T(8,128)(2,1)S(1)}, bf16[112,1024]{1,0:T(8,128)(2,1)S(1)}, u32[]{:S(2)}, u32[]{:S(2)}) %collective-permute-start.25) | collective-permute-done | bytes 229408 | tf_op jit(solution)/shard_map/ppermute | solution.py:34
  139.1 1.0 collective-permute-start.34
  140.2 1.8 %collective-permute-done.26.refs_3_ = bf16[112,1024]{1,0:T(8,128)(2,1)S(1)} collective-permute-done((bf16[112,1024]{1,0:T(8,128)(2,1)S(1)}, bf16[112,1024]{1,0:T(8,128)(2,1)S(1)}, u32[]{:S(2)}, u32[]{:S(2)}) %collective-permute-start.26) | collective-permute-done | bytes 229408 | tf_op jit(solution)/shard_map/ppermute | solution.py:34
  142.1 0.4 collective-permute-start.27
  142.5 1.7 %collective-permute-start.29 = (bf16[4,112,512]{2,1,0:T(8,128)(2,1)S(1)}, bf16[4,112,512]{2,1,0:T(8,128)(2,1)S(1)}, u32[]{:S(2)}, u32[]{:S(2)}) collective-permute-start(bf16[4,112,512]{2,1,0:T(8,128)(2,1)S(1)} %get-tuple-element.62.refs_1_), channel_id=1, source_target_pairs={{0,24},{1,25},{2,26},{3,27},{4,28},{5,29},{6,30},{7,31},{8,16},{9,... | collective-permute-start | bytes 1376264 | tf_op jit(solution)/shard_map/ppermute | solution.py:34
  144.4 2.1 %collective-permute-done.38.refs_4_ = bf16[4,112,512]{2,1,0:T(8,128)(2,1)S(1)} collective-permute-done((bf16[4,112,512]{2,1,0:T(8,128)(2,1)S(1)}, bf16[4,112,512]{2,1,0:T(8,128)(2,1)S(1)}, u32[]{:S(2)}, u32[]{:S(2)}) %collective-permute-start.38) | collective-permute-done | bytes 458784 | tf_op jit(solution)/shard_map/ppermute | solution.py:34
  146.5 4.9 %collective-permute-done.34.refs_0_ = bf16[4,112,512]{2,1,0:T(8,128)(2,1)S(1)} collective-permute-done((bf16[4,112,512]{2,1,0:T(8,128)(2,1)S(1)}, bf16[4,112,512]{2,1,0:T(8,128)(2,1)S(1)}, u32[]{:S(2)}, u32[]{:S(2)}) %collective-permute-start.34) | collective-permute-done | bytes 458784 | tf_op jit(solution)/shard_map/ppermute | solution.py:34
  151.4 0.3 collective-permute-start.32
  151.7 3.0 %collective-permute-start.28 = (bf16[4,112,512]{2,1,0:T(8,128)(2,1)S(1)}, bf16[4,112,512]{2,1,0:T(8,128)(2,1)S(1)}, u32[]{:S(2)}, u32[]{:S(2)}) collective-permute-start(bf16[4,112,512]{2,1,0:T(8,128)(2,1)S(1)} %collective-permute-done.27.refs_2_), channel_id=1, source_target_pairs={{0,24},{1,25},{2,26},{3,27},{4,28},{5,29},{6,30},{7,31},{8,16},{9,... | collective-permute-start | bytes 1376264 | tf_op jit(solution)/shard_map/ppermute | solution.py:34
  154.6 1.7 %collective-permute-done.29.refs_5_ = bf16[4,112,512]{2,1,0:T(8,128)(2,1)S(1)} collective-permute-done((bf16[4,112,512]{2,1,0:T(8,128)(2,1)S(1)}, bf16[4,112,512]{2,1,0:T(8,128)(2,1)S(1)}, u32[]{:S(2)}, u32[]{:S(2)}) %collective-permute-start.29) | collective-permute-done | bytes 458784 | tf_op jit(solution)/shard_map/ppermute | solution.py:34
  156.4 1.9 %place_update.4.refs_2_ = bf16[1792,2048]{1,0:T(8,128)(2,1)} custom-call(bf16[4,112,512]{2,1,0:T(8,128)(2,1)S(1)} %get-tuple-element.57.refs_4_.refs_0_, bf16[4,112,512]{2,1,0:T(8,128)(2,1)S(1)} %get-tuple-element.63.refs_1_, bf16[4,112,512]{2,1,0:T(8,128)(2,1)S(1)} %collective-permute-done.33.refs_2_, ...), custom_call_target="tpu_custom_call" | custom-call | bytes 5505024 | tf_op jit(solution)/shard_map/place_update/pallas_call | solution.py:212
  158.3 1.0 place_update.5.refs_6_
  159.3 1.2 collective-permute-done.31.refs_3_
  160.5 0.7 collective-permute-done.32.refs_4_
  161.2 1.7 %place_update.6.refs_2_ = bf16[1792,2048]{1,0:T(8,128)(2,1)} custom-call(bf16[4,112,512]{2,1,0:T(8,128)(2,1)S(1)} %get-tuple-element.61.refs_0_, bf16[4,112,512]{2,1,0:T(8,128)(2,1)S(1)} %get-tuple-element.62.refs_1_, bf16[4,112,512]{2,1,0:T(8,128)(2,1)S(1)} %collective-permute-done.27.refs_2_, ...), custom_call_target="tpu_custom_call", output_to_operand_aliasing={{}: (6, {})} | custom-call | bytes 5505024 | tf_op jit(solution)/shard_map/place_update/pallas_call | solution.py:212
  163.0 3.2 %collective-permute-done.28.refs_0_ = bf16[4,112,512]{2,1,0:T(8,128)(2,1)S(1)} collective-permute-done((bf16[4,112,512]{2,1,0:T(8,128)(2,1)S(1)}, bf16[4,112,512]{2,1,0:T(8,128)(2,1)S(1)}, u32[]{:S(2)}, u32[]{:S(2)}) %collective-permute-start.28) | collective-permute-done | bytes 458784 | tf_op jit(solution)/shard_map/ppermute | solution.py:34
  166.2 1.0 place_update.7
  (66 shorter events, 2.0 us)
Async XLA Ops:
  0.6 19.9 %collective-permute-start.1 = (bf16[1024,512]{1,0:T(8,128)(2,1)}, bf16[1024,512]{1,0:T(8,128)(2,1)S(1)}, u32[]{:S(2)}, u32[]{:S(2)}) collective-permute-start(bf16[1024,512]{1,0:T(8,128)(2,1)} %refs_1_.1), channel_id=1, source_target_pairs={{0,32},{32,0},{64,96},{96,64},{1,33},{33,1},{65,97},{97,65},{2,34}... | collective-permute-start | bytes 3145736 | tf_op jit(solution)/shard_map/ppermute | solution.py:38
  0.7 29.1 %collective-permute-start = (bf16[1024,512]{1,0:T(8,128)(2,1)}, bf16[1024,512]{1,0:T(8,128)(2,1)S(1)}, u32[]{:S(2)}, u32[]{:S(2)}) collective-permute-start(bf16[1024,512]{1,0:T(8,128)(2,1)} %refs_1_.1), channel_id=1, source_target_pairs={{0,64},{32,96},{64,0},{96,32},{1,65},{33,97},{65,1},{97,33},{2,66}... | collective-permute-start | bytes 3145736 | tf_op jit(solution)/shard_map/ppermute | solution.py:38
  2.5 3.1 %copy-start = (bf16[1792,2048]{1,0:T(8,128)(2,1)S(1)}, bf16[1792,2048]{1,0:T(8,128)(2,1)}, u32[]{:S(2)}) copy-start(bf16[1792,2048]{1,0:T(8,128)(2,1)} %refs_2_.7) | copy-start | bytes 22020100
  5.6 3.1 %copy-start.2 = (bf16[1,1792,2048]{2,1,0:T(8,128)(2,1)S(1)}, bf16[1,1792,2048]{2,1,0:T(8,128)(2,1)}, u32[]{:S(2)}) copy-start(bf16[1,1792,2048]{2,1,0:T(8,128)(2,1)} %param.8) | copy-start | bytes 22020100
  8.7 2.0 %copy-start.4 = (bf16[1024,1792]{1,0:T(8,128)(2,1)S(1)}, bf16[1024,1792]{1,0:T(8,128)(2,1)}, u32[]{:S(2)}) copy-start(bf16[1024,1792]{1,0:T(8,128)(2,1)} %refs_0_.7) | copy-start | bytes 11010052
  10.7 1.2 copy-start.5
  11.9 8.6 %copy-start.1 = (bf16[1792,2048]{1,0:T(8,128)(2,1)S(1)}, bf16[1792,2048]{1,0:T(8,128)(2,1)}, u32[]{:S(2)}) copy-start(bf16[1792,2048]{1,0:T(8,128)(2,1)} %refs_2_.7) | copy-start | bytes 22020100
  11.9 8.6 %copy-start.3 = (bf16[1,1792,2048]{2,1,0:T(8,128)(2,1)S(1)}, bf16[1,1792,2048]{2,1,0:T(8,128)(2,1)}, u32[]{:S(2)}) copy-start(bf16[1,1792,2048]{2,1,0:T(8,128)(2,1)} %param.8) | copy-start | bytes 22020100
  19.0 13.5 %collective-permute-start.3 = (bf16[2,4,112,512]{3,2,1,0:T(8,128)(2,1)S(1)}, bf16[2,4,112,512]{3,2,1,0:T(8,128)(2,1)S(1)}, u32[]{:S(2)}, u32[]{:S(2)}) collective-permute-start(bf16[2,4,112,512]{3,2,1,0:T(8,128)(2,1)S(1)} %get-tuple-element.37), channel_id=1, source_target_pairs={{0,8},{1,9},{2,10},{3,11},{4,12},{5,13},{6,14},{7,15},{8,0},{9,1},... | collective-permute-start | bytes 2752520 | tf_op jit(solution)/shard_map/ppermute | solution.py:34
  27.7 14.7 %collective-permute-start.2 = (bf16[2,4,112,512]{3,2,1,0:T(8,128)(2,1)S(1)}, bf16[2,4,112,512]{3,2,1,0:T(8,128)(2,1)S(1)}, u32[]{:S(2)}, u32[]{:S(2)}) collective-permute-start(bf16[2,4,112,512]{3,2,1,0:T(8,128)(2,1)S(1)} %get-tuple-element.36), channel_id=1, source_target_pairs={{0,24},{1,25},{2,26},{3,27},{4,28},{5,29},{6,30},{7,31},{8,16},{9,... | collective-permute-start | bytes 2752520 | tf_op jit(solution)/shard_map/ppermute | solution.py:34
  29.8 23.7 %collective-permute-start.4 = (bf16[1024,512]{1,0:T(8,128)(2,1)S(1)}, bf16[1024,512]{1,0:T(8,128)(2,1)S(1)}, u32[]{:S(2)}, u32[]{:S(2)}) collective-permute-start(bf16[1024,512]{1,0:T(8,128)(2,1)S(1)} %collective-permute-done.refs_1_), channel_id=1, source_target_pairs={{0,32},{32,0},{64,96},{96,64},{1,33},{33,1},{65,97},{97,65},{2,34}... | collective-permute-start | bytes 3145736 | tf_op jit(solution)/shard_map/ppermute | solution.py:38
  32.6 20.0 %collective-permute-start.6 = (bf16[4,112,512]{2,1,0:T(8,128)(2,1)S(1)}, bf16[4,112,512]{2,1,0:T(8,128)(2,1)S(1)}, u32[]{:S(2)}, u32[]{:S(2)}) collective-permute-start(bf16[4,112,512]{2,1,0:T(8,128)(2,1)S(1)} %forward.4.refs_2_), channel_id=1, source_target_pairs={{0,24},{1,25},{2,26},{3,27},{4,28},{5,29},{6,30},{7,31},{8,16},{9,... | collective-permute-start | bytes 1376264 | tf_op jit(solution)/shard_map/ppermute | solution.py:34
  42.5 10.1 %collective-permute-start.5 = (bf16[4,112,512]{2,1,0:T(8,128)(2,1)S(1)}, bf16[4,112,512]{2,1,0:T(8,128)(2,1)S(1)}, u32[]{:S(2)}, u32[]{:S(2)}) collective-permute-start(bf16[4,112,512]{2,1,0:T(8,128)(2,1)S(1)} %forward.5.refs_4_), channel_id=1, source_target_pairs={{0,8},{1,9},{2,10},{3,11},{4,12},{5,13},{6,14},{7,15},{8,0},{9,1},... | collective-permute-start | bytes 1376264 | tf_op jit(solution)/shard_map/ppermute | solution.py:34
  50.6 11.0 %copy-start.6 = (bf16[4,112,512]{2,1,0:T(8,128)(2,1)}, bf16[4,112,512]{2,1,0:T(8,128)(2,1)S(1)}, u32[]{:S(2)}) copy-start(bf16[4,112,512]{2,1,0:T(8,128)(2,1)S(1)} %get-tuple-element.38.refs_0_) | copy-start | bytes 1376260
  50.6 31.3 %collective-permute-start.7 = (bf16[2,4,112,512]{3,2,1,0:T(8,128)(2,1)}, bf16[2,4,112,512]{3,2,1,0:T(8,128)(2,1)S(1)}, u32[]{:S(2)}, u32[]{:S(2)}) collective-permute-start(bf16[2,4,112,512]{3,2,1,0:T(8,128)(2,1)} %get-tuple-element.44), channel_id=1, source_target_pairs={{0,8},{1,9},{2,10},{3,11},{4,12},{5,13},{6,14},{7,15},{8,0},{9,1},... | collective-permute-start | bytes 2752520 | tf_op jit(solution)/shard_map/ppermute | solution.py:34
  61.6 0.8 copy-start.8
  62.4 23.0 %collective-permute-start.8 = (bf16[2,4,112,512]{3,2,1,0:T(8,128)(2,1)}, bf16[2,4,112,512]{3,2,1,0:T(8,128)(2,1)S(1)}, u32[]{:S(2)}, u32[]{:S(2)}) collective-permute-start(bf16[2,4,112,512]{3,2,1,0:T(8,128)(2,1)} %get-tuple-element.45), channel_id=1, source_target_pairs={{0,24},{1,25},{2,26},{3,27},{4,28},{5,29},{6,30},{7,31},{8,16},{9,... | collective-permute-start | bytes 2752520 | tf_op jit(solution)/shard_map/ppermute | solution.py:34
  64.5 13.2 %collective-permute-start.10 = (bf16[112,1024]{1,0:T(8,128)(2,1)}, bf16[112,1024]{1,0:T(8,128)(2,1)S(1)}, u32[]{:S(2)}, u32[]{:S(2)}) collective-permute-start(bf16[112,1024]{1,0:T(8,128)(2,1)} %get-tuple-element.48), channel_id=1, source_target_pairs={{0,6},{1,7},{2,4},{3,5},{4,2},{5,3},{6,0},{7,1},{8,14},{9,15},{10,... | collective-permute-start | bytes 688136 | tf_op jit(solution)/shard_map/ppermute | solution.py:34
  68.5 9.2 %collective-permute-start.11 = (bf16[112,1024]{1,0:T(8,128)(2,1)}, bf16[112,1024]{1,0:T(8,128)(2,1)}, u32[]{:S(2)}, u32[]{:S(2)}) collective-permute-start(bf16[112,1024]{1,0:T(8,128)(2,1)} %get-tuple-element.49), channel_id=1, source_target_pairs={{0,4},{1,5},{2,6},{3,7},{4,0},{5,1},{6,2},{7,3},{8,12},{9,13},{10,... | collective-permute-start | bytes 688136 | tf_op jit(solution)/shard_map/ppermute | solution.py:34
  68.5 9.2 %collective-permute-start.9 = (bf16[112,1024]{1,0:T(8,128)(2,1)}, bf16[112,1024]{1,0:T(8,128)(2,1)}, u32[]{:S(2)}, u32[]{:S(2)}) collective-permute-start(bf16[112,1024]{1,0:T(8,128)(2,1)} %get-tuple-element.47), channel_id=1, source_target_pairs={{0,2},{1,3},{2,0},{3,1},{4,6},{5,7},{6,4},{7,5},{8,10},{9,11},{10,... | collective-permute-start | bytes 688136 | tf_op jit(solution)/shard_map/ppermute | solution.py:34
  69.4 29.1 %copy-start.7 = (bf16[4,112,512]{2,1,0:T(8,128)(2,1)S(1)}, bf16[4,112,512]{2,1,0:T(8,128)(2,1)}, u32[]{:S(2)}) copy-start(bf16[4,112,512]{2,1,0:T(8,128)(2,1)} %copy-done.6) | copy-start | bytes 1376260
  69.4 29.1 %copy-start.9 = (bf16[4,112,512]{2,1,0:T(8,128)(2,1)S(1)}, bf16[4,112,512]{2,1,0:T(8,128)(2,1)}, u32[]{:S(2)}) copy-start(bf16[4,112,512]{2,1,0:T(8,128)(2,1)} %copy-done.8) | copy-start | bytes 1376260
  78.9 6.4 %collective-permute-start.12 = (bf16[56,1024]{1,0:T(8,128)(2,1)S(1)}, bf16[56,1024]{1,0:T(8,128)(2,1)S(1)}, u32[]{:S(2)}, u32[]{:S(2)}) collective-permute-start(bf16[56,1024]{1,0:T(8,128)(2,1)S(1)} %get-tuple-element.51.refs_2_), channel_id=1, source_target_pairs={{0,1},{1,0},{2,3},{3,2},{4,5},{5,4},{6,7},{7,6},{8,9},{9,8},{10,11... | collective-permute-start | bytes 344072 | tf_op jit(solution)/shard_map/ppermute | solution.py:34
  82.0 15.8 %collective-permute-start.14 = (bf16[4,112,512]{2,1,0:T(8,128)(2,1)S(1)}, bf16[4,112,512]{2,1,0:T(8,128)(2,1)S(1)}, u32[]{:S(2)}, u32[]{:S(2)}) collective-permute-start(bf16[4,112,512]{2,1,0:T(8,128)(2,1)S(1)} %forward.6.refs_3_), channel_id=1, source_target_pairs={{0,24},{1,25},{2,26},{3,27},{4,28},{5,29},{6,30},{7,31},{8,16},{9,... | collective-permute-start | bytes 1376264 | tf_op jit(solution)/shard_map/ppermute | solution.py:34
  85.5 12.9 %collective-permute-start.13 = (bf16[4,112,512]{2,1,0:T(8,128)(2,1)S(1)}, bf16[4,112,512]{2,1,0:T(8,128)(2,1)S(1)}, u32[]{:S(2)}, u32[]{:S(2)}) collective-permute-start(bf16[4,112,512]{2,1,0:T(8,128)(2,1)S(1)} %forward.7.refs_2_), channel_id=1, source_target_pairs={{0,8},{1,9},{2,10},{3,11},{4,12},{5,13},{6,14},{7,15},{8,0},{9,1},... | collective-permute-start | bytes 1376264 | tf_op jit(solution)/shard_map/ppermute | solution.py:34
  85.6 6.4 %collective-permute-start.15 = (bf16[56,1024]{1,0:T(8,128)(2,1)S(1)}, bf16[56,1024]{1,0:T(8,128)(2,1)S(1)}, u32[]{:S(2)}, u32[]{:S(2)}) collective-permute-start(bf16[56,1024]{1,0:T(8,128)(2,1)S(1)} %get-tuple-element.52.refs_2_.refs_0_), channel_id=1, source_target_pairs={{0,1},{1,0},{2,3},{3,2},{4,5},{5,4},{6,7},{7,6},{8,9},{9,8},{10,11... | collective-permute-start | bytes 344072 | tf_op jit(solution)/shard_map/ppermute | solution.py:34
  92.0 11.8 %collective-permute-start.19 = (bf16[112,1024]{1,0:T(8,128)(2,1)S(1)}, bf16[112,1024]{1,0:T(8,128)(2,1)S(1)}, u32[]{:S(2)}, u32[]{:S(2)}) collective-permute-start(bf16[112,1024]{1,0:T(8,128)(2,1)S(1)} %pair.2.refs_6_.refs_0_), channel_id=1, source_target_pairs={{0,2},{1,3},{2,0},{3,1},{4,6},{5,7},{6,4},{7,5},{8,10},{9,11},{10,... | collective-permute-start | bytes 688136 | tf_op jit(solution)/shard_map/ppermute | solution.py:34
  92.1 13.0 %collective-permute-start.20 = (bf16[112,1024]{1,0:T(8,128)(2,1)S(1)}, bf16[112,1024]{1,0:T(8,128)(2,1)S(1)}, u32[]{:S(2)}, u32[]{:S(2)}) collective-permute-start(bf16[112,1024]{1,0:T(8,128)(2,1)S(1)} %pair.2.refs_6_.refs_0_), channel_id=1, source_target_pairs={{0,6},{1,7},{2,4},{3,5},{4,2},{5,3},{6,0},{7,1},{8,14},{9,15},{10,... | collective-permute-start | bytes 688136 | tf_op jit(solution)/shard_map/ppermute | solution.py:34
  96.4 8.7 %collective-permute-start.21 = (bf16[112,1024]{1,0:T(8,128)(2,1)S(1)}, bf16[112,1024]{1,0:T(8,128)(2,1)S(1)}, u32[]{:S(2)}, u32[]{:S(2)}) collective-permute-start(bf16[112,1024]{1,0:T(8,128)(2,1)S(1)} %pair.2.refs_6_.refs_0_), channel_id=1, source_target_pairs={{0,4},{1,5},{2,6},{3,7},{4,0},{5,1},{6,2},{7,3},{8,12},{9,13},{10,... | collective-permute-start | bytes 688136 | tf_op jit(solution)/shard_map/ppermute | solution.py:34
  98.8 9.4 %collective-permute-start.16 = (bf16[112,1024]{1,0:T(8,128)(2,1)S(1)}, bf16[112,1024]{1,0:T(8,128)(2,1)S(1)}, u32[]{:S(2)}, u32[]{:S(2)}) collective-permute-start(bf16[112,1024]{1,0:T(8,128)(2,1)S(1)} %get-tuple-element.54), channel_id=1, source_target_pairs={{0,2},{1,3},{2,0},{3,1},{4,6},{5,7},{6,4},{7,5},{8,10},{9,11},{10,... | collective-permute-start | bytes 688136 | tf_op jit(solution)/shard_map/ppermute | solution.py:34
  98.9 13.3 %collective-permute-start.17 = (bf16[112,1024]{1,0:T(8,128)(2,1)S(1)}, bf16[112,1024]{1,0:T(8,128)(2,1)S(1)}, u32[]{:S(2)}, u32[]{:S(2)}) collective-permute-start(bf16[112,1024]{1,0:T(8,128)(2,1)S(1)} %get-tuple-element.55), channel_id=1, source_target_pairs={{0,6},{1,7},{2,4},{3,5},{4,2},{5,3},{6,0},{7,1},{8,14},{9,15},{10,... | collective-permute-start | bytes 688136 | tf_op jit(solution)/shard_map/ppermute | solution.py:34
  103.8 11.3 %collective-permute-start.18 = (bf16[112,1024]{1,0:T(8,128)(2,1)S(1)}, bf16[112,1024]{1,0:T(8,128)(2,1)S(1)}, u32[]{:S(2)}, u32[]{:S(2)}) collective-permute-start(bf16[112,1024]{1,0:T(8,128)(2,1)S(1)} %get-tuple-element.56), channel_id=1, source_target_pairs={{0,4},{1,5},{2,6},{3,7},{4,0},{5,1},{6,2},{7,3},{8,12},{9,13},{10,... | collective-permute-start | bytes 688136 | tf_op jit(solution)/shard_map/ppermute | solution.py:34
  105.2 27.1 %collective-permute-start.33 = (bf16[4,112,512]{2,1,0:T(8,128)(2,1)S(1)}, bf16[4,112,512]{2,1,0:T(8,128)(2,1)S(1)}, u32[]{:S(2)}, u32[]{:S(2)}) collective-permute-start(bf16[4,112,512]{2,1,0:T(8,128)(2,1)S(1)} %get-tuple-element.57.refs_4_.refs_0_), channel_id=1, source_target_pairs={{0,8},{1,9},{2,10},{3,11},{4,12},{5,13},{6,14},{7,15},{8,0},{9,1},... | collective-permute-start | bytes 1376264 | tf_op jit(solution)/shard_map/ppermute | solution.py:34
  108.2 34.4 %collective-permute-start.35 = (bf16[4,112,512]{2,1,0:T(8,128)(2,1)S(1)}, bf16[4,112,512]{2,1,0:T(8,128)(2,1)S(1)}, u32[]{:S(2)}, u32[]{:S(2)}) collective-permute-start(bf16[4,112,512]{2,1,0:T(8,128)(2,1)S(1)} %get-tuple-element.63.refs_1_), channel_id=1, source_target_pairs={{0,24},{1,25},{2,26},{3,27},{4,28},{5,29},{6,30},{7,31},{8,16},{9,... | collective-permute-start | bytes 1376264 | tf_op jit(solution)/shard_map/ppermute | solution.py:34
  115.2 6.4 %collective-permute-start.22 = (bf16[56,1024]{1,0:T(8,128)(2,1)S(1)}, bf16[56,1024]{1,0:T(8,128)(2,1)S(1)}, u32[]{:S(2)}, u32[]{:S(2)}) collective-permute-start(bf16[56,1024]{1,0:T(8,128)(2,1)S(1)} %get-tuple-element.59.refs_3_), channel_id=1, source_target_pairs={{0,1},{1,0},{2,3},{3,2},{4,5},{5,4},{6,7},{7,6},{8,9},{9,8},{10,11... | collective-permute-start | bytes 344072 | tf_op jit(solution)/shard_map/ppermute | solution.py:34
  121.8 6.4 %collective-permute-start.23 = (bf16[56,1024]{1,0:T(8,128)(2,1)S(1)}, bf16[56,1024]{1,0:T(8,128)(2,1)S(1)}, u32[]{:S(2)}, u32[]{:S(2)}) collective-permute-start(bf16[56,1024]{1,0:T(8,128)(2,1)S(1)} %get-tuple-element.60.refs_0_.refs_2_), channel_id=1, source_target_pairs={{0,1},{1,0},{2,3},{3,2},{4,5},{5,4},{6,7},{7,6},{8,9},{9,8},{10,11... | collective-permute-start | bytes 344072 | tf_op jit(solution)/shard_map/ppermute | solution.py:34
  128.2 8.6 %collective-permute-start.24 = (bf16[112,1024]{1,0:T(8,128)(2,1)S(1)}, bf16[112,1024]{1,0:T(8,128)(2,1)S(1)}, u32[]{:S(2)}, u32[]{:S(2)}) collective-permute-start(bf16[112,1024]{1,0:T(8,128)(2,1)S(1)} %pair.3.refs_0_.refs_4_), channel_id=1, source_target_pairs={{0,2},{1,3},{2,0},{3,1},{4,6},{5,7},{6,4},{7,5},{8,10},{9,11},{10,... | collective-permute-start | bytes 688136 | tf_op jit(solution)/shard_map/ppermute | solution.py:34
  128.4 10.8 %collective-permute-start.25 = (bf16[112,1024]{1,0:T(8,128)(2,1)S(1)}, bf16[112,1024]{1,0:T(8,128)(2,1)S(1)}, u32[]{:S(2)}, u32[]{:S(2)}) collective-permute-start(bf16[112,1024]{1,0:T(8,128)(2,1)S(1)} %pair.3.refs_0_.refs_4_), channel_id=1, source_target_pairs={{0,6},{1,7},{2,4},{3,5},{4,2},{5,3},{6,0},{7,1},{8,14},{9,15},{10,... | collective-permute-start | bytes 688136 | tf_op jit(solution)/shard_map/ppermute | solution.py:34
  129.9 12.2 %collective-permute-start.26 = (bf16[112,1024]{1,0:T(8,128)(2,1)S(1)}, bf16[112,1024]{1,0:T(8,128)(2,1)S(1)}, u32[]{:S(2)}, u32[]{:S(2)}) collective-permute-start(bf16[112,1024]{1,0:T(8,128)(2,1)S(1)} %pair.3.refs_0_.refs_4_), channel_id=1, source_target_pairs={{0,4},{1,5},{2,6},{3,7},{4,0},{5,1},{6,2},{7,3},{8,12},{9,13},{10,... | collective-permute-start | bytes 688136 | tf_op jit(solution)/shard_map/ppermute | solution.py:34
  132.4 12.0 %collective-permute-start.37 = (bf16[4,112,512]{2,1,0:T(8,128)(2,1)S(1)}, bf16[4,112,512]{2,1,0:T(8,128)(2,1)S(1)}, u32[]{:S(2)}, u32[]{:S(2)}) collective-permute-start(bf16[4,112,512]{2,1,0:T(8,128)(2,1)S(1)} %get-tuple-element.63.refs_1_), channel_id=1, source_target_pairs={{0,8},{1,9},{2,10},{3,11},{4,12},{5,13},{6,14},{7,15},{8,0},{9,1},... | collective-permute-start | bytes 1376264 | tf_op jit(solution)/shard_map/ppermute | solution.py:34
  136.8 9.7 %collective-permute-start.38 = (bf16[4,112,512]{2,1,0:T(8,128)(2,1)S(1)}, bf16[4,112,512]{2,1,0:T(8,128)(2,1)S(1)}, u32[]{:S(2)}, u32[]{:S(2)}) collective-permute-start(bf16[4,112,512]{2,1,0:T(8,128)(2,1)S(1)} %get-tuple-element.57.refs_4_.refs_0_), channel_id=1, source_target_pairs={{0,24},{1,25},{2,26},{3,27},{4,28},{5,29},{6,30},{7,31},{8,16},{9,... | collective-permute-start | bytes 1376264 | tf_op jit(solution)/shard_map/ppermute | solution.py:34
  139.1 12.3 %collective-permute-start.34 = (bf16[4,112,512]{2,1,0:T(8,128)(2,1)S(1)}, bf16[4,112,512]{2,1,0:T(8,128)(2,1)S(1)}, u32[]{:S(2)}, u32[]{:S(2)}) collective-permute-start(bf16[4,112,512]{2,1,0:T(8,128)(2,1)S(1)} %collective-permute-done.33.refs_2_), channel_id=1, source_target_pairs={{0,24},{1,25},{2,26},{3,27},{4,28},{5,29},{6,30},{7,31},{8,16},{9,... | collective-permute-start | bytes 1376264 | tf_op jit(solution)/shard_map/ppermute | solution.py:34
  142.1 9.6 %collective-permute-start.27 = (bf16[4,112,512]{2,1,0:T(8,128)(2,1)S(1)}, bf16[4,112,512]{2,1,0:T(8,128)(2,1)S(1)}, u32[]{:S(2)}, u32[]{:S(2)}) collective-permute-start(bf16[4,112,512]{2,1,0:T(8,128)(2,1)S(1)} %get-tuple-element.61.refs_0_), channel_id=1, source_target_pairs={{0,8},{1,9},{2,10},{3,11},{4,12},{5,13},{6,14},{7,15},{8,0},{9,1},... | collective-permute-start | bytes 1376264 | tf_op jit(solution)/shard_map/ppermute | solution.py:34
  142.5 13.8 %collective-permute-start.29 = (bf16[4,112,512]{2,1,0:T(8,128)(2,1)S(1)}, bf16[4,112,512]{2,1,0:T(8,128)(2,1)S(1)}, u32[]{:S(2)}, u32[]{:S(2)}) collective-permute-start(bf16[4,112,512]{2,1,0:T(8,128)(2,1)S(1)} %get-tuple-element.62.refs_1_), channel_id=1, source_target_pairs={{0,24},{1,25},{2,26},{3,27},{4,28},{5,29},{6,30},{7,31},{8,16},{9,... | collective-permute-start | bytes 1376264 | tf_op jit(solution)/shard_map/ppermute | solution.py:34
  144.3 13.9 %collective-permute-start.36 = (bf16[4,112,512]{2,1,0:T(8,128)(2,1)S(1)}, bf16[4,112,512]{2,1,0:T(8,128)(2,1)S(1)}, u32[]{:S(2)}, u32[]{:S(2)}) collective-permute-start(bf16[4,112,512]{2,1,0:T(8,128)(2,1)S(1)} %collective-permute-done.35.refs_5_), channel_id=1, source_target_pairs={{0,8},{1,9},{2,10},{3,11},{4,12},{5,13},{6,14},{7,15},{8,0},{9,1},... | collective-permute-start | bytes 1376264 | tf_op jit(solution)/shard_map/ppermute | solution.py:34
  146.5 14.0 %collective-permute-start.31 = (bf16[4,112,512]{2,1,0:T(8,128)(2,1)S(1)}, bf16[4,112,512]{2,1,0:T(8,128)(2,1)S(1)}, u32[]{:S(2)}, u32[]{:S(2)}) collective-permute-start(bf16[4,112,512]{2,1,0:T(8,128)(2,1)S(1)} %get-tuple-element.62.refs_1_), channel_id=1, source_target_pairs={{0,8},{1,9},{2,10},{3,11},{4,12},{5,13},{6,14},{7,15},{8,0},{9,1},... | collective-permute-start | bytes 1376264 | tf_op jit(solution)/shard_map/ppermute | solution.py:34
  151.4 9.8 %collective-permute-start.32 = (bf16[4,112,512]{2,1,0:T(8,128)(2,1)S(1)}, bf16[4,112,512]{2,1,0:T(8,128)(2,1)S(1)}, u32[]{:S(2)}, u32[]{:S(2)}) collective-permute-start(bf16[4,112,512]{2,1,0:T(8,128)(2,1)S(1)} %get-tuple-element.61.refs_0_), channel_id=1, source_target_pairs={{0,24},{1,25},{2,26},{3,27},{4,28},{5,29},{6,30},{7,31},{8,16},{9,... | collective-permute-start | bytes 1376264 | tf_op jit(solution)/shard_map/ppermute | solution.py:34
  151.7 14.5 %collective-permute-start.28 = (bf16[4,112,512]{2,1,0:T(8,128)(2,1)S(1)}, bf16[4,112,512]{2,1,0:T(8,128)(2,1)S(1)}, u32[]{:S(2)}, u32[]{:S(2)}) collective-permute-start(bf16[4,112,512]{2,1,0:T(8,128)(2,1)S(1)} %collective-permute-done.27.refs_2_), channel_id=1, source_target_pairs={{0,24},{1,25},{2,26},{3,27},{4,28},{5,29},{6,30},{7,31},{8,16},{9,... | collective-permute-start | bytes 1376264 | tf_op jit(solution)/shard_map/ppermute | solution.py:34
  156.3 9.8 %collective-permute-start.30 = (bf16[4,112,512]{2,1,0:T(8,128)(2,1)S(1)}, bf16[4,112,512]{2,1,0:T(8,128)(2,1)S(1)}, u32[]{:S(2)}, u32[]{:S(2)}) collective-permute-start(bf16[4,112,512]{2,1,0:T(8,128)(2,1)S(1)} %collective-permute-done.29.refs_5_), channel_id=1, source_target_pairs={{0,8},{1,9},{2,10},{3,11},{4,12},{5,13},{6,14},{7,15},{8,0},{9,1},... | collective-permute-start | bytes 1376264 | tf_op jit(solution)/shard_map/ppermute | solution.py:34
  156.4 2.9 %copy-start.10 = (f32[56,2048]{1,0:T(8,128)}, f32[56,2048]{1,0:T(8,128)S(1)}, u32[]{:S(2)}) copy-start(f32[56,2048]{1,0:T(8,128)S(1)} %slice_dynamic-update-slice_fusion) | copy-start | bytes 1376260

commit v2 on v1

v2 whole, which is shorter than its diff:
```python
import jax
import jax.numpy as jnp
from jax import lax
from jax.experimental import pallas as pl
from jax.experimental.pallas import tpu as pltpu
from jax.sharding import PartitionSpec as P

CLIP = 1.5
BLOCK = 128
WAYS = 4
GRAY = (0, 1, 3, 2)
TILE = 448
GROUP = 64
LOCAL_MIB = 40
MIB = 1024 * 1024
F32 = jnp.float32
BF16 = jnp.bfloat16
AXES = ("tp", "dp")
COST_BYTES = 40000000
LOCAL_BYTES = 1000000


def permute(array, phase, mask):
    pairs = []
    for tp in range(4):
        for x in range(4):
            for z in range(4):
                for half in range(2):
                    to_x, to_z, to_half = x, z, half
                    if phase == 2:
                        to_half = 1 - half
                    elif (tp + phase) % 2 == 0:
                        to_x = GRAY[GRAY[x] ^ mask]
                    else:
                        to_z = GRAY[GRAY[z] ^ mask]
                    pairs.append((tp * 32 + x * 8 + z * 2 + half, tp * 32 + to_x * 8 + to_z * 2 + to_half))
    return lax.ppermute(array, AXES, pairs)


def swap_tp(array, mask):
    return lax.ppermute(array, "tp", [(i, i ^ mask) for i in range(4)])


def clipped(part):
    square = jnp.sum(part * part, axis=1, keepdims=True) * (CLIP * CLIP / BLOCK) + CLIP * CLIP * 1e-06
    bound = square * lax.rsqrt(square)
    return jnp.clip(part, -bound, bound)


def coordinates():
    tp, dp = lax.axis_index("tp"), lax.axis_index("dp")
    return tp, dp // 8, (dp // 2) % 4, dp % 2


def ring_rows(first, second):
    tp, x, z, _ = coordinates()
    core = tp % 2
    on_x = first + core * (second - first)
    on_z = second + core * (first - second)
    code_x = x ^ (x >> 1) ^ on_x
    code_z = z ^ (z >> 1) ^ on_z
    return pl.multiple_of((code_x ^ (code_x >> 1)) * 448 + (code_z ^ (code_z >> 1)) * 112, 16)


def local_kernel(chunk, sides, tile, *refs):
    count = len(sides)
    acts, momentum, resid = refs[:3]
    cotans = refs[3 : 3 + count]
    values, moments, resids, *grads, sems = refs[-6:]
    outs = refs[-6 - 3 * count : -6]
    turned = refs[-7 - 3 * count]
    rows, width = values.shape
    turn = acts.shape[0] == cotans[0].shape[0]
    steps = rows // tile
    running = []
    for index, side in enumerate(sides):
        column = pl.ds(pl.multiple_of((coordinates()[0] ^ (2 * chunk + side)) * width, width), width)
        for step in range(steps):
            at = pl.ds(step * tile, tile)
            copies = [
                pltpu.make_async_copy(momentum.at[at, column], moments.at[index, at], sems.at[index, 0, step]),
                pltpu.make_async_copy(resid.at[at, column], resids.at[index, at], sems.at[index, 1, step]),
            ]
            running.append(copies)
            for copy in copies:
                copy.start()

    def compress(index, step):
        for copy in running[index * steps + step]:
            copy.wait()
        grad = grads[step % 2]
        for low in range(0, tile, GROUP):
            at = slice(step * tile + low, step * tile + min(low + GROUP, tile))
            for start in range(0, width, BLOCK):
                lanes = slice(start, start + BLOCK)
                total = 0.9 * moments[index, at, lanes].astype(F32) + resids[index, at, lanes].astype(F32)
                total = total + 0.1 * grad[at.start - step * tile : at.stop - step * tile, lanes]
                values[at, lanes] = clipped(total).astype(BF16)

    for index, side in enumerate(sides):
        for step in range(steps):
            at = slice(step * tile, step * tile + tile)
            if turn:
                turned[at, :] = acts[:, at].T
                block = turned[at, :]
            else:
                block = acts[at, :]
            grads[step % 2][...] = jnp.dot(block, cotans[index][...], preferred_element_type=F32)
            if step:
                compress(index, step - 1)
        compress(index, steps - 1)

        send, keep, cross = outs[3 * index : 3 * index + 3]
        for second in range(WAYS):
            for first in range(WAYS):
                to = {0: keep, 1 + side: send.at[0], 2 - side: cross, 3: send.at[1]}[first]
                to[second] = values[pl.ds(ring_rows(first, second), 112), :]


def local_values(chunk, sides, acts, cotans, momentum, resid, after):
    depth, width = cotans[0].shape
    turn = acts.shape[0] == depth
    rows, count = momentum.shape[0], len(sides)
    tile = 256 if turn else TILE
    hbm, vmem = pl.BlockSpec(memory_space=pltpu.HBM), pl.BlockSpec(memory_space=pltpu.VMEM)
    part = shape(BF16, WAYS, 112, width)
    return pl.pallas_call(
        lambda *refs: local_kernel(chunk, sides, tile, *refs),
        in_specs=[vmem, hbm, hbm] + [vmem] * count + [pl.BlockSpec(memory_space=pl.ANY)] * len(after),
        out_specs=[vmem] * (3 * count + turn),
        out_shape=[shape(BF16, rows, depth)] * turn + [shape(BF16, 2, WAYS, 112, width), part, part] * count,
        scratch_shapes=[pltpu.VMEM((rows, width), BF16)]
        + [pltpu.VMEM((count, rows, width), BF16)] * 2
        + [pltpu.VMEM((tile, width), F32)] * 2
        + [pltpu.SemaphoreType.DMA((count, 2, rows // tile))],
        compiler_params=pltpu.CompilerParams(vmem_limit_bytes=LOCAL_MIB * MIB),
        cost_estimate=pl.CostEstimate(flops=0, bytes_accessed=LOCAL_BYTES, transcendentals=0),
        name="local_values",
    )(acts, momentum, resid, *cotans, *after)


def add(*terms):
    total = terms[0].astype(F32)
    for term in terms[1:]:
        total = total + term.astype(F32)
    return total


def small_call(kernel, name, out_shape, *args, after=()):
    count = len(args)
    return pl.pallas_call(
        lambda *refs: kernel(*refs[:count], *refs[count + len(after) :]),
        in_specs=[pl.BlockSpec(memory_space=pltpu.VMEM)] * count + [pl.BlockSpec(memory_space=pl.ANY)] * len(after),
        out_specs=[pl.BlockSpec(memory_space=pltpu.VMEM)] * len(out_shape),
        out_shape=out_shape,
        compiler_params=pltpu.CompilerParams(vmem_limit_bytes=4 * MIB),
        cost_estimate=pl.CostEstimate(flops=0, bytes_accessed=COST_BYTES, transcendentals=0),
        name=name,
    )(*args, *after)


def shape(dtype, *dims):
    return jax.ShapeDtypeStruct(dims, dtype)


def forward_kernel(*refs):
    count = len(refs) // 3
    for cross, got, out in zip(refs[:count], refs[count : 2 * count], refs[2 * count :]):
        out[...] = add(cross[...], got[1]).astype(BF16)


def ring_sum_kernel(keep0, keep1, r0, r1, u0, u1, *outs):
    width = keep0.shape[-1]
    for second, out in enumerate(outs):
        out[:, :width] = add(keep0[second], r0[0, second], u1[second]).astype(out.dtype)
        out[:, width:] = add(keep1[second], r1[0, second], u0[second]).astype(out.dtype)


def split_kernel(z0, w1, w2, w3, keep, send):
    total = add(z0[...], w1[...], w2[...], w3[...])
    low, high = total[:56], total[56:]
    is_low = coordinates()[3] == 0
    keep[...] = jnp.where(is_low, low, high)
    send[...] = jnp.where(is_low, high, low).astype(BF16)


def owner_kernel(chunk, keep, got, server, *refs):
    corrected, update = refs[-2:]
    half = keep.shape[1] // 2
    for side in (0, 1):
        column = pl.ds(pl.multiple_of((coordinates()[0] ^ (2 * chunk + side)) * half, half), half)
        lanes = slice(side * half, side * half + half)
        value = add(keep[:, lanes], got[:, lanes]) * (1.0 / 32) + server[:, column]
        corrected[:, column if chunk else lanes] = value
        if chunk:
            earlier = pl.ds(pl.multiple_of((coordinates()[0] ^ side) * half, half), half)
            corrected[:, earlier] = refs[0][:, lanes]
        for start in range(0, half, BLOCK):
            run = slice(side * half + start, side * half + start + BLOCK)
            update[:, run] = clipped(value[:, start : start + BLOCK]).astype(BF16)


def pair_kernel(own, other, out):
    is_low = coordinates()[3] == 0
    out[:56] = jnp.where(is_low, own[...], other[...])
    out[56:] = jnp.where(is_low, other[...], own[...])


def halves_kernel(got0, got1, out0, out1):
    width = out0.shape[-1]
    out0[...] = got0[:, :, :width]
    out1[...] = got1[:, :, width:]


def copy_kernel(source, out):
    out[...] = source[...]


def whole_stack_kernel(*refs):
    for index, piece in enumerate(refs[:-1]):
        refs[-1][index] = piece[...]


def stack_kernel(a, b, c, d, out0, out1):
    width = out0.shape[-1]
    for index, piece in enumerate((a, b, c, d)):
        out0[index] = piece[:, :width]
        out1[index] = piece[:, width:]


def place_kernel(pieces, *refs):
    out, sems = refs[-2:]
    tp = coordinates()[0]
    running = []
    for source, (first, chunk, sides) in zip(refs, pieces):
        width = source.shape[-1] // len(sides)
        for index, side in enumerate(sides):
            columns = pl.ds(pl.multiple_of((tp ^ (2 * chunk + side)) * width, width), width)
            for second in range(WAYS):
                rows = pl.ds(ring_rows(first, second), 112)
                piece = source.at[second, :, pl.ds(index * width, width)]
                copy = pltpu.make_async_copy(piece, out.at[rows, columns], sems.at[len(running)])
                copy.start()
                running.append(copy)
    for copy in running:
        copy.wait()


def place(pieces, arrays, rows, columns, so_far):
    chained = so_far is not None
    any_space = pl.BlockSpec(memory_space=pl.ANY)
    return pl.pallas_call(
        lambda *refs: place_kernel(pieces, *refs),
        in_specs=[pl.BlockSpec(memory_space=pltpu.VMEM)] * len(arrays) + [any_space] * chained,
        out_specs=any_space,
        out_shape=shape(BF16, rows, columns),
        scratch_shapes=[pltpu.SemaphoreType.DMA((WAYS * sum(len(p[2]) for p in pieces),))],
        input_output_aliases={len(arrays): 0} if chained else {},
        compiler_params=pltpu.CompilerParams(vmem_limit_bytes=4 * MIB),
        cost_estimate=pl.CostEstimate(flops=0, bytes_accessed=COST_BYTES, transcendentals=0),
        name="place_update",
    )(*arrays, *((so_far,) if chained else ()))


class Chunk:
    def __init__(self, index, data, cotans, gather):
        self.index, self.data, self.cotans, self.gather = index, data, cotans, gather
        self.rows, self.half = data[1].shape[0], cotans[0].shape[1]
        self.width = 2 * self.half
        self.part = shape(BF16, WAYS, 112, self.half)
        self.held = {}

    def local(self, sides, after):
        acts, momentum, resid, _ = self.data
        outs = local_values(self.index, sides, acts, [self.cotans[s] for s in sides], momentum, resid, after)
        if len(outs) == 3 * len(sides) + 1:
            self.data[0], *outs = outs
        for index, side in enumerate(sides):
            send, keep, cross = outs[3 * index : 3 * index + 3]
            self.held[side] = (permute(send, 0, 1 + side), keep, cross)
        return outs[-1]

    def forward(self, sides, after):
        held = [self.held[side] for side in sides]
        args = [cross for _, _, cross in held] + [got for got, _, _ in held]
        outs = small_call(forward_kernel, "forward", [self.part] * len(sides), *args, after=after)
        for side, out in zip(sides, outs):
            self.held[side] += (permute(out, 0, 2 - side),)
        return outs[0]

    def ring_sum(self, after):
        (r0, keep0, _, u1), (r1, keep1, _, u0) = self.held[0], self.held[1]
        wide = [shape(t, 112, self.width) for t in (F32, BF16, BF16, BF16)]
        outs = small_call(ring_sum_kernel, "ring_sum", wide, keep0, keep1, r0, r1, u0, u1, after=after)
        self.sums = [outs[0]] + [permute(outs[mask], 1, mask) for mask in (1, 2, 3)]
        return outs[0]

    def split(self, after):
        out_shape = [shape(F32, 56, self.width), shape(BF16, 56, self.width)]
        self.kept, send = small_call(split_kernel, "split", out_shape, *self.sums, after=after)
        self.got = permute(send, 2, 0)
        return send

    def owner(self, after, earlier=()):
        server_err = self.data[3]
        out_shape = [shape(F32, 56, server_err.shape[1] if earlier else self.width), shape(BF16, 56, self.width)]
        args = (self.kept, self.got, server_err, *earlier)
        kernel = lambda *refs: owner_kernel(self.index, *refs)
        self.value, self.mine = small_call(kernel, "owner", out_shape, *args, after=after)
        self.other = permute(self.mine, 2, 0)
        return self.mine

    def pair(self, after):
        out_shape = [shape(BF16, 112, self.width)]
        (out,) = small_call(pair_kernel, "pair", out_shape, self.mine, self.other, after=after)
        self.ring = [out] + [permute(out, 1, mask) for mask in (1, 2, 3)]
        return out

    def stack(self, after):
        if self.gather == "sides":
            own0, own1 = small_call(stack_kernel, "stack", [self.part, self.part], *self.ring, after=after)
            a0, b1 = permute(own0, 0, 1), permute(own1, 0, 2)
            b0, a1 = permute(own0, 0, 2), permute(own1, 0, 1)
            self.final = [[(0, own0, (0,)), (0, own1, (1,)), (1, a0, (0,)), (1, a1, (1,)), (2, b0, (0,)), (2, b1, (1,))]]
            self.final += [[(3, permute(a0, 0, 2), (0,)), (3, permute(b1, 0, 1), (1,))]]
            return own0
        whole = shape(BF16, WAYS, 112, self.width)
        (own,) = small_call(whole_stack_kernel, "stack", [whole], *self.ring, after=after)
        self.final = [[(0, own, (0, 1)), (1, permute(own, 0, 1), (0, 1)), (2, permute(own, 0, 2), (0, 1))]]
        if self.gather == "direct":
            self.final += [[(3, permute(own, 0, 3), (0, 1))]]
        return own

    def halves(self, after):
        a, b = self.final[0][1][1], self.final[0][2][1]
        left, right = small_call(halves_kernel, "halves", [self.part, self.part], a, b, after=after)
        self.final += [[(3, permute(left, 0, 2), (0,)), (3, permute(right, 0, 1), (1,))]]
        return left

    def place(self, update):
        for group in self.final:
            pieces = [(first, self.index, sides) for first, _, sides in group]
            update = place(pieces, [array for _, array, _ in group], self.rows, 2 * self.width, update)
        return update


GATHERS = ("sides", "sides")
ORDER = (
    "La0", "La1", "Fa0", "G", "Lb0", "Lb1", "Fb0", "Fa1", "Fb1", "Sa",
    "Sb", "Pa", "Pb", "Oa", "Ob", "Qa", "Qb", "Ka", "Kb",
)


def body(hidden, grad_out, momentum, worker_err, server_err):
    far = swap_tp(grad_out, 2)
    near = swap_tp(grad_out, 1)
    data = [hidden, momentum, worker_err[0], server_err]
    chunks = {"a": Chunk(0, data, (grad_out, near), GATHERS[0])}
    last = ()
    for word in ORDER:
        if word == "G":
            (far,) = small_call(copy_kernel, "take_far", [shape(BF16, *far.shape)], far, after=last)
            chunks["b"] = Chunk(1, data, (far, swap_tp(far, 1)), GATHERS[1])
            last = (far,)
            continue
        chunk, sides = chunks[word[1]], tuple(int(c) for c in word[2:])
        if word[0] == "L":
            out = chunk.local(sides, last)
        elif word[0] == "F":
            out = chunk.forward(sides, last)
        elif word[0] == "O":
            out = chunk.owner(last, (chunks["a"].value,) if word[1] == "b" else ())
        else:
            steps = {"S": chunk.ring_sum, "P": chunk.split, "Q": chunk.pair, "K": chunk.stack, "H": chunk.halves}
            out = steps[word[0]](last)
        last = (out,)
    update = chunks["b"].place(chunks["a"].place(None))
    return (update, chunks["b"].value)


def solution(mesh):
    placed = (
        P("dp", "tp"),
        P("dp", "tp"),
        P("tp", None),
        P("dp", "tp", None),
        P(("tp", "dp"), None),
    )
    return jax.shard_map(
        body,
        mesh=mesh,
        in_specs=placed,
        out_specs=(P("tp", None), P(("tp", "dp"), None)),
        check_vma=False,
    )
```

time: 168 us -> 147 us (0.88)
  Pallas kernels: 39.2 us -> 23.8 us
  local copies, waits for them, and re-layouts: 11.5 us -> 3.27 us
  waiting for transfers between devices: 57.3 us -> 64.6 us
  starting transfers between devices: 58.1 us -> 54 us
    pallas_call x4, Pallas kernels: 30.1 us -> 15.9 us  [local_values(): pl.pallas_call(lambda *refs: local_kernel(chunk, sides, tile, *refs), in_...]
    unnamed x22 -> x8, local copies, waits for them, and re-layouts: 10.3 us -> 3.27 us
    ppermute x36, waiting for transfers between devices: 57.3 us -> 61.8 us  [permute(): return lax.ppermute(array, AXES, pairs)]
    ppermute x36, starting transfers between devices: 55.8 us -> 52.1 us  [permute(): return lax.ppermute(array, AXES, pairs)]
    ppermute x3, waiting for transfers between devices: 0.01 us -> 2.81 us  [swap_tp(): return lax.ppermute(array, 'tp', [(i, i ^ mask) for i in range(4)])]
    pallas_call x14 -> x15, Pallas kernels: 3.53 us -> 2.56 us  [small_call(): pl.pallas_call(lambda *refs: kernel(*refs[:count], *refs[count + len(afte...]
  transfers between devices with their start and end apart: 39 -> 39, of which waited for: 19 -> 21; matrix products, arithmetic and copies ran while one was open for 1% -> 0% of each run, Pallas kernels for 23% -> 15%
where the time goes in v2:
time: 147 us
  waiting for transfers between devices  64.6 us (44%)
  starting transfers between devices  54 us (37%)
  Pallas kernels  23.8 us (16%)
  local copies, waits for them, and re-layouts  3.27 us (2%)
    ppermute x36, waiting for transfers between devices, permute(): return lax.ppermute(array, AXES, pairs)  61.8 us
    ppermute x36, starting transfers between devices, permute(): return lax.ppermute(array, AXES, pairs)  52.1 us
    pallas_call x4, Pallas kernels, local_values(): pl.pallas_call(lambda *refs: local_kernel(chunk, sides, tile, *refs), in_...  15.9 us
    pallas_call x4, Pallas kernels, place(): pl.pallas_call(lambda *refs: place_kernel(pieces, *refs), in_specs=[pl.Bl...  5.39 us
    unnamed x8, local copies, waits for them, and re-layouts  3.27 us
  transfers between devices with their start and end apart: 39, of which 21 were waited for; matrix products, arithmetic and copies ran while one was open for 0% of the time, Pallas kernels for 15%

profile of v2, /device:TPU:0, one launch (start us, length us, event | category | flops | bytes accessed | tf_op | source)
XLA Modules:
  0.0 146.8 jit_solution(9777615442521108496)
XLA Ops:
  0.7 1.7 %collective-permute-start = (bf16[1024,512]{1,0:T(8,128)(2,1)}, bf16[1024,512]{1,0:T(8,128)(2,1)S(1)}, u32[]{:S(2)}, u32[]{:S(2)}) collective-permute-start(bf16[1024,512]{1,0:T(8,128)(2,1)} %refs_3_.1), channel_id=1, source_target_pairs={{0,64},{32,96},{64,0},{96,32},{1,65},{33,97},{65,1},{97,33},{2,66}... | collective-permute-start | bytes 3145736 | tf_op jit(solution)/shard_map/ppermute | solution.py:41
  2.5 2.0 %copy-done.1 = bf16[1024,1792]{1,0:T(8,128)(2,1)S(1)} copy-done((bf16[1024,1792]{1,0:T(8,128)(2,1)S(1)}, bf16[1024,1792]{1,0:T(8,128)(2,1)}, u32[]{:S(2)}) %copy-start.1) | copy-done | bytes 3670040
  4.5 1.2 copy-done.3
  5.7 4.4 %local_values.4 = (bf16[1792,1024]{1,0:T(8,128)(2,1)S(1)}, bf16[2,4,112,512]{3,2,1,0:T(8,128)(2,1)S(1)}, bf16[4,112,512]{2,1,0:T(8,128)(2,1)S(1)}, bf16[4,112,512]{2,1,0:T(8,128)(2,1)S(1)}) custom-call(bf16[1024,1792]{1,0:T(8,128)(2,1)S(1)} %copy-done.1, bf16[1792,2048]{1,0:T(8,128)(2,1)} %refs_1_.7, bf16[1792,2048]{1,0:T(8,128)(2,1)} %bitcast.1, ...), custom_call_target="tpu_custom_call" | custom-call | bytes 1000000 | tf_op jit(solution)/shard_map/local_values/pallas_call | solution.py:127
  10.1 1.6 %collective-permute-start.1 = (bf16[2,4,112,512]{3,2,1,0:T(8,128)(2,1)S(1)}, bf16[2,4,112,512]{3,2,1,0:T(8,128)(2,1)S(1)}, u32[]{:S(2)}, u32[]{:S(2)}) collective-permute-start(bf16[2,4,112,512]{3,2,1,0:T(8,128)(2,1)S(1)} %get-tuple-element.37), channel_id=1, source_target_pairs={{0,8},{1,9},{2,10},{3,11},{4,12},{5,13},{6,14},{7,15},{8,0},{9,1},... | collective-permute-start | bytes 2752520 | tf_op jit(solution)/shard_map/ppermute | solution.py:37
  11.7 3.8 %local_values.5 = (bf16[2,4,112,512]{3,2,1,0:T(8,128)(2,1)S(1)}, bf16[4,112,512]{2,1,0:T(8,128)(2,1)S(1)}, bf16[4,112,512]{2,1,0:T(8,128)(2,1)S(1)}) custom-call(bf16[1792,1024]{1,0:T(8,128)(2,1)S(1)} %get-tuple-element.35.refs_0_, bf16[1792,2048]{1,0:T(8,128)(2,1)S(1)} %copy-done, bf16[1792,2048]{1,0:T(8,128)(2,1)} %bitcast.2, ...), custom_call_target="tpu_custom_call" | custom-call | bytes 1000000 | tf_op jit(solution)/shard_map/local_values/pallas_call | solution.py:127
  15.5 8.1 %collective-permute-done.1.refs_1_.refs_2_ = bf16[2,4,112,512]{3,2,1,0:T(8,128)(2,1)S(1)} collective-permute-done((bf16[2,4,112,512]{3,2,1,0:T(8,128)(2,1)S(1)}, bf16[2,4,112,512]{3,2,1,0:T(8,128)(2,1)S(1)}, u32[]{:S(2)}, u32[]{:S(2)}) %collective-permute-start.1) | collective-permute-done | bytes 917536 | tf_op jit(solution)/shard_map/ppermute | solution.py:37
  23.7 2.8 %collective-permute-done.refs_0_ = bf16[1024,512]{1,0:T(8,128)(2,1)S(1)} collective-permute-done((bf16[1024,512]{1,0:T(8,128)(2,1)}, bf16[1024,512]{1,0:T(8,128)(2,1)S(1)}, u32[]{:S(2)}, u32[]{:S(2)}) %collective-permute-start) | collective-permute-done | bytes 1048608 | tf_op jit(solution)/shard_map/ppermute | solution.py:41
  26.7 3.8 %local_values.6 = (bf16[2,4,112,512]{3,2,1,0:T(8,128)(2,1)S(1)}, bf16[4,112,512]{2,1,0:T(8,128)(2,1)S(1)}, bf16[4,112,512]{2,1,0:T(8,128)(2,1)S(1)}) custom-call(bf16[1792,1024]{1,0:T(8,128)(2,1)S(1)} %get-tuple-element.35.refs_0_, bf16[1792,2048]{1,0:T(8,128)(2,1)S(1)} %copy-done, bf16[1792,2048]{1,0:T(8,128)(2,1)} %bitcast.3, ...), custom_call_target="tpu_custom_call" | custom-call | bytes 1000000 | tf_op jit(solution)/shard_map/local_values/pallas_call | solution.py:127
  30.5 1.7 %collective-permute-start.4 = (bf16[2,4,112,512]{3,2,1,0:T(8,128)(2,1)S(1)}, bf16[2,4,112,512]{3,2,1,0:T(8,128)(2,1)S(1)}, u32[]{:S(2)}, u32[]{:S(2)}) collective-permute-start(bf16[2,4,112,512]{3,2,1,0:T(8,128)(2,1)S(1)} %get-tuple-element.42), channel_id=1, source_target_pairs={{0,8},{1,9},{2,10},{3,11},{4,12},{5,13},{6,14},{7,15},{8,0},{9,1},... | collective-permute-start | bytes 2752520 | tf_op jit(solution)/shard_map/ppermute | solution.py:37
  32.2 2.1 %collective-permute-start.6 = (bf16[2,4,112,512]{3,2,1,0:T(8,128)(2,1)S(1)}, bf16[2,4,112,512]{3,2,1,0:T(8,128)(2,1)S(1)}, u32[]{:S(2)}, u32[]{:S(2)}) collective-permute-start(bf16[2,4,112,512]{3,2,1,0:T(8,128)(2,1)S(1)} %get-tuple-element.45), channel_id=1, source_target_pairs={{0,24},{1,25},{2,26},{3,27},{4,28},{5,29},{6,30},{7,31},{8,16},{9,... | collective-permute-start | bytes 2752520 | tf_op jit(solution)/shard_map/ppermute | solution.py:37
  34.3 3.8 %local_values.7 = (bf16[2,4,112,512]{3,2,1,0:T(8,128)(2,1)S(1)}, bf16[4,112,512]{2,1,0:T(8,128)(2,1)S(1)}, bf16[4,112,512]{2,1,0:T(8,128)(2,1)S(1)}) custom-call(bf16[1792,1024]{1,0:T(8,128)(2,1)S(1)} %get-tuple-element.35.refs_0_, bf16[1792,2048]{1,0:T(8,128)(2,1)S(1)} %copy-done, bf16[1792,2048]{1,0:T(8,128)(2,1)} %bitcast.4, ...), custom_call_target="tpu_custom_call" | custom-call | bytes 1000000 | tf_op jit(solution)/shard_map/local_values/pallas_call | solution.py:127
  38.1 1.2 collective-permute-start.5
  39.3 2.1 %collective-permute-start.10 = (bf16[4,112,512]{2,1,0:T(8,128)(2,1)S(1)}, bf16[4,112,512]{2,1,0:T(8,128)(2,1)S(1)}, u32[]{:S(2)}, u32[]{:S(2)}) collective-permute-start(bf16[4,112,512]{2,1,0:T(8,128)(2,1)S(1)} %forward.4.refs_1_), channel_id=1, source_target_pairs={{0,24},{1,25},{2,26},{3,27},{4,28},{5,29},{6,30},{7,31},{8,16},{9,... | collective-permute-start | bytes 1376264 | tf_op jit(solution)/shard_map/ppermute | solution.py:37
  41.4 2.6 %collective-permute-done.4.refs_1_.refs_2_ = bf16[2,4,112,512]{3,2,1,0:T(8,128)(2,1)S(1)} collective-permute-done((bf16[2,4,112,512]{3,2,1,0:T(8,128)(2,1)S(1)}, bf16[2,4,112,512]{3,2,1,0:T(8,128)(2,1)S(1)}, u32[]{:S(2)}, u32[]{:S(2)}) %collective-permute-start.4) | collective-permute-done | bytes 917536 | tf_op jit(solution)/shard_map/ppermute | solution.py:37
  44.1 2.7 %collective-permute-done.6.refs_1_.refs_3_ = bf16[2,4,112,512]{3,2,1,0:T(8,128)(2,1)S(1)} collective-permute-done((bf16[2,4,112,512]{3,2,1,0:T(8,128)(2,1)S(1)}, bf16[2,4,112,512]{3,2,1,0:T(8,128)(2,1)S(1)}, u32[]{:S(2)}, u32[]{:S(2)}) %collective-permute-start.6) | collective-permute-done | bytes 917536 | tf_op jit(solution)/shard_map/ppermute | solution.py:37
  47.0 2.2 %collective-permute-start.8 = (bf16[4,112,512]{2,1,0:T(8,128)(2,1)S(1)}, bf16[4,112,512]{2,1,0:T(8,128)(2,1)S(1)}, u32[]{:S(2)}, u32[]{:S(2)}) collective-permute-start(bf16[4,112,512]{2,1,0:T(8,128)(2,1)S(1)} %forward.5.refs_2_), channel_id=1, source_target_pairs={{0,24},{1,25},{2,26},{3,27},{4,28},{5,29},{6,30},{7,31},{8,16},{9,... | collective-permute-start | bytes 1376264 | tf_op jit(solution)/shard_map/ppermute | solution.py:37
  49.2 7.5 %collective-permute-done.5.refs_1_.refs_3_ = bf16[2,4,112,512]{3,2,1,0:T(8,128)(2,1)S(1)} collective-permute-done((bf16[2,4,112,512]{3,2,1,0:T(8,128)(2,1)S(1)}, bf16[2,4,112,512]{3,2,1,0:T(8,128)(2,1)S(1)}, u32[]{:S(2)}, u32[]{:S(2)}) %collective-permute-start.5) | collective-permute-done | bytes 917536 | tf_op jit(solution)/shard_map/ppermute | solution.py:37
  56.8 4.7 %collective-permute-done.10.refs_5_ = bf16[4,112,512]{2,1,0:T(8,128)(2,1)S(1)} collective-permute-done((bf16[4,112,512]{2,1,0:T(8,128)(2,1)S(1)}, bf16[4,112,512]{2,1,0:T(8,128)(2,1)S(1)}, u32[]{:S(2)}, u32[]{:S(2)}) %collective-permute-start.10) | collective-permute-done | bytes 458784 | tf_op jit(solution)/shard_map/ppermute | solution.py:37
  61.5 0.3 ring_sum.2
  61.9 2.0 %collective-permute-start.14 = (bf16[112,1024]{1,0:T(8,128)(2,1)S(1)}, bf16[112,1024]{1,0:T(8,128)(2,1)S(1)}, u32[]{:S(2)}, u32[]{:S(2)}) collective-permute-start(bf16[112,1024]{1,0:T(8,128)(2,1)S(1)} %get-tuple-element.53), channel_id=1, source_target_pairs={{0,2},{1,3},{2,0},{3,1},{4,6},{5,7},{6,4},{7,5},{8,10},{9,11},{10,... | collective-permute-start | bytes 688136 | tf_op jit(solution)/shard_map/ppermute | solution.py:37
  63.9 2.5 %collective-permute-start.15 = (bf16[112,1024]{1,0:T(8,128)(2,1)S(1)}, bf16[112,1024]{1,0:T(8,128)(2,1)S(1)}, u32[]{:S(2)}, u32[]{:S(2)}) collective-permute-start(bf16[112,1024]{1,0:T(8,128)(2,1)S(1)} %get-tuple-element.54), channel_id=1, source_target_pairs={{0,6},{1,7},{2,4},{3,5},{4,2},{5,3},{6,0},{7,1},{8,14},{9,15},{10,... | collective-permute-start | bytes 688136 | tf_op jit(solution)/shard_map/ppermute | solution.py:37
  66.4 1.1 collective-permute-start.16
  67.8 2.1 %collective-permute-start.11 = (bf16[112,1024]{1,0:T(8,128)(2,1)S(1)}, bf16[112,1024]{1,0:T(8,128)(2,1)S(1)}, u32[]{:S(2)}, u32[]{:S(2)}) collective-permute-start(bf16[112,1024]{1,0:T(8,128)(2,1)S(1)} %get-tuple-element.50), channel_id=1, source_target_pairs={{0,2},{1,3},{2,0},{3,1},{4,6},{5,7},{6,4},{7,5},{8,10},{9,11},{10,... | collective-permute-start | bytes 688136 | tf_op jit(solution)/shard_map/ppermute | solution.py:37
  69.8 2.7 %collective-permute-start.12 = (bf16[112,1024]{1,0:T(8,128)(2,1)S(1)}, bf16[112,1024]{1,0:T(8,128)(2,1)S(1)}, u32[]{:S(2)}, u32[]{:S(2)}) collective-permute-start(bf16[112,1024]{1,0:T(8,128)(2,1)S(1)} %get-tuple-element.51), channel_id=1, source_target_pairs={{0,6},{1,7},{2,4},{3,5},{4,2},{5,3},{6,0},{7,1},{8,14},{9,15},{10,... | collective-permute-start | bytes 688136 | tf_op jit(solution)/shard_map/ppermute | solution.py:37
  72.6 1.1 collective-permute-start.13
  74.0 3.3 %collective-permute-start.18 = (bf16[56,1024]{1,0:T(8,128)(2,1)S(1)}, bf16[56,1024]{1,0:T(8,128)(2,1)S(1)}, u32[]{:S(2)}, u32[]{:S(2)}) collective-permute-start(bf16[56,1024]{1,0:T(8,128)(2,1)S(1)} %get-tuple-element.56.refs_4_), channel_id=1, source_target_pairs={{0,1},{1,0},{2,3},{3,2},{4,5},{5,4},{6,7},{7,6},{8,9},{9,8},{10,11... | collective-permute-start | bytes 344072 | tf_op jit(solution)/shard_map/ppermute | solution.py:37
  77.3 1.2 collective-permute-done.12.refs_2_
  78.5 1.6 %collective-permute-done.13.refs_3_ = bf16[112,1024]{1,0:T(8,128)(2,1)S(1)} collective-permute-done((bf16[112,1024]{1,0:T(8,128)(2,1)S(1)}, bf16[112,1024]{1,0:T(8,128)(2,1)S(1)}, u32[]{:S(2)}, u32[]{:S(2)}) %collective-permute-start.13) | collective-permute-done | bytes 229408 | tf_op jit(solution)/shard_map/ppermute | solution.py:37
  80.2 3.3 %collective-permute-start.17 = (bf16[56,1024]{1,0:T(8,128)(2,1)S(1)}, bf16[56,1024]{1,0:T(8,128)(2,1)S(1)}, u32[]{:S(2)}, u32[]{:S(2)}) collective-permute-start(bf16[56,1024]{1,0:T(8,128)(2,1)S(1)} %get-tuple-element.58.refs_3_), channel_id=1, source_target_pairs={{0,1},{1,0},{2,3},{3,2},{4,5},{5,4},{6,7},{7,6},{8,9},{9,8},{10,11... | collective-permute-start | bytes 344072 | tf_op jit(solution)/shard_map/ppermute | solution.py:37
  83.7 0.4 collective-permute-start.20
  84.1 2.5 %collective-permute-done.17.refs_1_ = bf16[56,1024]{1,0:T(8,128)(2,1)S(1)} collective-permute-done((bf16[56,1024]{1,0:T(8,128)(2,1)S(1)}, bf16[56,1024]{1,0:T(8,128)(2,1)S(1)}, u32[]{:S(2)}, u32[]{:S(2)}) %collective-permute-start.17) | collective-permute-done | bytes 114720 | tf_op jit(solution)/shard_map/ppermute | solution.py:37
  86.6 0.9 owner.3
  87.5 2.6 %collective-permute-done.20.refs_1_ = bf16[56,1024]{1,0:T(8,128)(2,1)S(1)} collective-permute-done((bf16[56,1024]{1,0:T(8,128)(2,1)S(1)}, bf16[56,1024]{1,0:T(8,128)(2,1)S(1)}, u32[]{:S(2)}, u32[]{:S(2)}) %collective-permute-start.20) | collective-permute-done | bytes 114720 | tf_op jit(solution)/shard_map/ppermute | solution.py:37
  90.1 1.1 collective-permute-start.24
  91.2 1.6 %collective-permute-start.25 = (bf16[112,1024]{1,0:T(8,128)(2,1)S(1)}, bf16[112,1024]{1,0:T(8,128)(2,1)S(1)}, u32[]{:S(2)}, u32[]{:S(2)}) collective-permute-start(bf16[112,1024]{1,0:T(8,128)(2,1)S(1)} %pair.2.refs_2_.refs_0_), channel_id=1, source_target_pairs={{0,6},{1,7},{2,4},{3,5},{4,2},{5,3},{6,0},{7,1},{8,14},{9,15},{10,... | collective-permute-start | bytes 688136 | tf_op jit(solution)/shard_map/ppermute | solution.py:37
  92.8 1.5 %collective-permute-start.26 = (bf16[112,1024]{1,0:T(8,128)(2,1)S(1)}, bf16[112,1024]{1,0:T(8,128)(2,1)S(1)}, u32[]{:S(2)}, u32[]{:S(2)}) collective-permute-start(bf16[112,1024]{1,0:T(8,128)(2,1)S(1)} %pair.2.refs_2_.refs_0_), channel_id=1, source_target_pairs={{0,4},{1,5},{2,6},{3,7},{4,0},{5,1},{6,2},{7,3},{8,12},{9,13},{10,... | collective-permute-start | bytes 688136 | tf_op jit(solution)/shard_map/ppermute | solution.py:37
  94.3 1.0 collective-permute-start.19
  95.2 5.3 %collective-permute-done.19.refs_1_ = bf16[56,1024]{1,0:T(8,128)(2,1)S(1)} collective-permute-done((bf16[56,1024]{1,0:T(8,128)(2,1)S(1)}, bf16[56,1024]{1,0:T(8,128)(2,1)S(1)}, u32[]{:S(2)}, u32[]{:S(2)}) %collective-permute-start.19) | collective-permute-done | bytes 114720 | tf_op jit(solution)/shard_map/ppermute | solution.py:37
  100.6 0.7 collective-permute-done.25.refs_2_
  101.5 2.2 %collective-permute-start.35 = (bf16[4,112,512]{2,1,0:T(8,128)(2,1)S(1)}, bf16[4,112,512]{2,1,0:T(8,128)(2,1)S(1)}, u32[]{:S(2)}, u32[]{:S(2)}) collective-permute-start(bf16[4,112,512]{2,1,0:T(8,128)(2,1)S(1)} %get-tuple-element.66.refs_1_), channel_id=1, source_target_pairs={{0,24},{1,25},{2,26},{3,27},{4,28},{5,29},{6,30},{7,31},{8,16},{9,... | collective-permute-start | bytes 1376264 | tf_op jit(solution)/shard_map/ppermute | solution.py:37
  103.7 0.3 collective-permute-start.21
  104.0 2.6 %collective-permute-start.22 = (bf16[112,1024]{1,0:T(8,128)(2,1)S(1)}, bf16[112,1024]{1,0:T(8,128)(2,1)S(1)}, u32[]{:S(2)}, u32[]{:S(2)}) collective-permute-start(bf16[112,1024]{1,0:T(8,128)(2,1)S(1)} %pair.3.refs_4_.refs_0_), channel_id=1, source_target_pairs={{0,6},{1,7},{2,4},{3,5},{4,2},{5,3},{6,0},{7,1},{8,14},{9,15},{10,... | collective-permute-start | bytes 688136 | tf_op jit(solution)/shard_map/ppermute | solution.py:37
  106.6 1.5 collective-permute-start.23
  108.1 4.0 %collective-permute-done.21.refs_1_ = bf16[112,1024]{1,0:T(8,128)(2,1)S(1)} collective-permute-done((bf16[112,1024]{1,0:T(8,128)(2,1)S(1)}, bf16[112,1024]{1,0:T(8,128)(2,1)S(1)}, u32[]{:S(2)}, u32[]{:S(2)}) %collective-permute-start.21) | collective-permute-done | bytes 229408 | tf_op jit(solution)/shard_map/ppermute | solution.py:37
  112.1 1.4 collective-permute-start.37
  113.5 1.1 collective-permute-start.38
  114.6 4.7 %collective-permute-done.23.refs_3_ = bf16[112,1024]{1,0:T(8,128)(2,1)S(1)} collective-permute-done((bf16[112,1024]{1,0:T(8,128)(2,1)S(1)}, bf16[112,1024]{1,0:T(8,128)(2,1)S(1)}, u32[]{:S(2)}, u32[]{:S(2)}) %collective-permute-start.23) | collective-permute-done | bytes 229408 | tf_op jit(solution)/shard_map/ppermute | solution.py:37
  119.3 1.9 %collective-permute-start.27 = (bf16[4,112,512]{2,1,0:T(8,128)(2,1)S(1)}, bf16[4,112,512]{2,1,0:T(8,128)(2,1)S(1)}, u32[]{:S(2)}, u32[]{:S(2)}) collective-permute-start(bf16[4,112,512]{2,1,0:T(8,128)(2,1)S(1)} %get-tuple-element.64.refs_0_), channel_id=1, source_target_pairs={{0,8},{1,9},{2,10},{3,11},{4,12},{5,13},{6,14},{7,15},{8,0},{9,1},... | collective-permute-start | bytes 1376264 | tf_op jit(solution)/shard_map/ppermute | solution.py:37
  121.2 0.6 collective-permute-start.29
  121.8 2.6 %collective-permute-start.34 = (bf16[4,112,512]{2,1,0:T(8,128)(2,1)S(1)}, bf16[4,112,512]{2,1,0:T(8,128)(2,1)S(1)}, u32[]{:S(2)}, u32[]{:S(2)}) collective-permute-start(bf16[4,112,512]{2,1,0:T(8,128)(2,1)S(1)} %collective-permute-done.33.refs_2_), channel_id=1, source_target_pairs={{0,24},{1,25},{2,26},{3,27},{4,28},{5,29},{6,30},{7,31},{8,16},{9,... | collective-permute-start | bytes 1376264 | tf_op jit(solution)/shard_map/ppermute | solution.py:37
  124.5 2.0 %collective-permute-start.36 = (bf16[4,112,512]{2,1,0:T(8,128)(2,1)S(1)}, bf16[4,112,512]{2,1,0:T(8,128)(2,1)S(1)}, u32[]{:S(2)}, u32[]{:S(2)}) collective-permute-start(bf16[4,112,512]{2,1,0:T(8,128)(2,1)S(1)} %collective-permute-done.35.refs_5_), channel_id=1, source_target_pairs={{0,8},{1,9},{2,10},{3,11},{4,12},{5,13},{6,14},{7,15},{8,0},{9,1},... | collective-permute-start | bytes 1376264 | tf_op jit(solution)/shard_map/ppermute | solution.py:37
  126.5 1.6 %collective-permute-done.27.refs_2_ = bf16[4,112,512]{2,1,0:T(8,128)(2,1)S(1)} collective-permute-done((bf16[4,112,512]{2,1,0:T(8,128)(2,1)S(1)}, bf16[4,112,512]{2,1,0:T(8,128)(2,1)S(1)}, u32[]{:S(2)}, u32[]{:S(2)}) %collective-permute-start.27) | collective-permute-done | bytes 458784 | tf_op jit(solution)/shard_map/ppermute | solution.py:37
  128.1 0.7 collective-permute-start.32
  128.8 2.1 %collective-permute-done.29.refs_5_ = bf16[4,112,512]{2,1,0:T(8,128)(2,1)S(1)} collective-permute-done((bf16[4,112,512]{2,1,0:T(8,128)(2,1)S(1)}, bf16[4,112,512]{2,1,0:T(8,128)(2,1)S(1)}, u32[]{:S(2)}, u32[]{:S(2)}) %collective-permute-start.29) | collective-permute-done | bytes 458784 | tf_op jit(solution)/shard_map/ppermute | solution.py:37
  130.9 0.6 collective-permute-start.28
  131.5 4.3 %collective-permute-done.34.refs_0_ = bf16[4,112,512]{2,1,0:T(8,128)(2,1)S(1)} collective-permute-done((bf16[4,112,512]{2,1,0:T(8,128)(2,1)S(1)}, bf16[4,112,512]{2,1,0:T(8,128)(2,1)S(1)}, u32[]{:S(2)}, u32[]{:S(2)}) %collective-permute-start.34) | collective-permute-done | bytes 458784 | tf_op jit(solution)/shard_map/ppermute | solution.py:37
  135.8 1.7 %place_update.4.refs_2_ = bf16[1792,2048]{1,0:T(8,128)(2,1)} custom-call(bf16[4,112,512]{2,1,0:T(8,128)(2,1)S(1)} %get-tuple-element.63.refs_4_.refs_0_, bf16[4,112,512]{2,1,0:T(8,128)(2,1)S(1)} %get-tuple-element.66.refs_1_, bf16[4,112,512]{2,1,0:T(8,128)(2,1)S(1)} %collective-permute-done.33.refs_2_, ...), custom_call_target="tpu_custom_call" | custom-call | bytes 40000000 | tf_op jit(solution)/shard_map/place_update/pallas_call | solution.py:252
  137.5 0.4 collective-permute-done.36.refs_1_
  137.9 1.0 place_update.5.refs_6_
  138.9 1.8 %collective-permute-done.32.refs_4_ = bf16[4,112,512]{2,1,0:T(8,128)(2,1)S(1)} collective-permute-done((bf16[4,112,512]{2,1,0:T(8,128)(2,1)S(1)}, bf16[4,112,512]{2,1,0:T(8,128)(2,1)S(1)}, u32[]{:S(2)}, u32[]{:S(2)}) %collective-permute-start.32) | collective-permute-done | bytes 458784 | tf_op jit(solution)/shard_map/ppermute | solution.py:37
  140.7 1.7 %place_update.6.refs_2_ = bf16[1792,2048]{1,0:T(8,128)(2,1)} custom-call(bf16[4,112,512]{2,1,0:T(8,128)(2,1)S(1)} %get-tuple-element.64.refs_0_, bf16[4,112,512]{2,1,0:T(8,128)(2,1)S(1)} %get-tuple-element.65.refs_1_, bf16[4,112,512]{2,1,0:T(8,128)(2,1)S(1)} %collective-permute-done.27.refs_2_, ...), custom_call_target="tpu_custom_call", output_to_operand_aliasing={{}: (6, {})} | custom-call | bytes 40000000 | tf_op jit(solution)/shard_map/place_update/pallas_call | solution.py:252
  142.4 3.2 %collective-permute-done.28.refs_0_ = bf16[4,112,512]{2,1,0:T(8,128)(2,1)S(1)} collective-permute-done((bf16[4,112,512]{2,1,0:T(8,128)(2,1)S(1)}, bf16[4,112,512]{2,1,0:T(8,128)(2,1)S(1)}, u32[]{:S(2)}, u32[]{:S(2)}) %collective-permute-start.28) | collective-permute-done | bytes 458784 | tf_op jit(solution)/shard_map/ppermute | solution.py:37
  145.6 1.0 place_update.7
  (45 shorter events, 2.1 us)
Async XLA Ops:
  0.6 11.1 %collective-permute-start.2 = (bf16[1024,512]{1,0:T(8,128)(2,1)}, bf16[1024,512]{1,0:T(8,128)(2,1)S(1)}, u32[]{:S(2)}, u32[]{:S(2)}) collective-permute-start(bf16[1024,512]{1,0:T(8,128)(2,1)} %refs_3_.1), channel_id=1, source_target_pairs={{0,32},{32,0},{64,96},{96,64},{1,33},{33,1},{65,97},{97,65},{2,34}... | collective-permute-start | bytes 3145736 | tf_op jit(solution)/shard_map/ppermute | solution.py:41
  0.7 25.8 %collective-permute-start = (bf16[1024,512]{1,0:T(8,128)(2,1)}, bf16[1024,512]{1,0:T(8,128)(2,1)S(1)}, u32[]{:S(2)}, u32[]{:S(2)}) collective-permute-start(bf16[1024,512]{1,0:T(8,128)(2,1)} %refs_3_.1), channel_id=1, source_target_pairs={{0,64},{32,96},{64,0},{96,32},{1,65},{33,97},{65,1},{97,33},{2,66}... | collective-permute-start | bytes 3145736 | tf_op jit(solution)/shard_map/ppermute | solution.py:41
  2.5 2.0 %copy-start.1 = (bf16[1024,1792]{1,0:T(8,128)(2,1)S(1)}, bf16[1024,1792]{1,0:T(8,128)(2,1)}, u32[]{:S(2)}) copy-start(bf16[1024,1792]{1,0:T(8,128)(2,1)} %refs_0_.1) | copy-start | bytes 11010052
  4.5 1.2 copy-start.3
  5.7 6.0 %copy-start = (bf16[1792,2048]{1,0:T(8,128)(2,1)S(1)}, bf16[1792,2048]{1,0:T(8,128)(2,1)}, u32[]{:S(2)}) copy-start(bf16[1792,2048]{1,0:T(8,128)(2,1)} %refs_1_.7) | copy-start | bytes 22020100
  10.1 13.5 %collective-permute-start.1 = (bf16[2,4,112,512]{3,2,1,0:T(8,128)(2,1)S(1)}, bf16[2,4,112,512]{3,2,1,0:T(8,128)(2,1)S(1)}, u32[]{:S(2)}, u32[]{:S(2)}) collective-permute-start(bf16[2,4,112,512]{3,2,1,0:T(8,128)(2,1)S(1)} %get-tuple-element.37), channel_id=1, source_target_pairs={{0,8},{1,9},{2,10},{3,11},{4,12},{5,13},{6,14},{7,15},{8,0},{9,1},... | collective-permute-start | bytes 2752520 | tf_op jit(solution)/shard_map/ppermute | solution.py:37
  26.6 7.7 %collective-permute-start.3 = (bf16[1024,512]{1,0:T(8,128)(2,1)S(1)}, bf16[1024,512]{1,0:T(8,128)(2,1)S(1)}, u32[]{:S(2)}, u32[]{:S(2)}) collective-permute-start(bf16[1024,512]{1,0:T(8,128)(2,1)S(1)} %take_far.1.refs_3_.refs_4_), channel_id=1, source_target_pairs={{0,32},{32,0},{64,96},{96,64},{1,33},{33,1},{65,97},{97,65},{2,34}... | collective-permute-start | bytes 3145736 | tf_op jit(solution)/shard_map/ppermute | solution.py:41
  30.5 13.5 %collective-permute-start.4 = (bf16[2,4,112,512]{3,2,1,0:T(8,128)(2,1)S(1)}, bf16[2,4,112,512]{3,2,1,0:T(8,128)(2,1)S(1)}, u32[]{:S(2)}, u32[]{:S(2)}) collective-permute-start(bf16[2,4,112,512]{3,2,1,0:T(8,128)(2,1)S(1)} %get-tuple-element.42), channel_id=1, source_target_pairs={{0,8},{1,9},{2,10},{3,11},{4,12},{5,13},{6,14},{7,15},{8,0},{9,1},... | collective-permute-start | bytes 2752520 | tf_op jit(solution)/shard_map/ppermute | solution.py:37
  32.2 14.6 %collective-permute-start.6 = (bf16[2,4,112,512]{3,2,1,0:T(8,128)(2,1)S(1)}, bf16[2,4,112,512]{3,2,1,0:T(8,128)(2,1)S(1)}, u32[]{:S(2)}, u32[]{:S(2)}) collective-permute-start(bf16[2,4,112,512]{3,2,1,0:T(8,128)(2,1)S(1)} %get-tuple-element.45), channel_id=1, source_target_pairs={{0,24},{1,25},{2,26},{3,27},{4,28},{5,29},{6,30},{7,31},{8,16},{9,... | collective-permute-start | bytes 2752520 | tf_op jit(solution)/shard_map/ppermute | solution.py:37
  38.1 18.5 %collective-permute-start.5 = (bf16[2,4,112,512]{3,2,1,0:T(8,128)(2,1)S(1)}, bf16[2,4,112,512]{3,2,1,0:T(8,128)(2,1)S(1)}, u32[]{:S(2)}, u32[]{:S(2)}) collective-permute-start(bf16[2,4,112,512]{3,2,1,0:T(8,128)(2,1)S(1)} %get-tuple-element.43), channel_id=1, source_target_pairs={{0,24},{1,25},{2,26},{3,27},{4,28},{5,29},{6,30},{7,31},{8,16},{9,... | collective-permute-start | bytes 2752520 | tf_op jit(solution)/shard_map/ppermute | solution.py:37
  39.3 22.2 %collective-permute-start.10 = (bf16[4,112,512]{2,1,0:T(8,128)(2,1)S(1)}, bf16[4,112,512]{2,1,0:T(8,128)(2,1)S(1)}, u32[]{:S(2)}, u32[]{:S(2)}) collective-permute-start(bf16[4,112,512]{2,1,0:T(8,128)(2,1)S(1)} %forward.4.refs_1_), channel_id=1, source_target_pairs={{0,24},{1,25},{2,26},{3,27},{4,28},{5,29},{6,30},{7,31},{8,16},{9,... | collective-permute-start | bytes 1376264 | tf_op jit(solution)/shard_map/ppermute | solution.py:37
  44.1 39.4 %copy-start.2 = (f32[56,2048]{1,0:T(8,128)S(1)}, f32[56,2048]{1,0:T(8,128)}, u32[]{:S(2)}) copy-start(f32[56,2048]{1,0:T(8,128)} %refs_2_.3) | copy-start | bytes 1376260
  46.9 14.6 %collective-permute-start.9 = (bf16[4,112,512]{2,1,0:T(8,128)(2,1)S(1)}, bf16[4,112,512]{2,1,0:T(8,128)(2,1)S(1)}, u32[]{:S(2)}, u32[]{:S(2)}) collective-permute-start(bf16[4,112,512]{2,1,0:T(8,128)(2,1)S(1)} %forward.6.refs_2_), channel_id=1, source_target_pairs={{0,8},{1,9},{2,10},{3,11},{4,12},{5,13},{6,14},{7,15},{8,0},{9,1},... | collective-permute-start | bytes 1376264 | tf_op jit(solution)/shard_map/ppermute | solution.py:37
  47.0 20.5 %collective-permute-start.8 = (bf16[4,112,512]{2,1,0:T(8,128)(2,1)S(1)}, bf16[4,112,512]{2,1,0:T(8,128)(2,1)S(1)}, u32[]{:S(2)}, u32[]{:S(2)}) collective-permute-start(bf16[4,112,512]{2,1,0:T(8,128)(2,1)S(1)} %forward.5.refs_2_), channel_id=1, source_target_pairs={{0,24},{1,25},{2,26},{3,27},{4,28},{5,29},{6,30},{7,31},{8,16},{9,... | collective-permute-start | bytes 1376264 | tf_op jit(solution)/shard_map/ppermute | solution.py:37
  56.7 10.7 %collective-permute-start.7 = (bf16[4,112,512]{2,1,0:T(8,128)(2,1)S(1)}, bf16[4,112,512]{2,1,0:T(8,128)(2,1)S(1)}, u32[]{:S(2)}, u32[]{:S(2)}) collective-permute-start(bf16[4,112,512]{2,1,0:T(8,128)(2,1)S(1)} %forward.7.refs_6_), channel_id=1, source_target_pairs={{0,8},{1,9},{2,10},{3,11},{4,12},{5,13},{6,14},{7,15},{8,0},{9,1},... | collective-permute-start | bytes 1376264 | tf_op jit(solution)/shard_map/ppermute | solution.py:37
  61.9 10.7 %collective-permute-start.14 = (bf16[112,1024]{1,0:T(8,128)(2,1)S(1)}, bf16[112,1024]{1,0:T(8,128)(2,1)S(1)}, u32[]{:S(2)}, u32[]{:S(2)}) collective-permute-start(bf16[112,1024]{1,0:T(8,128)(2,1)S(1)} %get-tuple-element.53), channel_id=1, source_target_pairs={{0,2},{1,3},{2,0},{3,1},{4,6},{5,7},{6,4},{7,5},{8,10},{9,11},{10,... | collective-permute-start | bytes 688136 | tf_op jit(solution)/shard_map/ppermute | solution.py:37
  63.9 9.8 %collective-permute-start.15 = (bf16[112,1024]{1,0:T(8,128)(2,1)S(1)}, bf16[112,1024]{1,0:T(8,128)(2,1)S(1)}, u32[]{:S(2)}, u32[]{:S(2)}) collective-permute-start(bf16[112,1024]{1,0:T(8,128)(2,1)S(1)} %get-tuple-element.54), channel_id=1, source_target_pairs={{0,6},{1,7},{2,4},{3,5},{4,2},{5,3},{6,0},{7,1},{8,14},{9,15},{10,... | collective-permute-start | bytes 688136 | tf_op jit(solution)/shard_map/ppermute | solution.py:37
  66.4 7.5 %collective-permute-start.16 = (bf16[112,1024]{1,0:T(8,128)(2,1)S(1)}, bf16[112,1024]{1,0:T(8,128)(2,1)S(1)}, u32[]{:S(2)}, u32[]{:S(2)}) collective-permute-start(bf16[112,1024]{1,0:T(8,128)(2,1)S(1)} %get-tuple-element.55), channel_id=1, source_target_pairs={{0,4},{1,5},{2,6},{3,7},{4,0},{5,1},{6,2},{7,3},{8,12},{9,13},{10,... | collective-permute-start | bytes 688136 | tf_op jit(solution)/shard_map/ppermute | solution.py:37
  67.8 9.5 %collective-permute-start.11 = (bf16[112,1024]{1,0:T(8,128)(2,1)S(1)}, bf16[112,1024]{1,0:T(8,128)(2,1)S(1)}, u32[]{:S(2)}, u32[]{:S(2)}) collective-permute-start(bf16[112,1024]{1,0:T(8,128)(2,1)S(1)} %get-tuple-element.50), channel_id=1, source_target_pairs={{0,2},{1,3},{2,0},{3,1},{4,6},{5,7},{6,4},{7,5},{8,10},{9,11},{10,... | collective-permute-start | bytes 688136 | tf_op jit(solution)/shard_map/ppermute | solution.py:37
  69.8 8.7 %collective-permute-start.12 = (bf16[112,1024]{1,0:T(8,128)(2,1)S(1)}, bf16[112,1024]{1,0:T(8,128)(2,1)S(1)}, u32[]{:S(2)}, u32[]{:S(2)}) collective-permute-start(bf16[112,1024]{1,0:T(8,128)(2,1)S(1)} %get-tuple-element.51), channel_id=1, source_target_pairs={{0,6},{1,7},{2,4},{3,5},{4,2},{5,3},{6,0},{7,1},{8,14},{9,15},{10,... | collective-permute-start | bytes 688136 | tf_op jit(solution)/shard_map/ppermute | solution.py:37
  72.6 7.6 %collective-permute-start.13 = (bf16[112,1024]{1,0:T(8,128)(2,1)S(1)}, bf16[112,1024]{1,0:T(8,128)(2,1)S(1)}, u32[]{:S(2)}, u32[]{:S(2)}) collective-permute-start(bf16[112,1024]{1,0:T(8,128)(2,1)S(1)} %get-tuple-element.52), channel_id=1, source_target_pairs={{0,4},{1,5},{2,6},{3,7},{4,0},{5,1},{6,2},{7,3},{8,12},{9,13},{10,... | collective-permute-start | bytes 688136 | tf_op jit(solution)/shard_map/ppermute | solution.py:37
  74.0 9.5 %collective-permute-start.18 = (bf16[56,1024]{1,0:T(8,128)(2,1)S(1)}, bf16[56,1024]{1,0:T(8,128)(2,1)S(1)}, u32[]{:S(2)}, u32[]{:S(2)}) collective-permute-start(bf16[56,1024]{1,0:T(8,128)(2,1)S(1)} %get-tuple-element.56.refs_4_), channel_id=1, source_target_pairs={{0,1},{1,0},{2,3},{3,2},{4,5},{5,4},{6,7},{7,6},{8,9},{9,8},{10,11... | collective-permute-start | bytes 344072 | tf_op jit(solution)/shard_map/ppermute | solution.py:37
  80.2 6.4 %collective-permute-start.17 = (bf16[56,1024]{1,0:T(8,128)(2,1)S(1)}, bf16[56,1024]{1,0:T(8,128)(2,1)S(1)}, u32[]{:S(2)}, u32[]{:S(2)}) collective-permute-start(bf16[56,1024]{1,0:T(8,128)(2,1)S(1)} %get-tuple-element.58.refs_3_), channel_id=1, source_target_pairs={{0,1},{1,0},{2,3},{3,2},{4,5},{5,4},{6,7},{7,6},{8,9},{9,8},{10,11... | collective-permute-start | bytes 344072 | tf_op jit(solution)/shard_map/ppermute | solution.py:37
  83.7 6.4 %collective-permute-start.20 = (bf16[56,1024]{1,0:T(8,128)(2,1)S(1)}, bf16[56,1024]{1,0:T(8,128)(2,1)S(1)}, u32[]{:S(2)}, u32[]{:S(2)}) collective-permute-start(bf16[56,1024]{1,0:T(8,128)(2,1)S(1)} %get-tuple-element.61.refs_4_.refs_0_), channel_id=1, source_target_pairs={{0,1},{1,0},{2,3},{3,2},{4,5},{5,4},{6,7},{7,6},{8,9},{9,8},{10,11... | collective-permute-start | bytes 344072 | tf_op jit(solution)/shard_map/ppermute | solution.py:37
  90.1 10.5 %collective-permute-start.24 = (bf16[112,1024]{1,0:T(8,128)(2,1)S(1)}, bf16[112,1024]{1,0:T(8,128)(2,1)S(1)}, u32[]{:S(2)}, u32[]{:S(2)}) collective-permute-start(bf16[112,1024]{1,0:T(8,128)(2,1)S(1)} %pair.2.refs_2_.refs_0_), channel_id=1, source_target_pairs={{0,2},{1,3},{2,0},{3,1},{4,6},{5,7},{6,4},{7,5},{8,10},{9,11},{10,... | collective-permute-start | bytes 688136 | tf_op jit(solution)/shard_map/ppermute | solution.py:37
  91.2 10.1 %collective-permute-start.25 = (bf16[112,1024]{1,0:T(8,128)(2,1)S(1)}, bf16[112,1024]{1,0:T(8,128)(2,1)S(1)}, u32[]{:S(2)}, u32[]{:S(2)}) collective-permute-start(bf16[112,1024]{1,0:T(8,128)(2,1)S(1)} %pair.2.refs_2_.refs_0_), channel_id=1, source_target_pairs={{0,6},{1,7},{2,4},{3,5},{4,2},{5,3},{6,0},{7,1},{8,14},{9,15},{10,... | collective-permute-start | bytes 688136 | tf_op jit(solution)/shard_map/ppermute | solution.py:37
  92.8 8.6 %collective-permute-start.26 = (bf16[112,1024]{1,0:T(8,128)(2,1)S(1)}, bf16[112,1024]{1,0:T(8,128)(2,1)S(1)}, u32[]{:S(2)}, u32[]{:S(2)}) collective-permute-start(bf16[112,1024]{1,0:T(8,128)(2,1)S(1)} %pair.2.refs_2_.refs_0_), channel_id=1, source_target_pairs={{0,4},{1,5},{2,6},{3,7},{4,0},{5,1},{6,2},{7,3},{8,12},{9,13},{10,... | collective-permute-start | bytes 688136 | tf_op jit(solution)/shard_map/ppermute | solution.py:37
  94.3 6.3 %collective-permute-start.19 = (bf16[56,1024]{1,0:T(8,128)(2,1)S(1)}, bf16[56,1024]{1,0:T(8,128)(2,1)S(1)}, u32[]{:S(2)}, u32[]{:S(2)}) collective-permute-start(bf16[56,1024]{1,0:T(8,128)(2,1)S(1)} %get-tuple-element.62.refs_2_.refs_0_), channel_id=1, source_target_pairs={{0,1},{1,0},{2,3},{3,2},{4,5},{5,4},{6,7},{7,6},{8,9},{9,8},{10,11... | collective-permute-start | bytes 344072 | tf_op jit(solution)/shard_map/ppermute | solution.py:37
  101.4 19.8 %collective-permute-start.33 = (bf16[4,112,512]{2,1,0:T(8,128)(2,1)S(1)}, bf16[4,112,512]{2,1,0:T(8,128)(2,1)S(1)}, u32[]{:S(2)}, u32[]{:S(2)}) collective-permute-start(bf16[4,112,512]{2,1,0:T(8,128)(2,1)S(1)} %get-tuple-element.63.refs_4_.refs_0_), channel_id=1, source_target_pairs={{0,8},{1,9},{2,10},{3,11},{4,12},{5,13},{6,14},{7,15},{8,0},{9,1},... | collective-permute-start | bytes 1376264 | tf_op jit(solution)/shard_map/ppermute | solution.py:37
  101.5 20.3 %collective-permute-start.35 = (bf16[4,112,512]{2,1,0:T(8,128)(2,1)S(1)}, bf16[4,112,512]{2,1,0:T(8,128)(2,1)S(1)}, u32[]{:S(2)}, u32[]{:S(2)}) collective-permute-start(bf16[4,112,512]{2,1,0:T(8,128)(2,1)S(1)} %get-tuple-element.66.refs_1_), channel_id=1, source_target_pairs={{0,24},{1,25},{2,26},{3,27},{4,28},{5,29},{6,30},{7,31},{8,16},{9,... | collective-permute-start | bytes 1376264 | tf_op jit(solution)/shard_map/ppermute | solution.py:37
  103.7 8.5 %collective-permute-start.21 = (bf16[112,1024]{1,0:T(8,128)(2,1)S(1)}, bf16[112,1024]{1,0:T(8,128)(2,1)S(1)}, u32[]{:S(2)}, u32[]{:S(2)}) collective-permute-start(bf16[112,1024]{1,0:T(8,128)(2,1)S(1)} %pair.3.refs_4_.refs_0_), channel_id=1, source_target_pairs={{0,2},{1,3},{2,0},{3,1},{4,6},{5,7},{6,4},{7,5},{8,10},{9,11},{10,... | collective-permute-start | bytes 688136 | tf_op jit(solution)/shard_map/ppermute | solution.py:37
  104.0 9.5 %collective-permute-start.22 = (bf16[112,1024]{1,0:T(8,128)(2,1)S(1)}, bf16[112,1024]{1,0:T(8,128)(2,1)S(1)}, u32[]{:S(2)}, u32[]{:S(2)}) collective-permute-start(bf16[112,1024]{1,0:T(8,128)(2,1)S(1)} %pair.3.refs_4_.refs_0_), channel_id=1, source_target_pairs={{0,6},{1,7},{2,4},{3,5},{4,2},{5,3},{6,0},{7,1},{8,14},{9,15},{10,... | collective-permute-start | bytes 688136 | tf_op jit(solution)/shard_map/ppermute | solution.py:37
  106.6 12.6 %collective-permute-start.23 = (bf16[112,1024]{1,0:T(8,128)(2,1)S(1)}, bf16[112,1024]{1,0:T(8,128)(2,1)S(1)}, u32[]{:S(2)}, u32[]{:S(2)}) collective-permute-start(bf16[112,1024]{1,0:T(8,128)(2,1)S(1)} %pair.3.refs_4_.refs_0_), channel_id=1, source_target_pairs={{0,4},{1,5},{2,6},{3,7},{4,0},{5,1},{6,2},{7,3},{8,12},{9,13},{10,... | collective-permute-start | bytes 688136 | tf_op jit(solution)/shard_map/ppermute | solution.py:37
  112.1 12.3 %collective-permute-start.37 = (bf16[4,112,512]{2,1,0:T(8,128)(2,1)S(1)}, bf16[4,112,512]{2,1,0:T(8,128)(2,1)S(1)}, u32[]{:S(2)}, u32[]{:S(2)}) collective-permute-start(bf16[4,112,512]{2,1,0:T(8,128)(2,1)S(1)} %get-tuple-element.66.refs_1_), channel_id=1, source_target_pairs={{0,8},{1,9},{2,10},{3,11},{4,12},{5,13},{6,14},{7,15},{8,0},{9,1},... | collective-permute-start | bytes 1376264 | tf_op jit(solution)/shard_map/ppermute | solution.py:37
  113.5 10.9 %collective-permute-start.38 = (bf16[4,112,512]{2,1,0:T(8,128)(2,1)S(1)}, bf16[4,112,512]{2,1,0:T(8,128)(2,1)S(1)}, u32[]{:S(2)}, u32[]{:S(2)}) collective-permute-start(bf16[4,112,512]{2,1,0:T(8,128)(2,1)S(1)} %get-tuple-element.63.refs_4_.refs_0_), channel_id=1, source_target_pairs={{0,24},{1,25},{2,26},{3,27},{4,28},{5,29},{6,30},{7,31},{8,16},{9,... | collective-permute-start | bytes 1376264 | tf_op jit(solution)/shard_map/ppermute | solution.py:37
  119.3 8.8 %collective-permute-start.27 = (bf16[4,112,512]{2,1,0:T(8,128)(2,1)S(1)}, bf16[4,112,512]{2,1,0:T(8,128)(2,1)S(1)}, u32[]{:S(2)}, u32[]{:S(2)}) collective-permute-start(bf16[4,112,512]{2,1,0:T(8,128)(2,1)S(1)} %get-tuple-element.64.refs_0_), channel_id=1, source_target_pairs={{0,8},{1,9},{2,10},{3,11},{4,12},{5,13},{6,14},{7,15},{8,0},{9,1},... | collective-permute-start | bytes 1376264 | tf_op jit(solution)/shard_map/ppermute | solution.py:37
  121.2 9.7 %collective-permute-start.29 = (bf16[4,112,512]{2,1,0:T(8,128)(2,1)S(1)}, bf16[4,112,512]{2,1,0:T(8,128)(2,1)S(1)}, u32[]{:S(2)}, u32[]{:S(2)}) collective-permute-start(bf16[4,112,512]{2,1,0:T(8,128)(2,1)S(1)} %get-tuple-element.65.refs_1_), channel_id=1, source_target_pairs={{0,24},{1,25},{2,26},{3,27},{4,28},{5,29},{6,30},{7,31},{8,16},{9,... | collective-permute-start | bytes 1376264 | tf_op jit(solution)/shard_map/ppermute | solution.py:37
  121.8 14.0 %collective-permute-start.34 = (bf16[4,112,512]{2,1,0:T(8,128)(2,1)S(1)}, bf16[4,112,512]{2,1,0:T(8,128)(2,1)S(1)}, u32[]{:S(2)}, u32[]{:S(2)}) collective-permute-start(bf16[4,112,512]{2,1,0:T(8,128)(2,1)S(1)} %collective-permute-done.33.refs_2_), channel_id=1, source_target_pairs={{0,24},{1,25},{2,26},{3,27},{4,28},{5,29},{6,30},{7,31},{8,16},{9,... | collective-permute-start | bytes 1376264 | tf_op jit(solution)/shard_map/ppermute | solution.py:37
  124.4 14.5 %collective-permute-start.31 = (bf16[4,112,512]{2,1,0:T(8,128)(2,1)S(1)}, bf16[4,112,512]{2,1,0:T(8,128)(2,1)S(1)}, u32[]{:S(2)}, u32[]{:S(2)}) collective-permute-start(bf16[4,112,512]{2,1,0:T(8,128)(2,1)S(1)} %get-tuple-element.65.refs_1_), channel_id=1, source_target_pairs={{0,8},{1,9},{2,10},{3,11},{4,12},{5,13},{6,14},{7,15},{8,0},{9,1},... | collective-permute-start | bytes 1376264 | tf_op jit(solution)/shard_map/ppermute | solution.py:37
  124.5 13.5 %collective-permute-start.36 = (bf16[4,112,512]{2,1,0:T(8,128)(2,1)S(1)}, bf16[4,112,512]{2,1,0:T(8,128)(2,1)S(1)}, u32[]{:S(2)}, u32[]{:S(2)}) collective-permute-start(bf16[4,112,512]{2,1,0:T(8,128)(2,1)S(1)} %collective-permute-done.35.refs_5_), channel_id=1, source_target_pairs={{0,8},{1,9},{2,10},{3,11},{4,12},{5,13},{6,14},{7,15},{8,0},{9,1},... | collective-permute-start | bytes 1376264 | tf_op jit(solution)/shard_map/ppermute | solution.py:37
  128.1 12.6 %collective-permute-start.32 = (bf16[4,112,512]{2,1,0:T(8,128)(2,1)S(1)}, bf16[4,112,512]{2,1,0:T(8,128)(2,1)S(1)}, u32[]{:S(2)}, u32[]{:S(2)}) collective-permute-start(bf16[4,112,512]{2,1,0:T(8,128)(2,1)S(1)} %get-tuple-element.64.refs_0_), channel_id=1, source_target_pairs={{0,24},{1,25},{2,26},{3,27},{4,28},{5,29},{6,30},{7,31},{8,16},{9,... | collective-permute-start | bytes 1376264 | tf_op jit(solution)/shard_map/ppermute | solution.py:37
  130.9 14.7 %collective-permute-start.28 = (bf16[4,112,512]{2,1,0:T(8,128)(2,1)S(1)}, bf16[4,112,512]{2,1,0:T(8,128)(2,1)S(1)}, u32[]{:S(2)}, u32[]{:S(2)}) collective-permute-start(bf16[4,112,512]{2,1,0:T(8,128)(2,1)S(1)} %collective-permute-done.27.refs_2_), channel_id=1, source_target_pairs={{0,24},{1,25},{2,26},{3,27},{4,28},{5,29},{6,30},{7,31},{8,16},{9,... | collective-permute-start | bytes 1376264 | tf_op jit(solution)/shard_map/ppermute | solution.py:37
  135.8 9.8 %collective-permute-start.30 = (bf16[4,112,512]{2,1,0:T(8,128)(2,1)S(1)}, bf16[4,112,512]{2,1,0:T(8,128)(2,1)S(1)}, u32[]{:S(2)}, u32[]{:S(2)}) collective-permute-start(bf16[4,112,512]{2,1,0:T(8,128)(2,1)S(1)} %collective-permute-done.29.refs_5_), channel_id=1, source_target_pairs={{0,8},{1,9},{2,10},{3,11},{4,12},{5,13},{6,14},{7,15},{8,0},{9,1},... | collective-permute-start | bytes 1376264 | tf_op jit(solution)/shard_map/ppermute | solution.py:37

commit v3 on v2

--- a/solution.py
+++ b/solution.py
@@ -346,8 +346,8 @@
 
 GATHERS = ("sides", "sides")
 ORDER = (
-    "La0", "La1", "Fa0", "G", "Lb0", "Lb1", "Fb0", "Fa1", "Fb1", "Sa",
-    "Sb", "Pa", "Pb", "Oa", "Ob", "Qa", "Qb", "Ka", "Kb",
+    "La0", "La1", "Fa01", "G", "Lb0", "Lb1", "Fb0", "Fb1", "Sa", "Sb",
+    "Pa", "Pb", "Oa", "Ob", "Qa", "Qb", "Ka", "Kb",
 )
 
 

time: 147 us -> 142 us (0.966)
  starting transfers between devices: 54 us -> 51.3 us
  waiting for transfers between devices: 64.6 us -> 62.4 us
    ppermute x3, waiting for transfers between devices: 2.81 us -> 0.01 us  [swap_tp(): return lax.ppermute(array, 'tp', [(i, i ^ mask) for i in range(4)])]
    ppermute x36, starting transfers between devices: 52.1 us -> 49.4 us  [permute(): return lax.ppermute(array, AXES, pairs)]
  transfers between devices with their start and end apart: 39 -> 39, of which waited for: 21 -> 21; matrix products, arithmetic and copies ran while one was open for 0% -> 0% of each run, Pallas kernels for 15% -> 16%
where the time goes in v3:
time: 142 us
  waiting for transfers between devices  62.4 us (44%)
  starting transfers between devices  51.3 us (36%)
  Pallas kernels  23.8 us (17%)
  local copies, waits for them, and re-layouts  3.27 us (2%)
    ppermute x36, waiting for transfers between devices, permute(): return lax.ppermute(array, AXES, pairs)  62.4 us
    ppermute x36, starting transfers between devices, permute(): return lax.ppermute(array, AXES, pairs)  49.4 us
    pallas_call x4, Pallas kernels, local_values(): pl.pallas_call(lambda *refs: local_kernel(chunk, sides, tile, *refs), in_...  15.9 us
    pallas_call x4, Pallas kernels, place(): pl.pallas_call(lambda *refs: place_kernel(pieces, *refs), in_specs=[pl.Bl...  5.39 us
    unnamed x8, local copies, waits for them, and re-layouts  3.27 us
  transfers between devices with their start and end apart: 39, of which 21 were waited for; matrix products, arithmetic and copies ran while one was open for 0% of the time, Pallas kernels for 16%

profile of v3, /device:TPU:0, one launch (start us, length us, event | category | flops | bytes accessed | tf_op | source)
XLA Modules:
  0.0 141.9 jit_solution(18138511433301682773)
XLA Ops:
  0.7 1.7 %collective-permute-start = (bf16[1024,512]{1,0:T(8,128)(2,1)}, bf16[1024,512]{1,0:T(8,128)(2,1)S(1)}, u32[]{:S(2)}, u32[]{:S(2)}) collective-permute-start(bf16[1024,512]{1,0:T(8,128)(2,1)} %refs_3_.1), channel_id=1, source_target_pairs={{0,64},{32,96},{64,0},{96,32},{1,65},{33,97},{65,1},{97,33},{2,66}... | collective-permute-start | bytes 3145736 | tf_op jit(solution)/shard_map/ppermute | solution.py:41
  2.5 2.0 %copy-done.1 = bf16[1024,1792]{1,0:T(8,128)(2,1)S(1)} copy-done((bf16[1024,1792]{1,0:T(8,128)(2,1)S(1)}, bf16[1024,1792]{1,0:T(8,128)(2,1)}, u32[]{:S(2)}) %copy-start.1) | copy-done | bytes 3670040
  4.5 1.2 copy-done.3
  5.7 4.4 %local_values.4 = (bf16[1792,1024]{1,0:T(8,128)(2,1)S(1)}, bf16[2,4,112,512]{3,2,1,0:T(8,128)(2,1)S(1)}, bf16[4,112,512]{2,1,0:T(8,128)(2,1)S(1)}, bf16[4,112,512]{2,1,0:T(8,128)(2,1)S(1)}) custom-call(bf16[1024,1792]{1,0:T(8,128)(2,1)S(1)} %copy-done.1, bf16[1792,2048]{1,0:T(8,128)(2,1)} %refs_1_.7, bf16[1792,2048]{1,0:T(8,128)(2,1)} %bitcast.1, ...), custom_call_target="tpu_custom_call" | custom-call | bytes 1000000 | tf_op jit(solution)/shard_map/local_values/pallas_call | solution.py:127
  10.1 1.6 %collective-permute-start.2 = (bf16[2,4,112,512]{3,2,1,0:T(8,128)(2,1)S(1)}, bf16[2,4,112,512]{3,2,1,0:T(8,128)(2,1)S(1)}, u32[]{:S(2)}, u32[]{:S(2)}) collective-permute-start(bf16[2,4,112,512]{3,2,1,0:T(8,128)(2,1)S(1)} %get-tuple-element.40), channel_id=1, source_target_pairs={{0,8},{1,9},{2,10},{3,11},{4,12},{5,13},{6,14},{7,15},{8,0},{9,1},... | collective-permute-start | bytes 2752520 | tf_op jit(solution)/shard_map/ppermute | solution.py:37
  11.7 3.8 %local_values.5 = (bf16[2,4,112,512]{3,2,1,0:T(8,128)(2,1)S(1)}, bf16[4,112,512]{2,1,0:T(8,128)(2,1)S(1)}, bf16[4,112,512]{2,1,0:T(8,128)(2,1)S(1)}) custom-call(bf16[1792,1024]{1,0:T(8,128)(2,1)S(1)} %get-tuple-element.37.refs_0_, bf16[1792,2048]{1,0:T(8,128)(2,1)S(1)} %copy-done, bf16[1792,2048]{1,0:T(8,128)(2,1)} %bitcast.2, ...), custom_call_target="tpu_custom_call" | custom-call | bytes 1000000 | tf_op jit(solution)/shard_map/local_values/pallas_call | solution.py:127
  15.5 2.2 %collective-permute-start.3 = (bf16[2,4,112,512]{3,2,1,0:T(8,128)(2,1)S(1)}, bf16[2,4,112,512]{3,2,1,0:T(8,128)(2,1)S(1)}, u32[]{:S(2)}, u32[]{:S(2)}) collective-permute-start(bf16[2,4,112,512]{3,2,1,0:T(8,128)(2,1)S(1)} %get-tuple-element.41), channel_id=1, source_target_pairs={{0,24},{1,25},{2,26},{3,27},{4,28},{5,29},{6,30},{7,31},{8,16},{9,... | collective-permute-start | bytes 2752520 | tf_op jit(solution)/shard_map/ppermute | solution.py:37
  17.7 5.9 %collective-permute-done.2.refs_2_ = bf16[2,4,112,512]{3,2,1,0:T(8,128)(2,1)S(1)} collective-permute-done((bf16[2,4,112,512]{3,2,1,0:T(8,128)(2,1)S(1)}, bf16[2,4,112,512]{3,2,1,0:T(8,128)(2,1)S(1)}, u32[]{:S(2)}, u32[]{:S(2)}) %collective-permute-start.2) | collective-permute-done | bytes 917536 | tf_op jit(solution)/shard_map/ppermute | solution.py:37
  23.6 6.6 %collective-permute-done.3.refs_3_ = bf16[2,4,112,512]{3,2,1,0:T(8,128)(2,1)S(1)} collective-permute-done((bf16[2,4,112,512]{3,2,1,0:T(8,128)(2,1)S(1)}, bf16[2,4,112,512]{3,2,1,0:T(8,128)(2,1)S(1)}, u32[]{:S(2)}, u32[]{:S(2)}) %collective-permute-start.3) | collective-permute-done | bytes 917536 | tf_op jit(solution)/shard_map/ppermute | solution.py:37
  30.6 3.8 %local_values.6 = (bf16[2,4,112,512]{3,2,1,0:T(8,128)(2,1)S(1)}, bf16[4,112,512]{2,1,0:T(8,128)(2,1)S(1)}, bf16[4,112,512]{2,1,0:T(8,128)(2,1)S(1)}) custom-call(bf16[1792,1024]{1,0:T(8,128)(2,1)S(1)} %get-tuple-element.37.refs_0_, bf16[1792,2048]{1,0:T(8,128)(2,1)S(1)} %copy-done, bf16[1792,2048]{1,0:T(8,128)(2,1)} %bitcast.3, ...), custom_call_target="tpu_custom_call" | custom-call | bytes 1000000 | tf_op jit(solution)/shard_map/local_values/pallas_call | solution.py:127
  34.5 0.9 collective-permute-start.5
  35.3 3.8 %local_values.7 = (bf16[2,4,112,512]{3,2,1,0:T(8,128)(2,1)S(1)}, bf16[4,112,512]{2,1,0:T(8,128)(2,1)S(1)}, bf16[4,112,512]{2,1,0:T(8,128)(2,1)S(1)}) custom-call(bf16[1792,1024]{1,0:T(8,128)(2,1)S(1)} %get-tuple-element.37.refs_0_, bf16[1792,2048]{1,0:T(8,128)(2,1)S(1)} %copy-done, bf16[1792,2048]{1,0:T(8,128)(2,1)} %bitcast.4, ...), custom_call_target="tpu_custom_call" | custom-call | bytes 1000000 | tf_op jit(solution)/shard_map/local_values/pallas_call | solution.py:127
  39.2 2.2 %collective-permute-start.6 = (bf16[2,4,112,512]{3,2,1,0:T(8,128)(2,1)S(1)}, bf16[2,4,112,512]{3,2,1,0:T(8,128)(2,1)S(1)}, u32[]{:S(2)}, u32[]{:S(2)}) collective-permute-start(bf16[2,4,112,512]{3,2,1,0:T(8,128)(2,1)S(1)} %get-tuple-element.47), channel_id=1, source_target_pairs={{0,24},{1,25},{2,26},{3,27},{4,28},{5,29},{6,30},{7,31},{8,16},{9,... | collective-permute-start | bytes 2752520 | tf_op jit(solution)/shard_map/ppermute | solution.py:37
  41.4 1.1 collective-permute-start.10
  42.7 5.4 %collective-permute-done.5.refs_1_.refs_2_ = bf16[2,4,112,512]{3,2,1,0:T(8,128)(2,1)S(1)} collective-permute-done((bf16[2,4,112,512]{3,2,1,0:T(8,128)(2,1)S(1)}, bf16[2,4,112,512]{3,2,1,0:T(8,128)(2,1)S(1)}, u32[]{:S(2)}, u32[]{:S(2)}) %collective-permute-start.5) | collective-permute-done | bytes 917536 | tf_op jit(solution)/shard_map/ppermute | solution.py:37
  48.2 2.3 %collective-permute-start.8 = (bf16[4,112,512]{2,1,0:T(8,128)(2,1)S(1)}, bf16[4,112,512]{2,1,0:T(8,128)(2,1)S(1)}, u32[]{:S(2)}, u32[]{:S(2)}) collective-permute-start(bf16[4,112,512]{2,1,0:T(8,128)(2,1)S(1)} %forward.4.refs_2_), channel_id=1, source_target_pairs={{0,24},{1,25},{2,26},{3,27},{4,28},{5,29},{6,30},{7,31},{8,16},{9,... | collective-permute-start | bytes 1376264 | tf_op jit(solution)/shard_map/ppermute | solution.py:37
  50.5 3.4 %collective-permute-done.6.refs_1_.refs_3_ = bf16[2,4,112,512]{3,2,1,0:T(8,128)(2,1)S(1)} collective-permute-done((bf16[2,4,112,512]{3,2,1,0:T(8,128)(2,1)S(1)}, bf16[2,4,112,512]{3,2,1,0:T(8,128)(2,1)S(1)}, u32[]{:S(2)}, u32[]{:S(2)}) %collective-permute-start.6) | collective-permute-done | bytes 917536 | tf_op jit(solution)/shard_map/ppermute | solution.py:37
  54.3 4.5 %collective-permute-done.10.refs_5_ = bf16[4,112,512]{2,1,0:T(8,128)(2,1)S(1)} collective-permute-done((bf16[4,112,512]{2,1,0:T(8,128)(2,1)S(1)}, bf16[4,112,512]{2,1,0:T(8,128)(2,1)S(1)}, u32[]{:S(2)}, u32[]{:S(2)}) %collective-permute-start.10) | collective-permute-done | bytes 458784 | tf_op jit(solution)/shard_map/ppermute | solution.py:37
  58.8 0.3 ring_sum.2
  59.1 1.4 %collective-permute-start.14 = (bf16[112,1024]{1,0:T(8,128)(2,1)S(1)}, bf16[112,1024]{1,0:T(8,128)(2,1)S(1)}, u32[]{:S(2)}, u32[]{:S(2)}) collective-permute-start(bf16[112,1024]{1,0:T(8,128)(2,1)S(1)} %get-tuple-element.57), channel_id=1, source_target_pairs={{0,2},{1,3},{2,0},{3,1},{4,6},{5,7},{6,4},{7,5},{8,10},{9,11},{10,... | collective-permute-start | bytes 688136 | tf_op jit(solution)/shard_map/ppermute | solution.py:37
  60.5 2.5 %collective-permute-start.15 = (bf16[112,1024]{1,0:T(8,128)(2,1)S(1)}, bf16[112,1024]{1,0:T(8,128)(2,1)S(1)}, u32[]{:S(2)}, u32[]{:S(2)}) collective-permute-start(bf16[112,1024]{1,0:T(8,128)(2,1)S(1)} %get-tuple-element.58), channel_id=1, source_target_pairs={{0,6},{1,7},{2,4},{3,5},{4,2},{5,3},{6,0},{7,1},{8,14},{9,15},{10,... | collective-permute-start | bytes 688136 | tf_op jit(solution)/shard_map/ppermute | solution.py:37
  63.1 1.1 collective-permute-start.16
  64.1 0.3 ring_sum.3
  64.5 1.6 %collective-permute-start.11 = (bf16[112,1024]{1,0:T(8,128)(2,1)S(1)}, bf16[112,1024]{1,0:T(8,128)(2,1)S(1)}, u32[]{:S(2)}, u32[]{:S(2)}) collective-permute-start(bf16[112,1024]{1,0:T(8,128)(2,1)S(1)} %get-tuple-element.54), channel_id=1, source_target_pairs={{0,2},{1,3},{2,0},{3,1},{4,6},{5,7},{6,4},{7,5},{8,10},{9,11},{10,... | collective-permute-start | bytes 688136 | tf_op jit(solution)/shard_map/ppermute | solution.py:37
  66.1 2.7 %collective-permute-start.12 = (bf16[112,1024]{1,0:T(8,128)(2,1)S(1)}, bf16[112,1024]{1,0:T(8,128)(2,1)S(1)}, u32[]{:S(2)}, u32[]{:S(2)}) collective-permute-start(bf16[112,1024]{1,0:T(8,128)(2,1)S(1)} %get-tuple-element.55), channel_id=1, source_target_pairs={{0,6},{1,7},{2,4},{3,5},{4,2},{5,3},{6,0},{7,1},{8,14},{9,15},{10,... | collective-permute-start | bytes 688136 | tf_op jit(solution)/shard_map/ppermute | solution.py:37
  68.8 1.1 collective-permute-start.13
  69.9 0.7 collective-permute-done.16.refs_3_
  70.7 3.0 %collective-permute-start.18 = (bf16[56,1024]{1,0:T(8,128)(2,1)S(1)}, bf16[56,1024]{1,0:T(8,128)(2,1)S(1)}, u32[]{:S(2)}, u32[]{:S(2)}) collective-permute-start(bf16[56,1024]{1,0:T(8,128)(2,1)S(1)} %get-tuple-element.60.refs_4_), channel_id=1, source_target_pairs={{0,1},{1,0},{2,3},{3,2},{4,5},{5,4},{6,7},{7,6},{8,9},{9,8},{10,11... | collective-permute-start | bytes 344072 | tf_op jit(solution)/shard_map/ppermute | solution.py:37
  73.7 1.1 collective-permute-done.12.refs_2_
  74.8 1.5 %collective-permute-done.13.refs_3_ = bf16[112,1024]{1,0:T(8,128)(2,1)S(1)} collective-permute-done((bf16[112,1024]{1,0:T(8,128)(2,1)S(1)}, bf16[112,1024]{1,0:T(8,128)(2,1)S(1)}, u32[]{:S(2)}, u32[]{:S(2)}) %collective-permute-start.13) | collective-permute-done | bytes 229408 | tf_op jit(solution)/shard_map/ppermute | solution.py:37
  76.4 3.0 %collective-permute-start.17 = (bf16[56,1024]{1,0:T(8,128)(2,1)S(1)}, bf16[56,1024]{1,0:T(8,128)(2,1)S(1)}, u32[]{:S(2)}, u32[]{:S(2)}) collective-permute-start(bf16[56,1024]{1,0:T(8,128)(2,1)S(1)} %get-tuple-element.62.refs_3_), channel_id=1, source_target_pairs={{0,1},{1,0},{2,3},{3,2},{4,5},{5,4},{6,7},{7,6},{8,9},{9,8},{10,11... | collective-permute-start | bytes 344072 | tf_op jit(solution)/shard_map/ppermute | solution.py:37
  79.6 0.7 collective-permute-start.20
  80.3 3.3 %collective-permute-done.17.refs_1_ = bf16[56,1024]{1,0:T(8,128)(2,1)S(1)} collective-permute-done((bf16[56,1024]{1,0:T(8,128)(2,1)S(1)}, bf16[56,1024]{1,0:T(8,128)(2,1)S(1)}, u32[]{:S(2)}, u32[]{:S(2)}) %collective-permute-start.17) | collective-permute-done | bytes 114720 | tf_op jit(solution)/shard_map/ppermute | solution.py:37
  83.6 0.9 owner.3
  84.5 1.5 %collective-permute-done.20.refs_1_ = bf16[56,1024]{1,0:T(8,128)(2,1)S(1)} collective-permute-done((bf16[56,1024]{1,0:T(8,128)(2,1)S(1)}, bf16[56,1024]{1,0:T(8,128)(2,1)S(1)}, u32[]{:S(2)}, u32[]{:S(2)}) %collective-permute-start.20) | collective-permute-done | bytes 114720 | tf_op jit(solution)/shard_map/ppermute | solution.py:37
  86.0 1.1 collective-permute-start.24
  87.1 1.6 %collective-permute-start.25 = (bf16[112,1024]{1,0:T(8,128)(2,1)S(1)}, bf16[112,1024]{1,0:T(8,128)(2,1)S(1)}, u32[]{:S(2)}, u32[]{:S(2)}) collective-permute-start(bf16[112,1024]{1,0:T(8,128)(2,1)S(1)} %pair.2.refs_2_.refs_0_), channel_id=1, source_target_pairs={{0,6},{1,7},{2,4},{3,5},{4,2},{5,3},{6,0},{7,1},{8,14},{9,15},{10,... | collective-permute-start | bytes 688136 | tf_op jit(solution)/shard_map/ppermute | solution.py:37
  88.7 1.5 %collective-permute-start.26 = (bf16[112,1024]{1,0:T(8,128)(2,1)S(1)}, bf16[112,1024]{1,0:T(8,128)(2,1)S(1)}, u32[]{:S(2)}, u32[]{:S(2)}) collective-permute-start(bf16[112,1024]{1,0:T(8,128)(2,1)S(1)} %pair.2.refs_2_.refs_0_), channel_id=1, source_target_pairs={{0,4},{1,5},{2,6},{3,7},{4,0},{5,1},{6,2},{7,3},{8,12},{9,13},{10,... | collective-permute-start | bytes 688136 | tf_op jit(solution)/shard_map/ppermute | solution.py:37
  90.2 1.0 collective-permute-start.19
  91.2 5.3 %collective-permute-done.19.refs_1_ = bf16[56,1024]{1,0:T(8,128)(2,1)S(1)} collective-permute-done((bf16[56,1024]{1,0:T(8,128)(2,1)S(1)}, bf16[56,1024]{1,0:T(8,128)(2,1)S(1)}, u32[]{:S(2)}, u32[]{:S(2)}) %collective-permute-start.19) | collective-permute-done | bytes 114720 | tf_op jit(solution)/shard_map/ppermute | solution.py:37
  96.9 1.4 collective-permute-start.33
  98.2 2.4 %collective-permute-start.35 = (bf16[4,112,512]{2,1,0:T(8,128)(2,1)S(1)}, bf16[4,112,512]{2,1,0:T(8,128)(2,1)S(1)}, u32[]{:S(2)}, u32[]{:S(2)}) collective-permute-start(bf16[4,112,512]{2,1,0:T(8,128)(2,1)S(1)} %get-tuple-element.70.refs_1_), channel_id=1, source_target_pairs={{0,24},{1,25},{2,26},{3,27},{4,28},{5,29},{6,30},{7,31},{8,16},{9,... | collective-permute-start | bytes 1376264 | tf_op jit(solution)/shard_map/ppermute | solution.py:37
  100.6 0.3 collective-permute-start.21
  101.0 2.3 %collective-permute-start.22 = (bf16[112,1024]{1,0:T(8,128)(2,1)S(1)}, bf16[112,1024]{1,0:T(8,128)(2,1)S(1)}, u32[]{:S(2)}, u32[]{:S(2)}) collective-permute-start(bf16[112,1024]{1,0:T(8,128)(2,1)S(1)} %pair.3.refs_4_.refs_0_), channel_id=1, source_target_pairs={{0,6},{1,7},{2,4},{3,5},{4,2},{5,3},{6,0},{7,1},{8,14},{9,15},{10,... | collective-permute-start | bytes 688136 | tf_op jit(solution)/shard_map/ppermute | solution.py:37
  103.2 1.5 %collective-permute-start.23 = (bf16[112,1024]{1,0:T(8,128)(2,1)S(1)}, bf16[112,1024]{1,0:T(8,128)(2,1)S(1)}, u32[]{:S(2)}, u32[]{:S(2)}) collective-permute-start(bf16[112,1024]{1,0:T(8,128)(2,1)S(1)} %pair.3.refs_4_.refs_0_), channel_id=1, source_target_pairs={{0,4},{1,5},{2,6},{3,7},{4,0},{5,1},{6,2},{7,3},{8,12},{9,13},{10,... | collective-permute-start | bytes 688136 | tf_op jit(solution)/shard_map/ppermute | solution.py:37
  104.7 4.4 %collective-permute-done.21.refs_1_ = bf16[112,1024]{1,0:T(8,128)(2,1)S(1)} collective-permute-done((bf16[112,1024]{1,0:T(8,128)(2,1)S(1)}, bf16[112,1024]{1,0:T(8,128)(2,1)S(1)}, u32[]{:S(2)}, u32[]{:S(2)}) %collective-permute-start.21) | collective-permute-done | bytes 229408 | tf_op jit(solution)/shard_map/ppermute | solution.py:37
  109.1 1.1 collective-permute-done.22.refs_2_
  110.3 5.5 %collective-permute-done.23.refs_3_ = bf16[112,1024]{1,0:T(8,128)(2,1)S(1)} collective-permute-done((bf16[112,1024]{1,0:T(8,128)(2,1)S(1)}, bf16[112,1024]{1,0:T(8,128)(2,1)S(1)}, u32[]{:S(2)}, u32[]{:S(2)}) %collective-permute-start.23) | collective-permute-done | bytes 229408 | tf_op jit(solution)/shard_map/ppermute | solution.py:37
  116.2 0.5 collective-permute-start.29
  116.7 2.8 %collective-permute-start.34 = (bf16[4,112,512]{2,1,0:T(8,128)(2,1)S(1)}, bf16[4,112,512]{2,1,0:T(8,128)(2,1)S(1)}, u32[]{:S(2)}, u32[]{:S(2)}) collective-permute-start(bf16[4,112,512]{2,1,0:T(8,128)(2,1)S(1)} %collective-permute-done.33.refs_2_), channel_id=1, source_target_pairs={{0,24},{1,25},{2,26},{3,27},{4,28},{5,29},{6,30},{7,31},{8,16},{9,... | collective-permute-start | bytes 1376264 | tf_op jit(solution)/shard_map/ppermute | solution.py:37
  119.5 0.7 collective-permute-start.31
  120.2 1.3 collective-permute-start.36
  121.5 3.1 %collective-permute-done.27.refs_2_ = bf16[4,112,512]{2,1,0:T(8,128)(2,1)S(1)} collective-permute-done((bf16[4,112,512]{2,1,0:T(8,128)(2,1)S(1)}, bf16[4,112,512]{2,1,0:T(8,128)(2,1)S(1)}, u32[]{:S(2)}, u32[]{:S(2)}) %collective-permute-start.27) | collective-permute-done | bytes 458784 | tf_op jit(solution)/shard_map/ppermute | solution.py:37
  124.9 1.1 collective-permute-done.29.refs_5_
  126.0 1.9 %collective-permute-start.28 = (bf16[4,112,512]{2,1,0:T(8,128)(2,1)S(1)}, bf16[4,112,512]{2,1,0:T(8,128)(2,1)S(1)}, u32[]{:S(2)}, u32[]{:S(2)}) collective-permute-start(bf16[4,112,512]{2,1,0:T(8,128)(2,1)S(1)} %collective-permute-done.27.refs_2_), channel_id=1, source_target_pairs={{0,24},{1,25},{2,26},{3,27},{4,28},{5,29},{6,30},{7,31},{8,16},{9,... | collective-permute-start | bytes 1376264 | tf_op jit(solution)/shard_map/ppermute | solution.py:37
  127.9 3.0 %collective-permute-done.34.refs_0_ = bf16[4,112,512]{2,1,0:T(8,128)(2,1)S(1)} collective-permute-done((bf16[4,112,512]{2,1,0:T(8,128)(2,1)S(1)}, bf16[4,112,512]{2,1,0:T(8,128)(2,1)S(1)}, u32[]{:S(2)}, u32[]{:S(2)}) %collective-permute-start.34) | collective-permute-done | bytes 458784 | tf_op jit(solution)/shard_map/ppermute | solution.py:37
  130.9 0.7 collective-permute-start.30
  131.6 1.7 %place_update.4.refs_2_ = bf16[1792,2048]{1,0:T(8,128)(2,1)} custom-call(bf16[4,112,512]{2,1,0:T(8,128)(2,1)S(1)} %get-tuple-element.67.refs_4_.refs_0_, bf16[4,112,512]{2,1,0:T(8,128)(2,1)S(1)} %get-tuple-element.70.refs_1_, bf16[4,112,512]{2,1,0:T(8,128)(2,1)S(1)} %collective-permute-done.33.refs_2_, ...), custom_call_target="tpu_custom_call" | custom-call | bytes 40000000 | tf_op jit(solution)/shard_map/place_update/pallas_call | solution.py:252
  133.3 1.2 collective-permute-done.36.refs_1_
  134.5 1.0 place_update.5.refs_6_
  135.5 0.3 collective-permute-done.32.refs_4_
  135.8 1.7 %place_update.6.refs_2_ = bf16[1792,2048]{1,0:T(8,128)(2,1)} custom-call(bf16[4,112,512]{2,1,0:T(8,128)(2,1)S(1)} %get-tuple-element.68.refs_0_, bf16[4,112,512]{2,1,0:T(8,128)(2,1)S(1)} %get-tuple-element.69.refs_1_, bf16[4,112,512]{2,1,0:T(8,128)(2,1)S(1)} %collective-permute-done.27.refs_2_, ...), custom_call_target="tpu_custom_call", output_to_operand_aliasing={{}: (6, {})} | custom-call | bytes 40000000 | tf_op jit(solution)/shard_map/place_update/pallas_call | solution.py:252
  137.5 3.2 %collective-permute-done.28.refs_0_ = bf16[4,112,512]{2,1,0:T(8,128)(2,1)S(1)} collective-permute-done((bf16[4,112,512]{2,1,0:T(8,128)(2,1)S(1)}, bf16[4,112,512]{2,1,0:T(8,128)(2,1)S(1)}, u32[]{:S(2)}, u32[]{:S(2)}) %collective-permute-start.28) | collective-permute-done | bytes 458784 | tf_op jit(solution)/shard_map/ppermute | solution.py:37
  140.7 1.0 place_update.7
  (44 shorter events, 2.7 us)
Async XLA Ops:
  0.6 11.1 %collective-permute-start.1 = (bf16[1024,512]{1,0:T(8,128)(2,1)}, bf16[1024,512]{1,0:T(8,128)(2,1)S(1)}, u32[]{:S(2)}, u32[]{:S(2)}) collective-permute-start(bf16[1024,512]{1,0:T(8,128)(2,1)} %refs_3_.1), channel_id=1, source_target_pairs={{0,32},{32,0},{64,96},{96,64},{1,33},{33,1},{65,97},{97,65},{2,34}... | collective-permute-start | bytes 3145736 | tf_op jit(solution)/shard_map/ppermute | solution.py:41
  0.7 29.7 %collective-permute-start = (bf16[1024,512]{1,0:T(8,128)(2,1)}, bf16[1024,512]{1,0:T(8,128)(2,1)S(1)}, u32[]{:S(2)}, u32[]{:S(2)}) collective-permute-start(bf16[1024,512]{1,0:T(8,128)(2,1)} %refs_3_.1), channel_id=1, source_target_pairs={{0,64},{32,96},{64,0},{96,32},{1,65},{33,97},{65,1},{97,33},{2,66}... | collective-permute-start | bytes 3145736 | tf_op jit(solution)/shard_map/ppermute | solution.py:41
  2.5 2.0 %copy-start.1 = (bf16[1024,1792]{1,0:T(8,128)(2,1)S(1)}, bf16[1024,1792]{1,0:T(8,128)(2,1)}, u32[]{:S(2)}) copy-start(bf16[1024,1792]{1,0:T(8,128)(2,1)} %refs_0_.1) | copy-start | bytes 11010052
  4.5 1.2 copy-start.3
  5.7 6.0 %copy-start = (bf16[1792,2048]{1,0:T(8,128)(2,1)S(1)}, bf16[1792,2048]{1,0:T(8,128)(2,1)}, u32[]{:S(2)}) copy-start(bf16[1792,2048]{1,0:T(8,128)(2,1)} %refs_1_.7) | copy-start | bytes 22020100
  10.1 13.5 %collective-permute-start.2 = (bf16[2,4,112,512]{3,2,1,0:T(8,128)(2,1)S(1)}, bf16[2,4,112,512]{3,2,1,0:T(8,128)(2,1)S(1)}, u32[]{:S(2)}, u32[]{:S(2)}) collective-permute-start(bf16[2,4,112,512]{3,2,1,0:T(8,128)(2,1)S(1)} %get-tuple-element.40), channel_id=1, source_target_pairs={{0,8},{1,9},{2,10},{3,11},{4,12},{5,13},{6,14},{7,15},{8,0},{9,1},... | collective-permute-start | bytes 2752520 | tf_op jit(solution)/shard_map/ppermute | solution.py:37
  15.5 14.7 %collective-permute-start.3 = (bf16[2,4,112,512]{3,2,1,0:T(8,128)(2,1)S(1)}, bf16[2,4,112,512]{3,2,1,0:T(8,128)(2,1)S(1)}, u32[]{:S(2)}, u32[]{:S(2)}) collective-permute-start(bf16[2,4,112,512]{3,2,1,0:T(8,128)(2,1)S(1)} %get-tuple-element.41), channel_id=1, source_target_pairs={{0,24},{1,25},{2,26},{3,27},{4,28},{5,29},{6,30},{7,31},{8,16},{9,... | collective-permute-start | bytes 2752520 | tf_op jit(solution)/shard_map/ppermute | solution.py:37
  30.5 4.8 %collective-permute-start.4 = (bf16[1024,512]{1,0:T(8,128)(2,1)S(1)}, bf16[1024,512]{1,0:T(8,128)(2,1)S(1)}, u32[]{:S(2)}, u32[]{:S(2)}) collective-permute-start(bf16[1024,512]{1,0:T(8,128)(2,1)S(1)} %take_far.1.refs_3_.refs_4_), channel_id=1, source_target_pairs={{0,32},{32,0},{64,96},{96,64},{1,33},{33,1},{65,97},{97,65},{2,34}... | collective-permute-start | bytes 3145736 | tf_op jit(solution)/shard_map/ppermute | solution.py:41
  34.5 13.7 %collective-permute-start.5 = (bf16[2,4,112,512]{3,2,1,0:T(8,128)(2,1)S(1)}, bf16[2,4,112,512]{3,2,1,0:T(8,128)(2,1)S(1)}, u32[]{:S(2)}, u32[]{:S(2)}) collective-permute-start(bf16[2,4,112,512]{3,2,1,0:T(8,128)(2,1)S(1)} %get-tuple-element.46), channel_id=1, source_target_pairs={{0,8},{1,9},{2,10},{3,11},{4,12},{5,13},{6,14},{7,15},{8,0},{9,1},... | collective-permute-start | bytes 2752520 | tf_op jit(solution)/shard_map/ppermute | solution.py:37
  39.2 14.7 %collective-permute-start.6 = (bf16[2,4,112,512]{3,2,1,0:T(8,128)(2,1)S(1)}, bf16[2,4,112,512]{3,2,1,0:T(8,128)(2,1)S(1)}, u32[]{:S(2)}, u32[]{:S(2)}) collective-permute-start(bf16[2,4,112,512]{3,2,1,0:T(8,128)(2,1)S(1)} %get-tuple-element.47), channel_id=1, source_target_pairs={{0,24},{1,25},{2,26},{3,27},{4,28},{5,29},{6,30},{7,31},{8,16},{9,... | collective-permute-start | bytes 2752520 | tf_op jit(solution)/shard_map/ppermute | solution.py:37
  41.4 17.4 %collective-permute-start.10 = (bf16[4,112,512]{2,1,0:T(8,128)(2,1)S(1)}, bf16[4,112,512]{2,1,0:T(8,128)(2,1)S(1)}, u32[]{:S(2)}, u32[]{:S(2)}) collective-permute-start(bf16[4,112,512]{2,1,0:T(8,128)(2,1)S(1)} %get-tuple-element.42.refs_1_), channel_id=1, source_target_pairs={{0,24},{1,25},{2,26},{3,27},{4,28},{5,29},{6,30},{7,31},{8,16},{9,... | collective-permute-start | bytes 1376264 | tf_op jit(solution)/shard_map/ppermute | solution.py:37
  42.5 16.3 %collective-permute-start.9 = (bf16[4,112,512]{2,1,0:T(8,128)(2,1)S(1)}, bf16[4,112,512]{2,1,0:T(8,128)(2,1)S(1)}, u32[]{:S(2)}, u32[]{:S(2)}) collective-permute-start(bf16[4,112,512]{2,1,0:T(8,128)(2,1)S(1)} %get-tuple-element.51), channel_id=1, source_target_pairs={{0,8},{1,9},{2,10},{3,11},{4,12},{5,13},{6,14},{7,15},{8,0},{9,1},... | collective-permute-start | bytes 1376264 | tf_op jit(solution)/shard_map/ppermute | solution.py:37
  48.1 31.3 %copy-start.2 = (f32[56,2048]{1,0:T(8,128)S(1)}, f32[56,2048]{1,0:T(8,128)}, u32[]{:S(2)}) copy-start(f32[56,2048]{1,0:T(8,128)} %refs_2_.3) | copy-start | bytes 1376260
  48.2 15.9 %collective-permute-start.8 = (bf16[4,112,512]{2,1,0:T(8,128)(2,1)S(1)}, bf16[4,112,512]{2,1,0:T(8,128)(2,1)S(1)}, u32[]{:S(2)}, u32[]{:S(2)}) collective-permute-start(bf16[4,112,512]{2,1,0:T(8,128)(2,1)S(1)} %forward.4.refs_2_), channel_id=1, source_target_pairs={{0,24},{1,25},{2,26},{3,27},{4,28},{5,29},{6,30},{7,31},{8,16},{9,... | collective-permute-start | bytes 1376264 | tf_op jit(solution)/shard_map/ppermute | solution.py:37
  54.0 10.2 %collective-permute-start.7 = (bf16[4,112,512]{2,1,0:T(8,128)(2,1)S(1)}, bf16[4,112,512]{2,1,0:T(8,128)(2,1)S(1)}, u32[]{:S(2)}, u32[]{:S(2)}) collective-permute-start(bf16[4,112,512]{2,1,0:T(8,128)(2,1)S(1)} %forward.5.refs_6_), channel_id=1, source_target_pairs={{0,8},{1,9},{2,10},{3,11},{4,12},{5,13},{6,14},{7,15},{8,0},{9,1},... | collective-permute-start | bytes 1376264 | tf_op jit(solution)/shard_map/ppermute | solution.py:37
  59.1 9.7 %collective-permute-start.14 = (bf16[112,1024]{1,0:T(8,128)(2,1)S(1)}, bf16[112,1024]{1,0:T(8,128)(2,1)S(1)}, u32[]{:S(2)}, u32[]{:S(2)}) collective-permute-start(bf16[112,1024]{1,0:T(8,128)(2,1)S(1)} %get-tuple-element.57), channel_id=1, source_target_pairs={{0,2},{1,3},{2,0},{3,1},{4,6},{5,7},{6,4},{7,5},{8,10},{9,11},{10,... | collective-permute-start | bytes 688136 | tf_op jit(solution)/shard_map/ppermute | solution.py:37
  60.5 9.3 %collective-permute-start.15 = (bf16[112,1024]{1,0:T(8,128)(2,1)S(1)}, bf16[112,1024]{1,0:T(8,128)(2,1)S(1)}, u32[]{:S(2)}, u32[]{:S(2)}) collective-permute-start(bf16[112,1024]{1,0:T(8,128)(2,1)S(1)} %get-tuple-element.58), channel_id=1, source_target_pairs={{0,6},{1,7},{2,4},{3,5},{4,2},{5,3},{6,0},{7,1},{8,14},{9,15},{10,... | collective-permute-start | bytes 688136 | tf_op jit(solution)/shard_map/ppermute | solution.py:37
  63.1 7.5 %collective-permute-start.16 = (bf16[112,1024]{1,0:T(8,128)(2,1)S(1)}, bf16[112,1024]{1,0:T(8,128)(2,1)S(1)}, u32[]{:S(2)}, u32[]{:S(2)}) collective-permute-start(bf16[112,1024]{1,0:T(8,128)(2,1)S(1)} %get-tuple-element.59), channel_id=1, source_target_pairs={{0,4},{1,5},{2,6},{3,7},{4,0},{5,1},{6,2},{7,3},{8,12},{9,13},{10,... | collective-permute-start | bytes 688136 | tf_op jit(solution)/shard_map/ppermute | solution.py:37
  64.5 9.2 %collective-permute-start.11 = (bf16[112,1024]{1,0:T(8,128)(2,1)S(1)}, bf16[112,1024]{1,0:T(8,128)(2,1)S(1)}, u32[]{:S(2)}, u32[]{:S(2)}) collective-permute-start(bf16[112,1024]{1,0:T(8,128)(2,1)S(1)} %get-tuple-element.54), channel_id=1, source_target_pairs={{0,2},{1,3},{2,0},{3,1},{4,6},{5,7},{6,4},{7,5},{8,10},{9,11},{10,... | collective-permute-start | bytes 688136 | tf_op jit(solution)/shard_map/ppermute | solution.py:37
  66.1 8.7 %collective-permute-start.12 = (bf16[112,1024]{1,0:T(8,128)(2,1)S(1)}, bf16[112,1024]{1,0:T(8,128)(2,1)S(1)}, u32[]{:S(2)}, u32[]{:S(2)}) collective-permute-start(bf16[112,1024]{1,0:T(8,128)(2,1)S(1)} %get-tuple-element.55), channel_id=1, source_target_pairs={{0,6},{1,7},{2,4},{3,5},{4,2},{5,3},{6,0},{7,1},{8,14},{9,15},{10,... | collective-permute-start | bytes 688136 | tf_op jit(solution)/shard_map/ppermute | solution.py:37
  68.8 7.5 %collective-permute-start.13 = (bf16[112,1024]{1,0:T(8,128)(2,1)S(1)}, bf16[112,1024]{1,0:T(8,128)(2,1)S(1)}, u32[]{:S(2)}, u32[]{:S(2)}) collective-permute-start(bf16[112,1024]{1,0:T(8,128)(2,1)S(1)} %get-tuple-element.56), channel_id=1, source_target_pairs={{0,4},{1,5},{2,6},{3,7},{4,0},{5,1},{6,2},{7,3},{8,12},{9,13},{10,... | collective-permute-start | bytes 688136 | tf_op jit(solution)/shard_map/ppermute | solution.py:37
  70.7 8.7 %collective-permute-start.18 = (bf16[56,1024]{1,0:T(8,128)(2,1)S(1)}, bf16[56,1024]{1,0:T(8,128)(2,1)S(1)}, u32[]{:S(2)}, u32[]{:S(2)}) collective-permute-start(bf16[56,1024]{1,0:T(8,128)(2,1)S(1)} %get-tuple-element.60.refs_4_), channel_id=1, source_target_pairs={{0,1},{1,0},{2,3},{3,2},{4,5},{5,4},{6,7},{7,6},{8,9},{9,8},{10,11... | collective-permute-start | bytes 344072 | tf_op jit(solution)/shard_map/ppermute | solution.py:37
  76.4 7.2 %collective-permute-start.17 = (bf16[56,1024]{1,0:T(8,128)(2,1)S(1)}, bf16[56,1024]{1,0:T(8,128)(2,1)S(1)}, u32[]{:S(2)}, u32[]{:S(2)}) collective-permute-start(bf16[56,1024]{1,0:T(8,128)(2,1)S(1)} %get-tuple-element.62.refs_3_), channel_id=1, source_target_pairs={{0,1},{1,0},{2,3},{3,2},{4,5},{5,4},{6,7},{7,6},{8,9},{9,8},{10,11... | collective-permute-start | bytes 344072 | tf_op jit(solution)/shard_map/ppermute | solution.py:37
  79.6 6.4 %collective-permute-start.20 = (bf16[56,1024]{1,0:T(8,128)(2,1)S(1)}, bf16[56,1024]{1,0:T(8,128)(2,1)S(1)}, u32[]{:S(2)}, u32[]{:S(2)}) collective-permute-start(bf16[56,1024]{1,0:T(8,128)(2,1)S(1)} %get-tuple-element.65.refs_4_.refs_0_), channel_id=1, source_target_pairs={{0,1},{1,0},{2,3},{3,2},{4,5},{5,4},{6,7},{7,6},{8,9},{9,8},{10,11... | collective-permute-start | bytes 344072 | tf_op jit(solution)/shard_map/ppermute | solution.py:37
  86.0 10.5 %collective-permute-start.24 = (bf16[112,1024]{1,0:T(8,128)(2,1)S(1)}, bf16[112,1024]{1,0:T(8,128)(2,1)S(1)}, u32[]{:S(2)}, u32[]{:S(2)}) collective-permute-start(bf16[112,1024]{1,0:T(8,128)(2,1)S(1)} %pair.2.refs_2_.refs_0_), channel_id=1, source_target_pairs={{0,2},{1,3},{2,0},{3,1},{4,6},{5,7},{6,4},{7,5},{8,10},{9,11},{10,... | collective-permute-start | bytes 688136 | tf_op jit(solution)/shard_map/ppermute | solution.py:37
  87.1 9.7 %collective-permute-start.25 = (bf16[112,1024]{1,0:T(8,128)(2,1)S(1)}, bf16[112,1024]{1,0:T(8,128)(2,1)S(1)}, u32[]{:S(2)}, u32[]{:S(2)}) collective-permute-start(bf16[112,1024]{1,0:T(8,128)(2,1)S(1)} %pair.2.refs_2_.refs_0_), channel_id=1, source_target_pairs={{0,6},{1,7},{2,4},{3,5},{4,2},{5,3},{6,0},{7,1},{8,14},{9,15},{10,... | collective-permute-start | bytes 688136 | tf_op jit(solution)/shard_map/ppermute | solution.py:37
  88.7 8.1 %collective-permute-start.26 = (bf16[112,1024]{1,0:T(8,128)(2,1)S(1)}, bf16[112,1024]{1,0:T(8,128)(2,1)S(1)}, u32[]{:S(2)}, u32[]{:S(2)}) collective-permute-start(bf16[112,1024]{1,0:T(8,128)(2,1)S(1)} %pair.2.refs_2_.refs_0_), channel_id=1, source_target_pairs={{0,4},{1,5},{2,6},{3,7},{4,0},{5,1},{6,2},{7,3},{8,12},{9,13},{10,... | collective-permute-start | bytes 688136 | tf_op jit(solution)/shard_map/ppermute | solution.py:37
  90.2 6.3 %collective-permute-start.19 = (bf16[56,1024]{1,0:T(8,128)(2,1)S(1)}, bf16[56,1024]{1,0:T(8,128)(2,1)S(1)}, u32[]{:S(2)}, u32[]{:S(2)}) collective-permute-start(bf16[56,1024]{1,0:T(8,128)(2,1)S(1)} %get-tuple-element.66.refs_2_.refs_0_), channel_id=1, source_target_pairs={{0,1},{1,0},{2,3},{3,2},{4,5},{5,4},{6,7},{7,6},{8,9},{9,8},{10,11... | collective-permute-start | bytes 344072 | tf_op jit(solution)/shard_map/ppermute | solution.py:37
  96.9 19.3 %collective-permute-start.33 = (bf16[4,112,512]{2,1,0:T(8,128)(2,1)S(1)}, bf16[4,112,512]{2,1,0:T(8,128)(2,1)S(1)}, u32[]{:S(2)}, u32[]{:S(2)}) collective-permute-start(bf16[4,112,512]{2,1,0:T(8,128)(2,1)S(1)} %get-tuple-element.67.refs_4_.refs_0_), channel_id=1, source_target_pairs={{0,8},{1,9},{2,10},{3,11},{4,12},{5,13},{6,14},{7,15},{8,0},{9,1},... | collective-permute-start | bytes 1376264 | tf_op jit(solution)/shard_map/ppermute | solution.py:37
  98.2 18.5 %collective-permute-start.35 = (bf16[4,112,512]{2,1,0:T(8,128)(2,1)S(1)}, bf16[4,112,512]{2,1,0:T(8,128)(2,1)S(1)}, u32[]{:S(2)}, u32[]{:S(2)}) collective-permute-start(bf16[4,112,512]{2,1,0:T(8,128)(2,1)S(1)} %get-tuple-element.70.refs_1_), channel_id=1, source_target_pairs={{0,24},{1,25},{2,26},{3,27},{4,28},{5,29},{6,30},{7,31},{8,16},{9,... | collective-permute-start | bytes 1376264 | tf_op jit(solution)/shard_map/ppermute | solution.py:37
  100.6 8.5 %collective-permute-start.21 = (bf16[112,1024]{1,0:T(8,128)(2,1)S(1)}, bf16[112,1024]{1,0:T(8,128)(2,1)S(1)}, u32[]{:S(2)}, u32[]{:S(2)}) collective-permute-start(bf16[112,1024]{1,0:T(8,128)(2,1)S(1)} %pair.3.refs_4_.refs_0_), channel_id=1, source_target_pairs={{0,2},{1,3},{2,0},{3,1},{4,6},{5,7},{6,4},{7,5},{8,10},{9,11},{10,... | collective-permute-start | bytes 688136 | tf_op jit(solution)/shard_map/ppermute | solution.py:37
  101.0 9.2 %collective-permute-start.22 = (bf16[112,1024]{1,0:T(8,128)(2,1)S(1)}, bf16[112,1024]{1,0:T(8,128)(2,1)S(1)}, u32[]{:S(2)}, u32[]{:S(2)}) collective-permute-start(bf16[112,1024]{1,0:T(8,128)(2,1)S(1)} %pair.3.refs_4_.refs_0_), channel_id=1, source_target_pairs={{0,6},{1,7},{2,4},{3,5},{4,2},{5,3},{6,0},{7,1},{8,14},{9,15},{10,... | collective-permute-start | bytes 688136 | tf_op jit(solution)/shard_map/ppermute | solution.py:37
  103.2 12.6 %collective-permute-start.23 = (bf16[112,1024]{1,0:T(8,128)(2,1)S(1)}, bf16[112,1024]{1,0:T(8,128)(2,1)S(1)}, u32[]{:S(2)}, u32[]{:S(2)}) collective-permute-start(bf16[112,1024]{1,0:T(8,128)(2,1)S(1)} %pair.3.refs_4_.refs_0_), channel_id=1, source_target_pairs={{0,4},{1,5},{2,6},{3,7},{4,0},{5,1},{6,2},{7,3},{8,12},{9,13},{10,... | collective-permute-start | bytes 688136 | tf_op jit(solution)/shard_map/ppermute | solution.py:37
  109.1 10.4 %collective-permute-start.37 = (bf16[4,112,512]{2,1,0:T(8,128)(2,1)S(1)}, bf16[4,112,512]{2,1,0:T(8,128)(2,1)S(1)}, u32[]{:S(2)}, u32[]{:S(2)}) collective-permute-start(bf16[4,112,512]{2,1,0:T(8,128)(2,1)S(1)} %get-tuple-element.70.refs_1_), channel_id=1, source_target_pairs={{0,8},{1,9},{2,10},{3,11},{4,12},{5,13},{6,14},{7,15},{8,0},{9,1},... | collective-permute-start | bytes 1376264 | tf_op jit(solution)/shard_map/ppermute | solution.py:37
  110.2 10.1 %collective-permute-start.38 = (bf16[4,112,512]{2,1,0:T(8,128)(2,1)S(1)}, bf16[4,112,512]{2,1,0:T(8,128)(2,1)S(1)}, u32[]{:S(2)}, u32[]{:S(2)}) collective-permute-start(bf16[4,112,512]{2,1,0:T(8,128)(2,1)S(1)} %get-tuple-element.67.refs_4_.refs_0_), channel_id=1, source_target_pairs={{0,24},{1,25},{2,26},{3,27},{4,28},{5,29},{6,30},{7,31},{8,16},{9,... | collective-permute-start | bytes 1376264 | tf_op jit(solution)/shard_map/ppermute | solution.py:37
  115.9 8.8 %collective-permute-start.27 = (bf16[4,112,512]{2,1,0:T(8,128)(2,1)S(1)}, bf16[4,112,512]{2,1,0:T(8,128)(2,1)S(1)}, u32[]{:S(2)}, u32[]{:S(2)}) collective-permute-start(bf16[4,112,512]{2,1,0:T(8,128)(2,1)S(1)} %get-tuple-element.68.refs_0_), channel_id=1, source_target_pairs={{0,8},{1,9},{2,10},{3,11},{4,12},{5,13},{6,14},{7,15},{8,0},{9,1},... | collective-permute-start | bytes 1376264 | tf_op jit(solution)/shard_map/ppermute | solution.py:37
  116.2 9.8 %collective-permute-start.29 = (bf16[4,112,512]{2,1,0:T(8,128)(2,1)S(1)}, bf16[4,112,512]{2,1,0:T(8,128)(2,1)S(1)}, u32[]{:S(2)}, u32[]{:S(2)}) collective-permute-start(bf16[4,112,512]{2,1,0:T(8,128)(2,1)S(1)} %get-tuple-element.69.refs_1_), channel_id=1, source_target_pairs={{0,24},{1,25},{2,26},{3,27},{4,28},{5,29},{6,30},{7,31},{8,16},{9,... | collective-permute-start | bytes 1376264 | tf_op jit(solution)/shard_map/ppermute | solution.py:37
  116.7 14.2 %collective-permute-start.34 = (bf16[4,112,512]{2,1,0:T(8,128)(2,1)S(1)}, bf16[4,112,512]{2,1,0:T(8,128)(2,1)S(1)}, u32[]{:S(2)}, u32[]{:S(2)}) collective-permute-start(bf16[4,112,512]{2,1,0:T(8,128)(2,1)S(1)} %collective-permute-done.33.refs_2_), channel_id=1, source_target_pairs={{0,24},{1,25},{2,26},{3,27},{4,28},{5,29},{6,30},{7,31},{8,16},{9,... | collective-permute-start | bytes 1376264 | tf_op jit(solution)/shard_map/ppermute | solution.py:37
  119.5 16.0 %collective-permute-start.31 = (bf16[4,112,512]{2,1,0:T(8,128)(2,1)S(1)}, bf16[4,112,512]{2,1,0:T(8,128)(2,1)S(1)}, u32[]{:S(2)}, u32[]{:S(2)}) collective-permute-start(bf16[4,112,512]{2,1,0:T(8,128)(2,1)S(1)} %get-tuple-element.69.refs_1_), channel_id=1, source_target_pairs={{0,8},{1,9},{2,10},{3,11},{4,12},{5,13},{6,14},{7,15},{8,0},{9,1},... | collective-permute-start | bytes 1376264 | tf_op jit(solution)/shard_map/ppermute | solution.py:37
  120.2 14.2 %collective-permute-start.36 = (bf16[4,112,512]{2,1,0:T(8,128)(2,1)S(1)}, bf16[4,112,512]{2,1,0:T(8,128)(2,1)S(1)}, u32[]{:S(2)}, u32[]{:S(2)}) collective-permute-start(bf16[4,112,512]{2,1,0:T(8,128)(2,1)S(1)} %collective-permute-done.35.refs_5_), channel_id=1, source_target_pairs={{0,8},{1,9},{2,10},{3,11},{4,12},{5,13},{6,14},{7,15},{8,0},{9,1},... | collective-permute-start | bytes 1376264 | tf_op jit(solution)/shard_map/ppermute | solution.py:37
  124.6 11.1 %collective-permute-start.32 = (bf16[4,112,512]{2,1,0:T(8,128)(2,1)S(1)}, bf16[4,112,512]{2,1,0:T(8,128)(2,1)S(1)}, u32[]{:S(2)}, u32[]{:S(2)}) collective-permute-start(bf16[4,112,512]{2,1,0:T(8,128)(2,1)S(1)} %get-tuple-element.68.refs_0_), channel_id=1, source_target_pairs={{0,24},{1,25},{2,26},{3,27},{4,28},{5,29},{6,30},{7,31},{8,16},{9,... | collective-permute-start | bytes 1376264 | tf_op jit(solution)/shard_map/ppermute | solution.py:37
  126.0 14.7 %collective-permute-start.28 = (bf16[4,112,512]{2,1,0:T(8,128)(2,1)S(1)}, bf16[4,112,512]{2,1,0:T(8,128)(2,1)S(1)}, u32[]{:S(2)}, u32[]{:S(2)}) collective-permute-start(bf16[4,112,512]{2,1,0:T(8,128)(2,1)S(1)} %collective-permute-done.27.refs_2_), channel_id=1, source_target_pairs={{0,24},{1,25},{2,26},{3,27},{4,28},{5,29},{6,30},{7,31},{8,16},{9,... | collective-permute-start | bytes 1376264 | tf_op jit(solution)/shard_map/ppermute | solution.py:37
  130.9 9.8 %collective-permute-start.30 = (bf16[4,112,512]{2,1,0:T(8,128)(2,1)S(1)}, bf16[4,112,512]{2,1,0:T(8,128)(2,1)S(1)}, u32[]{:S(2)}, u32[]{:S(2)}) collective-permute-start(bf16[4,112,512]{2,1,0:T(8,128)(2,1)S(1)} %collective-permute-done.29.refs_5_), channel_id=1, source_target_pairs={{0,8},{1,9},{2,10},{3,11},{4,12},{5,13},{6,14},{7,15},{8,0},{9,1},... | collective-permute-start | bytes 1376264 | tf_op jit(solution)/shard_map/ppermute | solution.py:37
